TPU v7x, 32 devices: a whole 2x2x4 slice. The times are simulated.
32 devices in a mesh: doc: 2 (over x), seq: 16 (over z, y, core).
Axes of the slice: x: 2, y: 2, z: 4, core: 2. Of those that a mesh axis runs over, the one named last changes fastest.
Arguments:
- queries: bfloat16 [2, 2048, 1024], P('doc', 'seq'), may hold values from -7 to 7
- key_rows: bfloat16 [2, 2048, 1024], P('doc', 'seq'), may hold values from -7 to 7
- value_rows: bfloat16 [2, 2048, 1024], P('doc', 'seq'), may hold values from -5 to 5
- cotangent: bfloat16 [2, 2048, 1024], P('doc', 'seq'), may hold values from -3 to 3
- out_weight: bfloat16 [1024, 1024], P('doc'), may hold values from -0.1875 to 0.1875
- lengths: int32 [2, 4], P('doc'), may hold values from 1 to 16, 32 in all within a row
- upweight: int32 [2, 4], P('doc'), may hold values from 1 to 6, as said below
Outputs:
- layer_out: bfloat16 [2, 2048, 1024], P('doc', 'seq')
- grad_query: bfloat16 [2, 2048, 1024], P('doc', 'seq')
- grad_key: bfloat16 [2, 2048, 1024], P('doc', 'seq')
- grad_value: bfloat16 [2, 2048, 1024], P('doc', 'seq')
- grad_weight: float32 [1024, 1024], P('doc')
Inputs may be any that keep to these rules, and one draw needn't show every extreme that they name: Each sequence's documents fill it exactly: the lengths add up to 32, and the longest is 16. `upweight`: each entry is 1 or 6; every sequence has a document with factor 6.
All inputs are finite; a program needn't handle non-finite values.
Results may differ from a plain program's by a relative error of at most 0.0089.
Values may be sent and summed in bfloat16 or wider, within the bound.
No kernel may reach another device: no remote copies, remote signals or barrier semaphores. Data moves between devices by JAX's collectives and lax.ppermute only.
A program may use at most 128 MiB of HBM per device.

v0:
```python
import math

import jax
import jax.numpy as jnp
from jax import lax
from jax.sharding import PartitionSpec as P

HEADS = 16
HEAD_DIM = 64
WINDOW = 512
BLOCK = 64
DOCS = 4


def shifted(value, axis, steps):
    count = lax.axis_size(axis)
    first, last = (max(0, -steps), min(count, count - steps))
    return lax.ppermute(value, axis, [(source, source + steps) for source in range(first, last)])


def document_ids(lengths_row, positions):
    bounds = jnp.cumsum(lengths_row) * BLOCK
    return jnp.sum((positions[:, None] >= bounds[None, :]).astype(jnp.int32), axis=1)


def band_mask(query_pos, key_pos, query_doc, key_doc, seq_len):
    near_band = jnp.abs(query_pos[:, None] - key_pos[None, :]) <= WINDOW
    inside = (key_pos >= 0) & (key_pos < seq_len)
    return near_band & inside[None, :] & (query_doc[:, None] == key_doc[None, :])


def soft_weights(query_grp, key_grp, allowed):
    scores = jnp.einsum(
        "qhd,khd->hqk", query_grp, key_grp, preferred_element_type=jnp.float32
    ) * HEAD_DIM ** (-0.5)
    scores = jnp.where(allowed[None], scores, -jnp.inf)
    row_peak = jnp.max(scores, axis=2, keepdims=True)
    exponent = jnp.exp(scores - row_peak)
    return exponent / jnp.sum(exponent, axis=2, keepdims=True)


def body(queries, key_rows, value_rows, cotangent, out_weight, lengths, upweight):
    rows_here = queries.shape[1]
    model_width = queries.shape[2]
    seq_count = lax.axis_size("seq")
    doc_count = lax.axis_size("doc")
    seq_place = lax.axis_index("seq")
    seq_len = rows_here * seq_count
    edge_rows = min(WINDOW, rows_here)
    far_blocks = WINDOW // edge_rows
    key_span = rows_here + 2 * WINDOW
    score_scale = HEAD_DIM ** (-0.5)
    query_rows = queries[0]
    stacked = jnp.stack([key_rows[0], value_rows[0]])
    before_list = [shifted(stacked, "seq", distance) for distance in range(1, far_blocks + 1)]
    after_list = [shifted(stacked, "seq", -distance) for distance in range(1, far_blocks + 1)]
    extended = jnp.concatenate(before_list[::-1] + [stacked] + after_list, axis=1)
    key_ext = extended[0]
    value_ext = extended[1]
    row_base = seq_place * rows_here
    query_pos = row_base + jnp.arange(rows_here, dtype=jnp.int32)
    key_pos = row_base - WINDOW + jnp.arange(key_span, dtype=jnp.int32)
    lengths_row = lengths[0]
    query_doc = document_ids(lengths_row, query_pos)
    allowed = band_mask(query_pos, key_pos, query_doc, document_ids(lengths_row, key_pos), seq_len)
    matches = query_doc[:, None] == jnp.arange(DOCS, dtype=jnp.int32)[None, :]
    token_weight = jnp.sum(jnp.where(matches, upweight[0][None, :], 0), axis=1).astype(jnp.float32)
    group_heads = min(HEADS, max(1, 512 // rows_here))
    group_count = HEADS // group_heads
    group_cols = group_heads * HEAD_DIM

    def group_slices(group_index):
        col_start = group_index * group_cols
        query_grp = lax.dynamic_slice_in_dim(query_rows, col_start, group_cols, 1).reshape(
            rows_here, group_heads, HEAD_DIM
        )
        key_grp = lax.dynamic_slice_in_dim(key_ext, col_start, group_cols, 1).reshape(
            key_span, group_heads, HEAD_DIM
        )
        value_grp = lax.dynamic_slice_in_dim(value_ext, col_start, group_cols, 1).reshape(
            key_span, group_heads, HEAD_DIM
        )
        return (col_start, query_grp, key_grp, value_grp)

    def forward_group(group_index, attended_buf):
        col_start, query_grp, key_grp, value_grp = group_slices(group_index)
        prob_half = soft_weights(query_grp, key_grp, allowed).astype(jnp.bfloat16)
        mixed_rows = jnp.einsum(
            "hqk,khd->qhd", prob_half, value_grp, preferred_element_type=jnp.float32
        )
        mixed_rows = mixed_rows.reshape(rows_here, group_cols).astype(jnp.bfloat16)
        return lax.dynamic_update_slice_in_dim(attended_buf, mixed_rows, col_start, 1)

    attended = lax.fori_loop(
        0, group_count, forward_group, jnp.zeros((rows_here, model_width), jnp.bfloat16)
    )
    full_weight = lax.all_gather(out_weight, "doc", axis=0, tiled=True)
    layer_out = jnp.dot(attended, full_weight, preferred_element_type=jnp.float32).astype(
        jnp.bfloat16
    )
    grad_out = (token_weight[:, None] * cotangent[0].astype(jnp.float32)).astype(jnp.bfloat16)
    grad_attended = lax.dot_general(
        grad_out, full_weight, (((1,), (1,)), ((), ())), preferred_element_type=jnp.float32
    ).astype(jnp.bfloat16)
    partial_grad = lax.dot_general(
        attended, grad_out, (((0,), (0,)), ((), ())), preferred_element_type=jnp.float32
    )
    row_block = lax.psum_scatter(partial_grad, "doc", scatter_dimension=0, tiled=True)
    weight_sum = lax.psum(row_block, "seq")
    grad_weight = weight_sum * (1.0 / math.sqrt(rows_here * seq_count * doc_count))

    def backward_group(group_index, grad_state):
        grad_query_buf, own_grad, early_grad, later_grad = grad_state
        col_start, query_grp, key_grp, value_grp = group_slices(group_index)
        prob_full = soft_weights(query_grp, key_grp, allowed)
        prob_half = prob_full.astype(jnp.bfloat16)
        grad_grp = lax.dynamic_slice_in_dim(grad_attended, col_start, group_cols, 1).reshape(
            rows_here, group_heads, HEAD_DIM
        )
        grad_prob = jnp.einsum(
            "qhd,khd->hqk", grad_grp, value_grp, preferred_element_type=jnp.float32
        )
        centre = jnp.sum(prob_full * grad_prob, axis=2, keepdims=True)
        grad_score = (prob_full * (grad_prob - centre) * score_scale).astype(jnp.bfloat16)
        grad_query_grp = jnp.einsum(
            "hqk,khd->qhd", grad_score, key_grp, preferred_element_type=jnp.float32
        )
        grad_query_grp = grad_query_grp.reshape(rows_here, group_cols).astype(jnp.bfloat16)
        key_part = jnp.einsum(
            "hqk,qhd->khd", grad_score, query_grp, preferred_element_type=jnp.float32
        )
        value_part = jnp.einsum(
            "hqk,qhd->khd", prob_half, grad_grp, preferred_element_type=jnp.float32
        )
        both_parts = jnp.stack(
            [key_part.reshape(key_span, group_cols), value_part.reshape(key_span, group_cols)]
        )
        grad_query_buf = lax.dynamic_update_slice_in_dim(
            grad_query_buf, grad_query_grp, col_start, 1
        )
        own_grad = lax.dynamic_update_slice(
            own_grad, both_parts[:, WINDOW : WINDOW + rows_here], (0, 0, col_start)
        )
        early_grad = lax.dynamic_update_slice(
            early_grad, both_parts[:, :WINDOW].astype(jnp.bfloat16), (0, 0, col_start)
        )
        later_grad = lax.dynamic_update_slice(
            later_grad, both_parts[:, WINDOW + rows_here :].astype(jnp.bfloat16), (0, 0, col_start)
        )
        return (grad_query_buf, own_grad, early_grad, later_grad)

    grad_state = (
        jnp.zeros((rows_here, model_width), jnp.bfloat16),
        jnp.zeros((2, rows_here, model_width), jnp.float32),
        jnp.zeros((2, WINDOW, model_width), jnp.bfloat16),
        jnp.zeros((2, WINDOW, model_width), jnp.bfloat16),
    )
    grad_query, own_grad, early_grad, later_grad = lax.fori_loop(
        0, group_count, backward_group, grad_state
    )
    early_returned = [
        shifted(
            early_grad[:, WINDOW - distance * edge_rows : WINDOW - (distance - 1) * edge_rows],
            "seq",
            -distance,
        )
        for distance in range(1, far_blocks + 1)
    ]
    later_returned = [
        shifted(later_grad[:, (distance - 1) * edge_rows : distance * edge_rows], "seq", distance)
        for distance in range(1, far_blocks + 1)
    ]
    tail_extra = jnp.zeros((2, edge_rows, model_width), jnp.float32)
    for returned in early_returned:
        tail_extra = tail_extra + returned.astype(jnp.float32)
    head_extra = jnp.zeros((2, edge_rows, model_width), jnp.float32)
    for returned in later_returned:
        head_extra = head_extra + returned.astype(jnp.float32)
    own_grad = own_grad.at[:, rows_here - edge_rows :].add(tail_extra)
    own_grad = own_grad.at[:, :edge_rows].add(head_extra)
    grad_key = own_grad[0].astype(jnp.bfloat16)
    grad_value = own_grad[1].astype(jnp.bfloat16)
    return (layer_out[None], grad_query[None], grad_key[None], grad_value[None], grad_weight)


def solution(mesh):
    return jax.shard_map(
        body,
        mesh=mesh,
        in_specs=(
            P("doc", "seq", None),
            P("doc", "seq", None),
            P("doc", "seq", None),
            P("doc", "seq", None),
            P("doc", None),
            P("doc", None),
            P("doc", None),
        ),
        out_specs=(
            P("doc", "seq", None),
            P("doc", "seq", None),
            P("doc", "seq", None),
            P("doc", "seq", None),
            P("doc", None),
        ),
        check_vma=False,
    )
```

profile of v0, /device:TPU:0, one launch (start us, length us, event | category | flops | bytes accessed | tf_op | source)
XLA Modules:
  0.0 364.9 jit_solution(10054886679926181106)
XLA Ops:
  9.6 5.7 %collective-permute-start = (bf16[2,128,1024]{1,2,0:T(8,128)(2,1)S(1)}, bf16[2,128,1024]{1,2,0:T(8,128)(2,1)}, u32[]{:S(2)}, u32[]{:S(2)}) collective-permute-start(bf16[2,128,1024]{1,2,0:T(8,128)(2,1)S(1)} %pad_maximum_fusion.1), channel_id=1, source_target_pairs={{0,4},{1,5},{2,6},{3,7},{4,8},{5,9},{6,10},{7,11},{8,12},{9,13},{1... | collective-permute-start | bytes 1572872 | tf_op jit(solution)/shard_map/ppermute | solution.py:18
  15.3 2.6 collective-permute-start.1
  17.9 2.7 collective-permute-start.2
  20.6 2.6 collective-permute-start.3
  30.7 30.5 %collective-permute-done.2 = bf16[2,128,1024]{1,2,0:T(8,128)(2,1)S(1)} collective-permute-done((bf16[2,128,1024]{1,2,0:T(8,128)(2,1)S(1)}, bf16[2,128,1024]{1,2,0:T(8,128)(2,1)S(1)}, u32[]{:S(2)}, u32[]{:S(2)}) %collective-permute-start.2) | collective-permute-done | bytes 524320 | tf_op jit(solution)/shard_map/ppermute | solution.py:18
  63.3 8.9 %collective-permute-done.7 = bf16[2,128,1024]{1,2,0:T(8,128)(2,1)S(1)} collective-permute-done((bf16[2,128,1024]{1,2,0:T(8,128)(2,1)S(1)}, bf16[2,128,1024]{1,2,0:T(8,128)(2,1)S(1)}, u32[]{:S(2)}, u32[]{:S(2)}) %collective-permute-start.7) | collective-permute-done | bytes 524320 | tf_op jit(solution)/shard_map/ppermute | solution.py:18
  72.4 2.5 slice_bitcast_fusion
  74.9 29.0 %while.38 = (s32[]{:T(128)}, bf16[128,1024]{0,1:T(8,128)(2,1)S(1)}, bf16[1152,1024]{0,1:T(8,128)(2,1)}, bf16[128,1024]{0,1:T(8,128)(2,1)}, bf16[1152,1024]{0,1:T...) while((s32[]{:T(128)}, bf16[128,1024]{0,1:T(8,128)(2,1)S(1)}, ...), condition=%wide.region_6.7_spmd.clone, body=%wide.region_3.6_spmd.clone.sunk | while | flops 155452544 | bytes 8961351 | solution.py:94
  77.5 2.4 fusion.104
  79.9 2.3 fusion.105
  84.7 2.4 fusion.104
  87.1 2.3 fusion.105
  92.0 2.4 fusion.104
  94.4 2.3 fusion.105
  99.2 2.4 fusion.104
  101.6 2.3 fusion.105
  104.0 2.7 fusion.51
  106.9 3.1 convolution_convert_fusion
  112.0 1.6 broadcast.133.clone
  113.6 1.6 broadcast.133.clone2
  115.1 94.2 %while.39 = (s32[]{:T(128)}, bf16[128,1024]{1,0:T(8,128)(2,1)}, f32[2,128,1024]{2,1,0:T(8,128)}, bf16[2,512,1024]{2,1,0:T(8,128)(2,1)}, bf16[2,512,1024]{2,1,0:T...) while((s32[]{:T(128)}, bf16[128,1024]{1,0:T(8,128)(2,1)}, ...), condition=%wide.region_12.13_spmd.clone, body=%wide.region_8.12_spmd.clone.sunk | while | flops 390861184 | bytes 38351472 | solution.py:158
  120.8 2.3 fusion.118
  123.1 5.0 %fusion.119 = bf16[4,64,128]{2,1,0:T(8,128)(2,1)S(1)} fusion(bf16[1152,4,64]{0,2,1:T(8,128)(2,1)S(1)} %bitcast.100, f32[4,128,1152]{2,1,0:T(8,128)S(1)} %fusion.116, f32[4,128,1152]{2,1,0:T(8,128)} %get-tuple-element.651, f32[4,128]{1,0:T(4,128)S(1)} %get-tuple-element.652), kind=kOutput, calls=%fused_computation.43.clone.1 | convolution fusion | flops 79660672 | bytes 5376000 | tf_op jit(solution)/shard_map/while/body/eval_jaxpr/hqk,khd->qhd/dot_general | solution.py:125
  128.9 5.2 %fusion.120 = f32[4,64,1152]{2,1,0:T(8,128)S(1)} fusion(bf16[128,4,64]{0,2,1:T(8,128)(2,1)} %bitcast.104, f32[4,128,1152]{2,1,0:T(8,128)S(1)} %fusion.116, f32[4,128,1152]{2,1,0:T(8,128)} %get-tuple-element.651, f32[4,128]{1,0:T(4,128)} %copy-done.21), kind=kOutput, calls=%fused_computation.36.clone.1 | convolution fusion | flops 79627904 | bytes 5965824 | tf_op jit(solution)/shard_map/while/body/eval_jaxpr/hqk,qhd->khd/dot_general | solution.py:129
  134.1 2.3 fusion.121
  144.8 2.3 fusion.118
  147.2 4.7 %fusion.119 = bf16[4,64,128]{2,1,0:T(8,128)(2,1)S(1)} fusion(bf16[1152,4,64]{0,2,1:T(8,128)(2,1)S(1)} %bitcast.100, f32[4,128,1152]{2,1,0:T(8,128)S(1)} %fusion.116, f32[4,128,1152]{2,1,0:T(8,128)} %get-tuple-element.651, f32[4,128]{1,0:T(4,128)S(1)} %get-tuple-element.652), kind=kOutput, calls=%fused_computation.43.clone.1 | convolution fusion | flops 79660672 | bytes 5376000 | tf_op jit(solution)/shard_map/while/body/eval_jaxpr/hqk,khd->qhd/dot_general | solution.py:125
  152.7 5.0 %fusion.120 = f32[4,64,1152]{2,1,0:T(8,128)S(1)} fusion(bf16[128,4,64]{0,2,1:T(8,128)(2,1)} %bitcast.104, f32[4,128,1152]{2,1,0:T(8,128)S(1)} %fusion.116, f32[4,128,1152]{2,1,0:T(8,128)} %get-tuple-element.651, f32[4,128]{1,0:T(4,128)} %copy-done.21), kind=kOutput, calls=%fused_computation.36.clone.1 | convolution fusion | flops 79627904 | bytes 5965824 | tf_op jit(solution)/shard_map/while/body/eval_jaxpr/hqk,qhd->khd/dot_general | solution.py:129
  157.7 2.1 fusion.121
  168.2 2.3 fusion.118
  170.6 4.7 %fusion.119 = bf16[4,64,128]{2,1,0:T(8,128)(2,1)S(1)} fusion(bf16[1152,4,64]{0,2,1:T(8,128)(2,1)S(1)} %bitcast.100, f32[4,128,1152]{2,1,0:T(8,128)S(1)} %fusion.116, f32[4,128,1152]{2,1,0:T(8,128)} %get-tuple-element.651, f32[4,128]{1,0:T(4,128)S(1)} %get-tuple-element.652), kind=kOutput, calls=%fused_computation.43.clone.1 | convolution fusion | flops 79660672 | bytes 5376000 | tf_op jit(solution)/shard_map/while/body/eval_jaxpr/hqk,khd->qhd/dot_general | solution.py:125
  176.1 5.0 %fusion.120 = f32[4,64,1152]{2,1,0:T(8,128)S(1)} fusion(bf16[128,4,64]{0,2,1:T(8,128)(2,1)} %bitcast.104, f32[4,128,1152]{2,1,0:T(8,128)S(1)} %fusion.116, f32[4,128,1152]{2,1,0:T(8,128)} %get-tuple-element.651, f32[4,128]{1,0:T(4,128)} %copy-done.21), kind=kOutput, calls=%fused_computation.36.clone.1 | convolution fusion | flops 79627904 | bytes 5965824 | tf_op jit(solution)/shard_map/while/body/eval_jaxpr/hqk,qhd->khd/dot_general | solution.py:129
  181.1 2.1 fusion.121
  191.6 2.3 fusion.118
  194.0 4.7 %fusion.119 = bf16[4,64,128]{2,1,0:T(8,128)(2,1)S(1)} fusion(bf16[1152,4,64]{0,2,1:T(8,128)(2,1)S(1)} %bitcast.100, f32[4,128,1152]{2,1,0:T(8,128)S(1)} %fusion.116, f32[4,128,1152]{2,1,0:T(8,128)} %get-tuple-element.651, f32[4,128]{1,0:T(4,128)S(1)} %get-tuple-element.652), kind=kOutput, calls=%fused_computation.43.clone.1 | convolution fusion | flops 79660672 | bytes 5376000 | tf_op jit(solution)/shard_map/while/body/eval_jaxpr/hqk,khd->qhd/dot_general | solution.py:125
  199.5 5.0 %fusion.120 = f32[4,64,1152]{2,1,0:T(8,128)S(1)} fusion(bf16[128,4,64]{0,2,1:T(8,128)(2,1)} %bitcast.104, f32[4,128,1152]{2,1,0:T(8,128)S(1)} %fusion.116, f32[4,128,1152]{2,1,0:T(8,128)} %get-tuple-element.651, f32[4,128]{1,0:T(4,128)} %copy-done.21), kind=kOutput, calls=%fused_computation.36.clone.1 | convolution fusion | flops 79627904 | bytes 5965824 | tf_op jit(solution)/shard_map/while/body/eval_jaxpr/hqk,qhd->khd/dot_general | solution.py:129
  204.5 2.1 fusion.121
  209.3 2.7 fusion.58
  212.0 4.7 %collective-permute-start.15 = (bf16[2,128,1024]{2,1,0:T(8,128)(2,1)S(1)}, bf16[2,128,1024]{2,1,0:T(8,128)(2,1)S(1)}, u32[]{:S(2)}, u32[]{:S(2)}) collective-permute-start(bf16[2,128,1024]{2,1,0:T(8,128)(2,1)S(1)} %get-tuple-element.488), channel_id=1, source_target_pairs={{0,4},{1,5},{2,6},{3,7},{4,8},{5,9},{6,10},{7,11},{8,12},{9,13},{1... | collective-permute-start | bytes 1572872 | tf_op jit(solution)/shard_map/ppermute | solution.py:18
  218.0 3.6 collective-permute-start.13
  221.7 5.0 %collective-permute-start.12 = (bf16[2,128,1024]{2,1,0:T(8,128)(2,1)}, bf16[2,128,1024]{2,1,0:T(8,128)(2,1)}, u32[]{:S(2)}, u32[]{:S(2)}) collective-permute-start(bf16[2,128,1024]{2,1,0:T(8,128)(2,1)} %get-tuple-element.485), channel_id=1, source_target_pairs={{0,1},{1,2},{2,3},{3,4},{4,5},{5,6},{6,7},{7,8},{8,9},{9,10},{10,1... | collective-permute-start | bytes 1572872 | tf_op jit(solution)/shard_map/ppermute | solution.py:18
  228.1 1.4 collective-permute-start.11
  232.1 4.9 %collective-permute-done.13 = bf16[2,128,1024]{2,1,0:T(8,128)(2,1)} collective-permute-done((bf16[2,128,1024]{2,1,0:T(8,128)(2,1)S(1)}, bf16[2,128,1024]{2,1,0:T(8,128)(2,1)}, u32[]{:S(2)}, u32[]{:S(2)}) %collective-permute-start.13) | collective-permute-done | bytes 524320 | tf_op jit(solution)/shard_map/ppermute | solution.py:18
  239.6 5.7 %collective-permute-done.11 = bf16[2,128,1024]{2,1,0:T(8,128)(2,1)} collective-permute-done((bf16[2,128,1024]{2,1,0:T(8,128)(2,1)}, bf16[2,128,1024]{2,1,0:T(8,128)(2,1)}, u32[]{:S(2)}, u32[]{:S(2)}) %collective-permute-start.11) | collective-permute-done | bytes 524320 | tf_op jit(solution)/shard_map/ppermute | solution.py:18
  245.3 6.6 %collective-permute-done.9 = bf16[2,128,1024]{2,1,0:T(8,128)(2,1)} collective-permute-done((bf16[2,128,1024]{2,1,0:T(8,128)(2,1)}, bf16[2,128,1024]{2,1,0:T(8,128)(2,1)}, u32[]{:S(2)}, u32[]{:S(2)}) %collective-permute-start.9) | collective-permute-done | bytes 524320 | tf_op jit(solution)/shard_map/ppermute | solution.py:18
  251.8 2.8 add_convert_fusion
  255.4 99.7 %all-reduce.2.cloned.1.call-done = f32[512,1024]{1,0:T(8,128)} async-done(((f32[512,1024]{1,0:T(8,128)}), f32[512,1024]{1,0:T(8,128)}) %all-reduce.2.cloned.1.call-update) | async-done | bytes 2097168 | tf_op jit(solution)/shard_map/psum | solution.py:109
  355.2 3.2 broadcast_multiply_fusion
  (237 shorter events, 68.8 us)
Async XLA Ops:
  7.2 17.5 %copy-start.19 = (s32[1,4]{1,0:T(1,128)S(1)}, s32[1,4]{1,0:T(1,128)}, u32[]{:S(2)}) copy-start(s32[1,4]{1,0:T(1,128)} %param.24) | copy-start | bytes 52
  7.2 17.8 %copy-start.20 = (s32[1,4]{1,0:T(1,128)S(1)}, s32[1,4]{1,0:T(1,128)}, u32[]{:S(2)}) copy-start(s32[1,4]{1,0:T(1,128)} %param.25) | copy-start | bytes 52
  7.2 17.9 %copy-start.12 = (bf16[1,128,1024]{2,1,0:T(8,128)(2,1)S(1)}, bf16[1,128,1024]{2,1,0:T(8,128)(2,1)}, u32[]{:S(2)}) copy-start(bf16[1,128,1024]{2,1,0:T(8,128)(2,1)} %param.19) | copy-start | bytes 786436
  7.2 99.7 %all-gather.2.cloned.1.call-start = ((), (), s32[]{:S(2)}) async-start(), calls=%async_computation.1 | async-start | bytes 3145728 | tf_op jit(solution)/shard_map/all_gather | solution.py:97
  9.6 17.2 %collective-permute-start = (bf16[2,128,1024]{1,2,0:T(8,128)(2,1)S(1)}, bf16[2,128,1024]{1,2,0:T(8,128)(2,1)}, u32[]{:S(2)}, u32[]{:S(2)}) collective-permute-start(bf16[2,128,1024]{1,2,0:T(8,128)(2,1)S(1)} %pad_maximum_fusion.1), channel_id=1, source_target_pairs={{0,4},{1,5},{2,6},{3,7},{4,8},{5,9},{6,10},{7,11},{8,12},{9,13},{1... | collective-permute-start | bytes 1572872 | tf_op jit(solution)/shard_map/ppermute | solution.py:18
  15.3 13.9 %collective-permute-start.1 = (bf16[2,128,1024]{1,2,0:T(8,128)(2,1)S(1)}, bf16[2,128,1024]{1,2,0:T(8,128)(2,1)S(1)}, u32[]{:S(2)}, u32[]{:S(2)}) collective-permute-start(bf16[2,128,1024]{1,2,0:T(8,128)(2,1)S(1)} %pad_maximum_fusion.1), channel_id=1, source_target_pairs={{0,3},{1,4},{2,5},{3,6},{4,7},{5,8},{6,9},{7,10},{8,11},{9,12},{10... | collective-permute-start | bytes 1572872 | tf_op jit(solution)/shard_map/ppermute | solution.py:18
  17.9 43.2 %collective-permute-start.2 = (bf16[2,128,1024]{1,2,0:T(8,128)(2,1)S(1)}, bf16[2,128,1024]{1,2,0:T(8,128)(2,1)S(1)}, u32[]{:S(2)}, u32[]{:S(2)}) collective-permute-start(bf16[2,128,1024]{1,2,0:T(8,128)(2,1)S(1)} %pad_maximum_fusion.1), channel_id=1, source_target_pairs={{0,2},{1,3},{2,4},{3,5},{4,6},{5,7},{6,8},{7,9},{8,10},{9,11},{10,... | collective-permute-start | bytes 1572872 | tf_op jit(solution)/shard_map/ppermute | solution.py:18
  20.6 42.0 %collective-permute-start.3 = (bf16[2,128,1024]{1,2,0:T(8,128)(2,1)S(1)}, bf16[2,128,1024]{1,2,0:T(8,128)(2,1)S(1)}, u32[]{:S(2)}, u32[]{:S(2)}) collective-permute-start(bf16[2,128,1024]{1,2,0:T(8,128)(2,1)S(1)} %pad_maximum_fusion.1), channel_id=1, source_target_pairs={{0,1},{1,2},{2,3},{3,4},{4,5},{5,6},{6,7},{7,8},{8,9},{9,10},{10,1... | collective-permute-start | bytes 1572872 | tf_op jit(solution)/shard_map/ppermute | solution.py:18
  23.3 39.6 %collective-permute-start.4 = (bf16[2,128,1024]{1,2,0:T(8,128)(2,1)S(1)}, bf16[2,128,1024]{1,2,0:T(8,128)(2,1)S(1)}, u32[]{:S(2)}, u32[]{:S(2)}) collective-permute-start(bf16[2,128,1024]{1,2,0:T(8,128)(2,1)S(1)} %pad_maximum_fusion.1), channel_id=1, source_target_pairs={{1,0},{2,1},{3,2},{4,3},{5,4},{6,5},{7,6},{8,7},{9,8},{10,9},{11,1... | collective-permute-start | bytes 1572872 | tf_op jit(solution)/shard_map/ppermute | solution.py:18
  24.6 213.7 %reduce-scatter.2.cloned.1.call-start = ((), (), s32[]{:S(2)}) async-start(), calls=%async_computation.2 | async-start | bytes 6291456 | tf_op jit(solution)/shard_map/reduce_scatter | solution.py:108
  26.8 36.2 %collective-permute-start.5 = (bf16[2,128,1024]{1,2,0:T(8,128)(2,1)S(1)}, bf16[2,128,1024]{1,2,0:T(8,128)(2,1)S(1)}, u32[]{:S(2)}, u32[]{:S(2)}) collective-permute-start(bf16[2,128,1024]{1,2,0:T(8,128)(2,1)S(1)} %pad_maximum_fusion.1), channel_id=1, source_target_pairs={{2,0},{3,1},{4,2},{5,3},{6,4},{7,5},{8,6},{9,7},{10,8},{11,9},{12,... | collective-permute-start | bytes 1572872 | tf_op jit(solution)/shard_map/ppermute | solution.py:18
  29.3 33.9 %collective-permute-start.6 = (bf16[2,128,1024]{1,2,0:T(8,128)(2,1)S(1)}, bf16[2,128,1024]{1,2,0:T(8,128)(2,1)S(1)}, u32[]{:S(2)}, u32[]{:S(2)}) collective-permute-start(bf16[2,128,1024]{1,2,0:T(8,128)(2,1)S(1)} %pad_maximum_fusion.1), channel_id=1, source_target_pairs={{3,0},{4,1},{5,2},{6,3},{7,4},{8,5},{9,6},{10,7},{11,8},{12,9},{13... | collective-permute-start | bytes 1572872 | tf_op jit(solution)/shard_map/ppermute | solution.py:18
  61.2 11.1 %collective-permute-start.7 = (bf16[2,128,1024]{1,2,0:T(8,128)(2,1)S(1)}, bf16[2,128,1024]{1,2,0:T(8,128)(2,1)S(1)}, u32[]{:S(2)}, u32[]{:S(2)}) collective-permute-start(bf16[2,128,1024]{1,2,0:T(8,128)(2,1)S(1)} %pad_maximum_fusion.1), channel_id=1, source_target_pairs={{4,0},{5,1},{6,2},{7,3},{8,4},{9,5},{10,6},{11,7},{12,8},{13,9},{1... | collective-permute-start | bytes 1572872 | tf_op jit(solution)/shard_map/ppermute | solution.py:18
  74.9 29.0 %copy-start.7 = (bf16[1,128,1024]{2,1,0:T(8,128)(2,1)S(1)}, bf16[1,128,1024]{2,1,0:T(8,128)(2,1)}, u32[]{:S(2)}) copy-start(bf16[1,128,1024]{2,1,0:T(8,128)(2,1)} %param.22) | copy-start | bytes 786436
  106.7 248.5 %all-reduce.2.cloned.1.call-start = ((), (), s32[]{:S(2)}) async-start(), calls=%async_computation.3 | async-start | bytes 4194304 | tf_op jit(solution)/shard_map/psum | solution.py:109
  117.2 10.9 %copy-start.2 = (bf16[128,256]{0,1:T(8,128)(2,1)}, bf16[128,256]{0,1:T(8,128)(2,1)S(1)}, u32[]{:S(2)}) copy-start(bf16[128,256]{0,1:T(8,128)(2,1)S(1)} %copy.54) | copy-start | bytes 196612 | tf_op jit(solution)/shard_map/while
  119.8 8.3 %copy-start.6 = (bf16[128,256]{0,1:T(8,128)(2,1)}, bf16[128,256]{0,1:T(8,128)(2,1)S(1)}, u32[]{:S(2)}) copy-start(bf16[128,256]{0,1:T(8,128)(2,1)S(1)} %constant_dynamic-slice_fusion.18) | copy-start | bytes 196612 | tf_op jit(solution)/shard_map/while
  123.1 5.0 %copy-start.21 = (f32[4,128]{1,0:T(4,128)}, f32[4,128]{1,0:T(4,128)S(1)}, u32[]{:S(2)}) copy-start(f32[4,128]{1,0:T(4,128)S(1)} %get-tuple-element.652) | copy-start | bytes 6148 | tf_op jit(solution)/shard_map/while
  139.1 3.3 copy-start.13
  139.2 3.3 copy-start.15
  141.3 10.7 %copy-start.2 = (bf16[128,256]{0,1:T(8,128)(2,1)}, bf16[128,256]{0,1:T(8,128)(2,1)S(1)}, u32[]{:S(2)}) copy-start(bf16[128,256]{0,1:T(8,128)(2,1)S(1)} %copy.54) | copy-start | bytes 196612 | tf_op jit(solution)/shard_map/while
  143.8 8.1 %copy-start.6 = (bf16[128,256]{0,1:T(8,128)(2,1)}, bf16[128,256]{0,1:T(8,128)(2,1)S(1)}, u32[]{:S(2)}) copy-start(bf16[128,256]{0,1:T(8,128)(2,1)S(1)} %constant_dynamic-slice_fusion.18) | copy-start | bytes 196612 | tf_op jit(solution)/shard_map/while
  147.2 4.8 %copy-start.21 = (f32[4,128]{1,0:T(4,128)}, f32[4,128]{1,0:T(4,128)S(1)}, u32[]{:S(2)}) copy-start(f32[4,128]{1,0:T(4,128)S(1)} %get-tuple-element.652) | copy-start | bytes 6148 | tf_op jit(solution)/shard_map/while
  162.5 3.3 copy-start.13
  162.5 3.3 copy-start.15
  162.6 3.3 copy-start.17
  164.7 10.6 %copy-start.2 = (bf16[128,256]{0,1:T(8,128)(2,1)}, bf16[128,256]{0,1:T(8,128)(2,1)S(1)}, u32[]{:S(2)}) copy-start(bf16[128,256]{0,1:T(8,128)(2,1)S(1)} %copy.54) | copy-start | bytes 196612 | tf_op jit(solution)/shard_map/while
  167.2 8.1 %copy-start.6 = (bf16[128,256]{0,1:T(8,128)(2,1)}, bf16[128,256]{0,1:T(8,128)(2,1)S(1)}, u32[]{:S(2)}) copy-start(bf16[128,256]{0,1:T(8,128)(2,1)S(1)} %constant_dynamic-slice_fusion.18) | copy-start | bytes 196612 | tf_op jit(solution)/shard_map/while
  170.6 4.8 %copy-start.21 = (f32[4,128]{1,0:T(4,128)}, f32[4,128]{1,0:T(4,128)S(1)}, u32[]{:S(2)}) copy-start(f32[4,128]{1,0:T(4,128)S(1)} %get-tuple-element.652) | copy-start | bytes 6148 | tf_op jit(solution)/shard_map/while
  188.1 10.6 %copy-start.2 = (bf16[128,256]{0,1:T(8,128)(2,1)}, bf16[128,256]{0,1:T(8,128)(2,1)S(1)}, u32[]{:S(2)}) copy-start(bf16[128,256]{0,1:T(8,128)(2,1)S(1)} %copy.54) | copy-start | bytes 196612 | tf_op jit(solution)/shard_map/while
  190.6 8.1 %copy-start.6 = (bf16[128,256]{0,1:T(8,128)(2,1)}, bf16[128,256]{0,1:T(8,128)(2,1)S(1)}, u32[]{:S(2)}) copy-start(bf16[128,256]{0,1:T(8,128)(2,1)S(1)} %constant_dynamic-slice_fusion.18) | copy-start | bytes 196612 | tf_op jit(solution)/shard_map/while
  194.0 4.8 %copy-start.21 = (f32[4,128]{1,0:T(4,128)}, f32[4,128]{1,0:T(4,128)S(1)}, u32[]{:S(2)}) copy-start(f32[4,128]{1,0:T(4,128)S(1)} %get-tuple-element.652) | copy-start | bytes 6148 | tf_op jit(solution)/shard_map/while
  209.3 17.4 %copy-start.1 = (bf16[2,512,1024]{2,1,0:T(8,128)(2,1)S(1)}, bf16[2,512,1024]{2,1,0:T(8,128)(2,1)}, u32[]{:S(2)}) copy-start(bf16[2,512,1024]{2,1,0:T(8,128)(2,1)} %get-tuple-element.329) | copy-start | bytes 6291460
  212.0 17.5 %collective-permute-start.15 = (bf16[2,128,1024]{2,1,0:T(8,128)(2,1)S(1)}, bf16[2,128,1024]{2,1,0:T(8,128)(2,1)S(1)}, u32[]{:S(2)}, u32[]{:S(2)}) collective-permute-start(bf16[2,128,1024]{2,1,0:T(8,128)(2,1)S(1)} %get-tuple-element.488), channel_id=1, source_target_pairs={{0,4},{1,5},{2,6},{3,7},{4,8},{5,9},{6,10},{7,11},{8,12},{9,13},{1... | collective-permute-start | bytes 1572872 | tf_op jit(solution)/shard_map/ppermute | solution.py:18
  216.7 14.1 %collective-permute-start.14 = (bf16[2,128,1024]{2,1,0:T(8,128)(2,1)S(1)}, bf16[2,128,1024]{2,1,0:T(8,128)(2,1)S(1)}, u32[]{:S(2)}, u32[]{:S(2)}) collective-permute-start(bf16[2,128,1024]{2,1,0:T(8,128)(2,1)S(1)} %get-tuple-element.486), channel_id=1, source_target_pairs={{0,3},{1,4},{2,5},{3,6},{4,7},{5,8},{6,9},{7,10},{8,11},{9,12},{10... | collective-permute-start | bytes 1572872 | tf_op jit(solution)/shard_map/ppermute | solution.py:18
  218.0 18.9 %collective-permute-start.13 = (bf16[2,128,1024]{2,1,0:T(8,128)(2,1)S(1)}, bf16[2,128,1024]{2,1,0:T(8,128)(2,1)}, u32[]{:S(2)}, u32[]{:S(2)}) collective-permute-start(bf16[2,128,1024]{2,1,0:T(8,128)(2,1)S(1)} %get-tuple-element.487), channel_id=1, source_target_pairs={{0,2},{1,3},{2,4},{3,5},{4,6},{5,7},{6,8},{7,9},{8,10},{9,11},{10,... | collective-permute-start | bytes 1572872 | tf_op jit(solution)/shard_map/ppermute | solution.py:18
  221.7 17.9 %collective-permute-start.12 = (bf16[2,128,1024]{2,1,0:T(8,128)(2,1)}, bf16[2,128,1024]{2,1,0:T(8,128)(2,1)}, u32[]{:S(2)}, u32[]{:S(2)}) collective-permute-start(bf16[2,128,1024]{2,1,0:T(8,128)(2,1)} %get-tuple-element.485), channel_id=1, source_target_pairs={{0,1},{1,2},{2,3},{3,4},{4,5},{5,6},{6,7},{7,8},{8,9},{9,10},{10,1... | collective-permute-start | bytes 1572872 | tf_op jit(solution)/shard_map/ppermute | solution.py:18
  226.7 11.6 %copy-start = (bf16[1024,1024]{1,0:T(8,128)(2,1)S(1)}, bf16[1024,1024]{1,0:T(8,128)(2,1)}, u32[]{:S(2)}) copy-start(bf16[1024,1024]{1,0:T(8,128)(2,1)} %all-gather.2.cloned.1.call-done) | copy-start | bytes 6291460
  226.7 11.7 %copy-start.5 = (bf16[128,1024]{0,1:T(8,128)(2,1)S(1)}, bf16[128,1024]{0,1:T(8,128)(2,1)}, u32[]{:S(2)}) copy-start(bf16[128,1024]{0,1:T(8,128)(2,1)} %copy-done.4) | copy-start | bytes 786436
  228.1 17.2 %collective-permute-start.11 = (bf16[2,128,1024]{2,1,0:T(8,128)(2,1)}, bf16[2,128,1024]{2,1,0:T(8,128)(2,1)}, u32[]{:S(2)}, u32[]{:S(2)}) collective-permute-start(bf16[2,128,1024]{2,1,0:T(8,128)(2,1)} %get-tuple-element.484), channel_id=1, source_target_pairs={{4,0},{5,1},{6,2},{7,3},{8,4},{9,5},{10,6},{11,7},{12,8},{13,9},{1... | collective-permute-start | bytes 1572872 | tf_op jit(solution)/shard_map/ppermute | solution.py:18
  229.5 8.8 %copy-start.8 = (bf16[2,128,1024]{2,1,0:T(8,128)(2,1)}, bf16[2,128,1024]{2,1,0:T(8,128)(2,1)S(1)}, u32[]{:S(2)}) copy-start(bf16[2,128,1024]{2,1,0:T(8,128)(2,1)S(1)} %collective-permute-done.15) | copy-start | bytes 1572868
  229.5 15.8 %collective-permute-start.10 = (bf16[2,128,1024]{2,1,0:T(8,128)(2,1)}, bf16[2,128,1024]{2,1,0:T(8,128)(2,1)}, u32[]{:S(2)}, u32[]{:S(2)}) collective-permute-start(bf16[2,128,1024]{2,1,0:T(8,128)(2,1)} %get-tuple-element.482), channel_id=1, source_target_pairs={{3,0},{4,1},{5,2},{6,3},{7,4},{8,5},{9,6},{10,7},{11,8},{12,9},{13... | collective-permute-start | bytes 1572872 | tf_op jit(solution)/shard_map/ppermute | solution.py:18
  230.8 7.5 %copy-start.10 = (bf16[2,128,1024]{2,1,0:T(8,128)(2,1)}, bf16[2,128,1024]{2,1,0:T(8,128)(2,1)S(1)}, u32[]{:S(2)}) copy-start(bf16[2,128,1024]{2,1,0:T(8,128)(2,1)S(1)} %collective-permute-done.14) | copy-start | bytes 1572868
  230.8 21.0 %collective-permute-start.9 = (bf16[2,128,1024]{2,1,0:T(8,128)(2,1)}, bf16[2,128,1024]{2,1,0:T(8,128)(2,1)}, u32[]{:S(2)}, u32[]{:S(2)}) collective-permute-start(bf16[2,128,1024]{2,1,0:T(8,128)(2,1)} %get-tuple-element.483), channel_id=1, source_target_pairs={{2,0},{3,1},{4,2},{5,3},{6,4},{7,5},{8,6},{9,7},{10,8},{11,9},{12,... | collective-permute-start | bytes 1572872 | tf_op jit(solution)/shard_map/ppermute | solution.py:18
  237.0 14.8 %collective-permute-start.8 = (bf16[2,128,1024]{2,1,0:T(8,128)(2,1)}, bf16[2,128,1024]{2,1,0:T(8,128)(2,1)}, u32[]{:S(2)}, u32[]{:S(2)}) collective-permute-start(bf16[2,128,1024]{2,1,0:T(8,128)(2,1)} %get-tuple-element.481), channel_id=1, source_target_pairs={{1,0},{2,1},{3,2},{4,3},{5,4},{6,5},{7,6},{8,7},{9,8},{10,9},{11,1... | collective-permute-start | bytes 1572872 | tf_op jit(solution)/shard_map/ppermute | solution.py:18
  238.3 13.5 %copy-start.3 = (f32[2,128,1024]{2,1,0:T(8,128)S(1)}, f32[2,128,1024]{2,1,0:T(8,128)}, u32[]{:S(2)}) copy-start(f32[2,128,1024]{2,1,0:T(8,128)} %get-tuple-element.328) | copy-start | bytes 3145732
  238.4 13.5 %copy-start.9 = (bf16[2,128,1024]{2,1,0:T(8,128)(2,1)S(1)}, bf16[2,128,1024]{2,1,0:T(8,128)(2,1)}, u32[]{:S(2)}) copy-start(bf16[2,128,1024]{2,1,0:T(8,128)(2,1)} %copy-done.8) | copy-start | bytes 1572868
  238.4 13.4 %copy-start.11 = (bf16[2,128,1024]{2,1,0:T(8,128)(2,1)S(1)}, bf16[2,128,1024]{2,1,0:T(8,128)(2,1)}, u32[]{:S(2)}) copy-start(bf16[2,128,1024]{2,1,0:T(8,128)(2,1)} %copy-done.10) | copy-start | bytes 1572868
  (20 other events, 43.4 us)
Sparse Core Ops, SparseCore 0:
  24.7 34.1 all-gather.1
  106.8 56.0 reduce-scatter.1
  238.5 116.6 all-reduce.1
where the time goes:
time: 367 us; the launch traced here: 365 us
  waiting for transfers between devices  157 us (43%)
  matrix products  85.2 us (23%)
  local copies, waits for them, and re-layouts  55.6 us (15%)
  starting transfers between devices  39 us (11%)
  between operations  14.2 us (4%)
  other arithmetic  12.7 us (3%)
    psum x1, waiting for transfers between devices, body(): weight_sum = lax.psum(row_block, 'seq')  99.7 us
    ppermute x16, waiting for transfers between devices, shifted(): lax.ppermute(value, axis, [(source, source + steps) for source in range(f...  57.4 us
    ppermute x16, starting transfers between devices, shifted(): lax.ppermute(value, axis, [(source, source + steps) for source in range(f...  38.7 us
    dot_general x4, matrix products, backward_group(): jnp.einsum('hqk,qhd->khd', grad_score, query_grp, preferred_element_type=...  20.2 us
    dot_general x4, matrix products, backward_group(): jnp.einsum('hqk,khd->qhd', grad_score, key_grp, preferred_element_type=jn...  19.2 us
    sub x8, matrix products, soft_weights(): exponent = jnp.exp(scores - row_peak)  18.9 us
    dynamic_slice x8, local copies, waits for them, and re-layouts, group_slices(): lax.dynamic_slice_in_dim(key_ext, col_start, group_cols, 1)  9.87 us
    dot_general x4, matrix products, forward_group(): jnp.einsum('hqk,khd->qhd', prob_half, value_grp, preferred_element_type=j...  9.2 us
  transfers between devices with their start and end apart: 19, of which 7 were waited for; matrix products, arithmetic and copies ran while one was open for 40% of the time, Pallas kernels for 0%

commit v1 on v0

v1 whole, which is shorter than its diff:
```python
import functools
import math

import jax
import jax.numpy as jnp
from jax import lax
from jax.experimental import pallas as pl
from jax.experimental.pallas import tpu as pltpu
from jax.sharding import PartitionSpec as P

HEADS = 16
HEAD_DIM = 64
WINDOW = 512
BLOCK = 64
DOCS = 4
PAIR = 2 * HEAD_DIM
MASKED = -1e30
BF16 = jnp.bfloat16
F32 = jnp.float32

VMEM = pl.BlockSpec(memory_space=pltpu.VMEM)
SMEM = pl.BlockSpec(memory_space=pltpu.SMEM)


def call(kernel, out_shape, operands, scalars=0, scratch=(), flops=0, moved=0, vmem=24):
    outs = [jax.ShapeDtypeStruct(shape, kind) for shape, kind in out_shape]
    return pl.pallas_call(
        kernel,
        out_shape=outs,
        in_specs=[SMEM] * scalars + [VMEM] * (len(operands) - scalars),
        out_specs=[VMEM] * len(outs),
        scratch_shapes=list(scratch),
        compiler_params=pltpu.CompilerParams(vmem_limit_bytes=vmem << 20),
        cost_estimate=pl.CostEstimate(flops=flops, bytes_accessed=moved, transcendentals=0),
    )(*operands)


def dot_nn(a, b):
    return lax.dot_general(a, b, (((1,), (0,)), ((), ())), preferred_element_type=F32)


def dot_nt(a, b):
    return lax.dot_general(a, b, (((1,), (1,)), ((), ())), preferred_element_type=F32)


def doc_bounds(len_ref):
    ends = []
    total = 0
    for d in range(DOCS):
        total = total + len_ref[0, d] * BLOCK
        ends.append(total)
    return ends


def pack_kernel(group, len_ref, up_ref, q_ref, k_ref, v_ref, cot_ref, *outs):
    kv, qs, weighted = outs[:group], outs[group : 2 * group], outs[2 * group]
    rows = q_ref.shape[0]
    cols = q_ref.shape[1] // group
    place = lax.axis_index("seq")
    inner = lax.rem(place, group)
    for m in range(group):
        start = pl.multiple_of((inner ^ m) * cols, 128)
        kv[m][0:rows, :] = k_ref[:, pl.ds(start, cols)]
        kv[m][rows : 2 * rows, :] = v_ref[:, pl.ds(start, cols)]
        qs[m][...] = q_ref[:, pl.ds(start, cols)]
    ends = doc_bounds(len_ref)
    pos = place * rows + lax.broadcasted_iota(jnp.int32, (rows, 1), 0)
    factor = jnp.full((rows, 1), up_ref[0, 0], jnp.int32)
    for d in range(1, DOCS):
        factor = jnp.where(pos >= ends[d - 1], up_ref[0, d], factor)
    weighted[...] = (factor.astype(F32) * cot_ref[...].astype(F32)).astype(BF16)


def key_bias(len_ref, plane_start, block, rows, span):
    ends = doc_bounds(len_ref)
    first = plane_start + block * rows
    query = first + lax.broadcasted_iota(jnp.int32, (1, rows), 1)
    low = jnp.zeros((1, rows), jnp.int32)
    high = jnp.full((1, rows), ends[DOCS - 1], jnp.int32)
    for d in range(DOCS - 1):
        low = jnp.where(query >= ends[d], ends[d], low)
        high = jnp.where(query < ends[DOCS - 2 - d], ends[DOCS - 2 - d], high)
    low = jnp.maximum(low, query - WINDOW)
    high = jnp.minimum(high, query + WINDOW + 1)
    key = first - WINDOW + lax.broadcasted_iota(jnp.int32, (span, rows), 0)
    bias = jnp.where((key >= low) & (key < high), 0.0, MASKED).astype(F32)
    return jnp.concatenate([bias, bias], axis=1)


def stack_pair(block):
    lane = lax.broadcasted_iota(jnp.int32, block.shape, 1)
    zero = jnp.zeros_like(block)
    return jnp.concatenate(
        [jnp.where(lane < HEAD_DIM, block, zero), jnp.where(lane < HEAD_DIM, zero, block)], axis=0
    )


def unstack_pair(both, rows):
    return jnp.concatenate([both[:HEAD_DIM, :rows], both[HEAD_DIM:, rows:]], axis=0)


LOG2_SCALE = math.log2(math.e) * HEAD_DIM ** (-0.5)


def forward_kernel(group, len_ref, *refs):
    q_in, own, before, after = (refs[group * i : group * (i + 1)] for i in range(4))
    keys, vals, keys_t, queries, att_t, stats = refs[4 * group : 4 * group + 6]
    pieces = refs[4 * group + 6 : 5 * group + 6]
    vals_t, att = refs[5 * group + 6 :]
    rows, cols = q_in[0].shape
    plane = group * rows
    span = rows + 2 * WINDOW
    place = lax.axis_index("seq")
    inner = lax.rem(place, group)
    plane_start = (place - inner) * rows
    for m in range(group):
        spot = (inner ^ m) * rows
        queries[pl.ds(pl.multiple_of(spot, 128), rows), :] = q_in[m][...]
        for side, source in enumerate((before, own, after)):
            at = pl.ds(pl.multiple_of(side * plane + spot, 128), rows)
            keys[at, :] = source[m][0:rows, :]
            vals[at, :] = source[m][rows : 2 * rows, :]
    keys_t[...] = keys[...].T
    vals_t[...] = vals[...].T
    for block in range(group):
        bias = key_bias(len_ref, plane_start, block, rows, span)
        at = slice(block * rows, (block + 1) * rows)
        seen = slice(block * rows, block * rows + span)
        for pair in range(cols // PAIR):
            lanes = slice(pair * PAIR, (pair + 1) * PAIR)
            score = dot_nt(keys[seen, lanes], stack_pair(queries[at, lanes])) + bias
            peak = jnp.max(score, axis=0, keepdims=True)
            power = jnp.exp2((score - peak) * LOG2_SCALE)
            share = 1.0 / jnp.sum(power, axis=0, keepdims=True)
            unit = block * (cols // PAIR) + pair
            stats[unit, 0:1, :] = peak
            stats[unit, 1:2, :] = share
            prob = (power * share).astype(BF16)
            mixed = unstack_pair(dot_nn(vals_t[lanes, seen], prob), rows).astype(BF16)
            att_t[lanes, at] = mixed
            att[at, lanes] = mixed.T
    for m in range(group):
        pieces[m][...] = att[pl.ds(pl.multiple_of((inner ^ m) * rows, 128), rows), :]


def middle_kernel(group, fast, len_ref, att_t, near, far, *refs):
    grads = refs[:group]
    grad_att = refs[group]
    out = refs[group + 1 : -3]
    grad_all, weight, total = refs[-3:]
    rows = grads[0].shape[0]
    cols = att_t.shape[0]
    half = near.shape[0] // cols
    place = lax.axis_index("seq")
    inner = lax.rem(place, group)
    first = lax.axis_index("doc") if fast else 0
    start = pl.multiple_of(lax.rem(inner, half) * cols, 128)

    @pl.when(inner // half == first)
    def _():
        weight[...] = near[pl.ds(start, cols), :]

    @pl.when(inner // half != first)
    def _():
        weight[...] = far[pl.ds(start, cols), :]

    for m in range(group):
        grad_all[pl.ds(pl.multiple_of((inner ^ m) * rows, 128), rows), :] = grads[m][...]
    product = dot_nn(att_t[...], grad_all[...])
    if fast:
        total[...] = product.astype(BF16)
        count = len(out)
        part = cols // count
        outer = place // group
        for m in range(count):
            out[m][...] = total[pl.ds(pl.multiple_of((outer ^ m) * part, 16), part), :]
    else:
        out[0][...] = product
    grad_att[...] = dot_nt(grad_all[...], weight[...]).astype(BF16)


def project_kernel(group, fast, near, far, *refs):
    pieces, out, att = refs[:group], refs[group], refs[group + 1]
    cols = pieces[0].shape[1]
    depth = near.shape[0]
    inner = lax.rem(lax.axis_index("seq"), group)
    first = lax.axis_index("doc") if fast else 0
    for m in range(group):
        att[:, pl.ds(pl.multiple_of((inner ^ m) * cols, 128), cols)] = pieces[m][...]
    left = att[:, pl.ds(pl.multiple_of(first * depth, 128), depth)]
    right = att[:, pl.ds(pl.multiple_of((1 - first) * depth, 128), depth)]
    out[...] = (dot_nn(left, near[...]) + dot_nn(right, far[...])).astype(BF16)


def backward_kernel(
    group, pair, pairs, len_ref, keys, vals, keys_t, queries, grad_att, stats,
    to_before, own, to_after, grad_query, key_sum, value_sum,
):
    plane = queries.shape[0]
    rows = plane // group
    span = rows + 2 * WINDOW
    place = lax.axis_index("seq")
    plane_start = (place - lax.rem(place, group)) * rows
    lanes = slice(pair * PAIR, (pair + 1) * PAIR)
    key_sum[...] = jnp.zeros_like(key_sum)
    value_sum[...] = jnp.zeros_like(value_sum)
    for block in range(group):
        bias = key_bias(len_ref, plane_start, block, rows, span)
        at = slice(block * rows, (block + 1) * rows)
        seen = slice(block * rows, block * rows + span)
        unit = block * pairs + pair
        query = stack_pair(queries[at, lanes])
        grad = stack_pair(grad_att[at, lanes])
        score = dot_nt(keys[seen, lanes], query) + bias
        prob = jnp.exp2((score - stats[unit, 0:1, :]) * LOG2_SCALE) * stats[unit, 1:2, :]
        grad_prob = dot_nt(vals[seen, lanes], grad)
        centre = jnp.sum(prob * grad_prob, axis=0, keepdims=True)
        grad_score = (prob * (grad_prob - centre) * HEAD_DIM ** (-0.5)).astype(BF16)
        value_sum[seen, :] += dot_nn(prob.astype(BF16), grad)
        key_sum[seen, :] += dot_nn(grad_score, query)
        turned = unstack_pair(dot_nn(keys_t[lanes, seen], grad_score), rows)
        grad_query[at, :] = turned.astype(BF16).T
    for target, kept in ((to_before, 0), (own, plane), (to_after, 2 * plane)):
        target[0:plane, :] = key_sum[kept : kept + plane, :].astype(target.dtype)
        target[plane : 2 * plane, :] = value_sum[kept : kept + plane, :].astype(target.dtype)


def settle_kernel(group, own, from_after, from_before, grad_query, *pieces):
    plane = grad_query.shape[0]
    rows = plane // group
    inner = lax.rem(lax.axis_index("seq"), group)
    for m in range(group):
        spot = (inner ^ m) * rows
        pieces[m][0:rows, :] = grad_query[pl.ds(pl.multiple_of(spot, 128), rows), :]
        for part in range(2):
            at = pl.ds(pl.multiple_of(part * plane + spot, 128), rows)
            summed = own[at, :] + from_after[at, :].astype(F32) + from_before[at, :].astype(F32)
            pieces[m][(part + 1) * rows : (part + 2) * rows, :] = summed.astype(BF16)


def unpack_kernel(group, *refs):
    outs = refs[-3:]
    pieces = refs[:-3]
    pairs = len(pieces) // group
    rows = outs[0].shape[0]
    cols = outs[0].shape[1] // group
    inner = lax.rem(lax.axis_index("seq"), group)
    for pair in range(pairs):
        for m in range(group):
            at = pl.ds(pl.multiple_of((inner ^ m) * cols + pair * PAIR, 128), PAIR)
            for part in range(3):
                outs[part][:, at] = pieces[pair * group + m][part * rows : (part + 1) * rows, :]


def finish_kernel(group, count, scale, *refs):
    out = refs[-1]
    near, far = refs[:count], refs[count : 2 * count]
    place = lax.axis_index("seq")
    side = lax.rem(place, 2)
    outer = place // group
    part = near[0].shape[0]
    for source, base in ((near, side), (far, 1 - side)):
        for m in range(count):
            start = (base * count + (outer ^ m)) * part
            out[pl.ds(pl.multiple_of(start, 8), part), :] = source[m][...].astype(F32) * scale


def body(queries, key_rows, value_rows, cotangent, out_weight, lengths, upweight):
    rows = queries.shape[1]
    width = queries.shape[2]
    seq_count = lax.axis_size("seq")
    doc_count = lax.axis_size("doc")
    group = WINDOW // rows
    plane = group * rows
    cols = width // group
    pairs = cols // PAIR
    outer_count = seq_count // group
    units = group * pairs
    span = rows + 2 * WINDOW
    fast = doc_count == 2 and outer_count == 4 and group == 4
    scale = 1.0 / math.sqrt(rows * seq_count * doc_count)

    def inner_swap(value, m):
        return lax.ppermute(value, "seq", [(i, i ^ m) for i in range(seq_count)])

    def outer_swap(value, m):
        return lax.ppermute(value, "seq", [(i, i ^ (m * group)) for i in range(seq_count)])

    def outer_shift(value, step):
        pairs_of = [(i, i + step * group) for i in range(seq_count)]
        return lax.ppermute(value, "seq", [(a, b) for a, b in pairs_of if 0 <= b < seq_count])

    packed = call(
        functools.partial(pack_kernel, group),
        [((2 * rows, cols), BF16)] * group + [((rows, cols), BF16)] * group + [((rows, width), BF16)],
        (lengths, upweight, queries[0], key_rows[0], value_rows[0], cotangent[0]),
        scalars=2, flops=1 << 20, moved=4 << 20,
    )
    own_kv = [packed[0]] + [None] * (group - 1)
    order = list(range(group - 1, 0, -1))
    for m in order:
        own_kv[m] = inner_swap(packed[m], m)
    before = [outer_shift(own_kv[m], 1) for m in range(group)]
    after = [outer_shift(own_kv[m], -1) for m in range(group)]
    q_in = [packed[group]] + [inner_swap(packed[group + m], m) for m in range(1, group)]
    grads = {0: packed[2 * group]}
    step = group // 2
    while step > 0:
        grads.update({m | step: inner_swap(piece, step) for m, piece in grads.items()})
        step //= 2
    grads = [grads[m] for m in range(group)]
    if fast:
        near = out_weight
        far = lax.ppermute(out_weight, "doc", [(0, 1), (1, 0)])
    else:
        whole = lax.all_gather(out_weight, "doc", axis=0, tiled=True)
        near, far = whole[: width // 2], whole[width // 2 :]

    keys, vals, keys_t, query_all, att_t, stats, *att_pieces = call(
        functools.partial(forward_kernel, group),
        [((3 * plane, cols), BF16)] * 2
        + [((cols, 3 * plane), BF16), ((plane, cols), BF16), ((cols, plane), BF16)]
        + [((units, 8, 2 * rows), F32)]
        + [((rows, cols), BF16)] * group,
        (lengths, *q_in, *own_kv, *before, *after),
        scalars=1,
        scratch=[pltpu.VMEM((cols, 3 * plane), BF16), pltpu.VMEM((plane, cols), BF16)],
        flops=4 << 30, moved=4 << 20, vmem=32,
    )
    middle_out = (
        [((cols // outer_count, width), BF16)] * outer_count if fast else [((cols, width), F32)]
    )
    grad_att, *weight_parts = call(
        functools.partial(middle_kernel, group, fast),
        [((plane, cols), BF16)] + middle_out,
        (lengths, att_t, near, far, *grads),
        scalars=1,
        scratch=[
            pltpu.VMEM((plane, width), BF16),
            pltpu.VMEM((cols, width), BF16),
            pltpu.VMEM((cols, width), BF16),
        ],
        flops=1 << 30, moved=4 << 20,
    )

    if fast:
        swapped = [weight_parts[0]] + [outer_swap(weight_parts[m], m) for m in range(1, outer_count)]
        line = sum(part.astype(F32) for part in swapped).astype(BF16)
        half = group // 2
        flat = [(d, i) for d in range(doc_count) for i in range(seq_count)]
        first_pairs, second_pairs = [], []
        for d, i in flat:
            owner = (i % group) // half
            source = d * seq_count + i
            if d == owner:
                first_pairs.append((source, d * seq_count + (i ^ half)))
            else:
                first_pairs.append((source, owner * seq_count + i))
                second_pairs.append((source, owner * seq_count + (i ^ half)))
        got_first = lax.ppermute(line, ("doc", "seq"), first_pairs)
        got_second = lax.ppermute(line, ("doc", "seq"), second_pairs)
        inner = lax.axis_index("seq") % group
        is_owner = inner // half == lax.axis_index("doc")
        final = (
            got_first.astype(F32) + jnp.where(is_owner, line, got_second).astype(F32)
        ).astype(BF16)
        near_parts = [final] + [outer_swap(final, m) for m in range(1, outer_count)]
        far_parts = [inner_swap(part, 1) for part in near_parts]
        (grad_weight,) = call(
            functools.partial(finish_kernel, group, outer_count, scale),
            [((width // doc_count, width), F32)],
            (*near_parts, *far_parts), flops=1 << 20, moved=4 << 20,
        )
    else:
        inner = lax.axis_index("seq") % group
        placed = lax.dynamic_update_slice_in_dim(
            jnp.zeros((width, width), F32), weight_parts[0], inner * cols, 0
        )
        block = lax.psum_scatter(placed, "doc", scatter_dimension=0, tiled=True)
        grad_weight = lax.psum(block, "seq") * scale

    returned = []
    for pair in range(pairs):
        to_before, own, to_after, grad_query = call(
            functools.partial(backward_kernel, group, pair, pairs),
            [((2 * plane, PAIR), BF16), ((2 * plane, PAIR), F32), ((2 * plane, PAIR), BF16)]
            + [((plane, PAIR), BF16)],
            (lengths, keys, vals, keys_t, query_all, grad_att, stats),
            scalars=1,
            scratch=[pltpu.VMEM((3 * plane, PAIR), F32)] * 2,
            flops=4 << 30, moved=4 << 20, vmem=32,
        )
        from_after = outer_shift(to_before, -1)
        from_before = outer_shift(to_after, 1)
        pieces = call(
            functools.partial(settle_kernel, group),
            [((3 * rows, PAIR), BF16)] * group,
            (own, from_after, from_before, grad_query), flops=1 << 20, moved=2 << 20,
        )
        returned += [pieces[0]] + [inner_swap(pieces[m], m) for m in range(1, group)]
    grads_out = call(
        functools.partial(unpack_kernel, group),
        [((rows, width), BF16)] * 3,
        tuple(returned), flops=1 << 20, moved=2 << 20,
    )
    att_in = [att_pieces[0]] + [inner_swap(att_pieces[m], m) for m in range(1, group)]
    (layer_out,) = call(
        functools.partial(project_kernel, group, fast),
        [((rows, width), BF16)],
        (near, far, *att_in),
        scratch=[pltpu.VMEM((rows, width), BF16)],
        flops=1 << 30, moved=4 << 20,
    )
    grad_query, grad_key, grad_value = grads_out
    return (layer_out[None], grad_query[None], grad_key[None], grad_value[None], grad_weight)


def solution(mesh):
    spec = P("doc", "seq", None)
    return jax.shard_map(
        body,
        mesh=mesh,
        in_specs=(spec, spec, spec, spec, P("doc", None), P("doc", None), P("doc", None)),
        out_specs=(spec, spec, spec, spec, P("doc", None)),
        check_vma=False,
    )
```

time: 367 us -> 119 us (0.32)
  waiting for transfers between devices: 157 us -> 21.7 us
  matrix products: 85.2 us -> 0 us
  local copies, waits for them, and re-layouts: 55.6 us -> 5.79 us
  Pallas kernels: 0 us -> 26 us
  starting transfers between devices: 39 us -> 62 us
  between operations: 14.2 us -> 1.04 us
  other arithmetic: 12.7 us -> 1.75 us
    psum x1 -> x0, waiting for transfers between devices: 99.7 us -> none  [body(): weight_sum = lax.psum(row_block, 'seq')]
    dot_general x23 -> x0, matrix products: 66.2 us -> none  [the longest x4 20.2 us: backward_group(): jnp.einsum('hqk,qhd->khd', grad_score, query_grp, preferred_element_type=...]
    ppermute x16 -> x43, waiting for transfers between devices: 57.4 us -> 21.7 us  [the longest x6 9.8 us: outer_swap(): lax.ppermute(value, 'seq', [(i, i ^ m * group) for i in range(seq_count)])]
    pallas_call x0 -> x10, Pallas kernels: none -> 26 us  [call(): pl.pallas_call(kernel, out_shape=outs, in_specs=[SMEM] * scalars + [VMEM]...]
    dynamic_slice x28 -> x0, local copies, waits for them, and re-layouts: 25.1 us -> none  [the longest x8 9.87 us: group_slices(): lax.dynamic_slice_in_dim(key_ext, col_start, group_cols, 1)]
    ppermute x16 -> x43, starting transfers between devices: 38.7 us -> 62 us  [the longest x12 31.9 us: outer_shift(): lax.ppermute(value, 'seq', [(a, b) for a, b in pairs_of if 0 <= b < seq_c...]
    sub x8 -> x0, matrix products: 18.9 us -> none  [soft_weights(): exponent = jnp.exp(scores - row_peak)]
    dynamic_update_slice x32 -> x0, local copies, waits for them, and re-layouts: 12.4 us -> none  [the longest x8 4.98 us: backward_group(): lax.dynamic_update_slice(later_grad, both_parts[:, WINDOW + rows_here:].a...]
  transfers between devices with their start and end apart: 19 -> 43, of which waited for: 7 -> 9; matrix products, arithmetic and copies ran while one was open for 40% -> 1% of each run, Pallas kernels for 0% -> 21%
where the time goes in v1:
time: 119 us; the launch traced here: 118 us
  starting transfers between devices  62 us (52%)
  Pallas kernels  26 us (22%)
  waiting for transfers between devices  21.7 us (18%)
  local copies, waits for them, and re-layouts  5.79 us (5%)
  other arithmetic  1.75 us (1%)
    ppermute x12, starting transfers between devices, outer_shift(): lax.ppermute(value, 'seq', [(a, b) for a, b in pairs_of if 0 <= b < seq_c...  31.9 us
    pallas_call x10, Pallas kernels, call(): pl.pallas_call(kernel, out_shape=outs, in_specs=[SMEM] * scalars + [VMEM]...  26 us
    ppermute x22, starting transfers between devices, inner_swap(): return lax.ppermute(value, 'seq', [(i, i ^ m) for i in range(seq_count)])  16 us
    ppermute x6, waiting for transfers between devices, outer_swap(): lax.ppermute(value, 'seq', [(i, i ^ m * group) for i in range(seq_count)])  9.8 us
    ppermute x6, starting transfers between devices, outer_swap(): lax.ppermute(value, 'seq', [(i, i ^ m * group) for i in range(seq_count)])  8.89 us
    ppermute x12, waiting for transfers between devices, outer_shift(): lax.ppermute(value, 'seq', [(a, b) for a, b in pairs_of if 0 <= b < seq_c...  8.32 us
    unnamed x24, local copies, waits for them, and re-layouts  5.79 us
    ppermute x22, waiting for transfers between devices, inner_swap(): return lax.ppermute(value, 'seq', [(i, i ^ m) for i in range(seq_count)])  3.58 us
  transfers between devices with their start and end apart: 43, of which 9 were waited for; matrix products, arithmetic and copies ran while one was open for 1% of the time, Pallas kernels for 21%

profile of v1, /device:TPU:0, one launch (start us, length us, event | category | flops | bytes accessed | tf_op | source)
XLA Modules:
  0.0 118.3 jit_solution(17067168144817489611)
XLA Ops:
  0.6 3.0 %collective-permute-start = (bf16[512,1024]{1,0:T(8,128)(2,1)}, bf16[512,1024]{1,0:T(8,128)(2,1)S(1)}, u32[]{:S(2)}, u32[]{:S(2)}) collective-permute-start(bf16[512,1024]{1,0:T(8,128)(2,1)} %near.3), channel_id=1, source_target_pairs={{0,16},{16,0},{1,17},{17,1},{2,18},{18,2},{3,19},{19,3},{4,20},{20... | collective-permute-start | bytes 3145736 | tf_op jit(solution)/shard_map/ppermute | solution.py:314
  3.6 0.9 copy-done
  4.6 0.9 copy-done.1
  5.5 0.9 copy-done.2
  6.5 0.9 copy-done.3
  8.8 0.7 shard_map.110
  10.0 1.5 %collective-permute-start.2 = (bf16[128,256]{1,0:T(8,128)(2,1)S(1)}, bf16[128,256]{1,0:T(8,128)(2,1)S(1)}, u32[]{:S(2)}, u32[]{:S(2)}) collective-permute-start(bf16[128,256]{1,0:T(8,128)(2,1)S(1)} %get-tuple-element.50), channel_id=1, source_target_pairs={{0,2},{1,3},{2,0},{3,1},{4,6},{5,7},{6,4},{7,5},{8,10},{9,11},{10,... | collective-permute-start | bytes 196616 | tf_op jit(solution)/shard_map/ppermute | solution.py:284
  11.5 1.4 %collective-permute-start.5 = (bf16[256,256]{1,0:T(8,128)(2,1)S(1)}, bf16[256,256]{1,0:T(8,128)(2,1)S(1)}, u32[]{:S(2)}, u32[]{:S(2)}) collective-permute-start(bf16[256,256]{1,0:T(8,128)(2,1)S(1)} %get-tuple-element.54), channel_id=1, source_target_pairs={{0,2},{1,3},{2,0},{3,1},{4,6},{5,7},{6,4},{7,5},{8,10},{9,11},{10,... | collective-permute-start | bytes 393224 | tf_op jit(solution)/shard_map/ppermute | solution.py:284
  13.0 1.3 %collective-permute-done.2.refs_2_ = bf16[128,256]{1,0:T(8,128)(2,1)S(1)} collective-permute-done((bf16[128,256]{1,0:T(8,128)(2,1)S(1)}, bf16[128,256]{1,0:T(8,128)(2,1)S(1)}, u32[]{:S(2)}, u32[]{:S(2)}) %collective-permute-start.2) | collective-permute-done | bytes 65568 | tf_op jit(solution)/shard_map/ppermute | solution.py:284
  14.6 1.3 %collective-permute-done.3.refs_3_ = bf16[128,256]{1,0:T(8,128)(2,1)S(1)} collective-permute-done((bf16[128,256]{1,0:T(8,128)(2,1)S(1)}, bf16[128,256]{1,0:T(8,128)(2,1)S(1)}, u32[]{:S(2)}, u32[]{:S(2)}) %collective-permute-start.3) | collective-permute-done | bytes 65568 | tf_op jit(solution)/shard_map/ppermute | solution.py:284
  15.9 3.5 %collective-permute-start.7 = (bf16[256,256]{1,0:T(8,128)(2,1)S(1)}, bf16[256,256]{1,0:T(8,128)(2,1)S(1)}, u32[]{:S(2)}, u32[]{:S(2)}) collective-permute-start(bf16[256,256]{1,0:T(8,128)(2,1)S(1)} %get-tuple-element.52.refs_4_), channel_id=1, source_target_pairs={{0,4},{1,5},{2,6},{3,7},{4,8},{5,9},{6,10},{7,11},{8,12},{9,13},{1... | collective-permute-start | bytes 393224 | tf_op jit(solution)/shard_map/ppermute | solution.py:291
  19.4 1.3 %collective-permute-start.11 = (bf16[256,256]{1,0:T(8,128)(2,1)S(1)}, bf16[256,256]{1,0:T(8,128)(2,1)S(1)}, u32[]{:S(2)}, u32[]{:S(2)}) collective-permute-start(bf16[256,256]{1,0:T(8,128)(2,1)S(1)} %get-tuple-element.52.refs_4_), channel_id=1, source_target_pairs={{4,0},{5,1},{6,2},{7,3},{8,4},{9,5},{10,6},{11,7},{12,8},{13,9},{1... | collective-permute-start | bytes 393224 | tf_op jit(solution)/shard_map/ppermute | solution.py:291
  20.7 4.6 %collective-permute-start.8 = (bf16[256,256]{1,0:T(8,128)(2,1)S(1)}, bf16[256,256]{1,0:T(8,128)(2,1)S(1)}, u32[]{:S(2)}, u32[]{:S(2)}) collective-permute-start(bf16[256,256]{1,0:T(8,128)(2,1)S(1)} %collective-permute-done.4.refs_5_), channel_id=1, source_target_pairs={{0,4},{1,5},{2,6},{3,7},{4,8},{5,9},{6,10},{7,11},{8,12},{9,13},{1... | collective-permute-start | bytes 393224 | tf_op jit(solution)/shard_map/ppermute | solution.py:291
  25.9 3.5 %collective-permute-start.9 = (bf16[256,256]{1,0:T(8,128)(2,1)S(1)}, bf16[256,256]{1,0:T(8,128)(2,1)S(1)}, u32[]{:S(2)}, u32[]{:S(2)}) collective-permute-start(bf16[256,256]{1,0:T(8,128)(2,1)S(1)} %collective-permute-done.5.refs_6_), channel_id=1, source_target_pairs={{0,4},{1,5},{2,6},{3,7},{4,8},{5,9},{6,10},{7,11},{8,12},{9,13},{1... | collective-permute-start | bytes 393224 | tf_op jit(solution)/shard_map/ppermute | solution.py:291
  29.5 3.5 %collective-permute-start.10 = (bf16[256,256]{1,0:T(8,128)(2,1)S(1)}, bf16[256,256]{1,0:T(8,128)(2,1)S(1)}, u32[]{:S(2)}, u32[]{:S(2)}) collective-permute-start(bf16[256,256]{1,0:T(8,128)(2,1)S(1)} %collective-permute-done.6.refs_7_), channel_id=1, source_target_pairs={{0,4},{1,5},{2,6},{3,7},{4,8},{5,9},{6,10},{7,11},{8,12},{9,13},{1... | collective-permute-start | bytes 393224 | tf_op jit(solution)/shard_map/ppermute | solution.py:291
  33.0 1.3 %collective-permute-start.12 = (bf16[256,256]{1,0:T(8,128)(2,1)S(1)}, bf16[256,256]{1,0:T(8,128)(2,1)S(1)}, u32[]{:S(2)}, u32[]{:S(2)}) collective-permute-start(bf16[256,256]{1,0:T(8,128)(2,1)S(1)} %collective-permute-done.4.refs_5_), channel_id=1, source_target_pairs={{4,0},{5,1},{6,2},{7,3},{8,4},{9,5},{10,6},{11,7},{12,8},{13,9},{1... | collective-permute-start | bytes 393224 | tf_op jit(solution)/shard_map/ppermute | solution.py:291
  34.3 1.3 %collective-permute-start.13 = (bf16[256,256]{1,0:T(8,128)(2,1)S(1)}, bf16[256,256]{1,0:T(8,128)(2,1)S(1)}, u32[]{:S(2)}, u32[]{:S(2)}) collective-permute-start(bf16[256,256]{1,0:T(8,128)(2,1)S(1)} %collective-permute-done.5.refs_6_), channel_id=1, source_target_pairs={{4,0},{5,1},{6,2},{7,3},{8,4},{9,5},{10,6},{11,7},{12,8},{13,9},{1... | collective-permute-start | bytes 393224 | tf_op jit(solution)/shard_map/ppermute | solution.py:291
  35.9 1.3 %collective-permute-start.14 = (bf16[256,256]{1,0:T(8,128)(2,1)S(1)}, bf16[256,256]{1,0:T(8,128)(2,1)S(1)}, u32[]{:S(2)}, u32[]{:S(2)}) collective-permute-start(bf16[256,256]{1,0:T(8,128)(2,1)S(1)} %collective-permute-done.6.refs_7_), channel_id=1, source_target_pairs={{4,0},{5,1},{6,2},{7,3},{8,4},{9,5},{10,6},{11,7},{12,8},{13,9},{1... | collective-permute-start | bytes 393224 | tf_op jit(solution)/shard_map/ppermute | solution.py:291
  37.2 3.7 %collective-permute-done.12.refs_13_ = bf16[256,256]{1,0:T(8,128)(2,1)S(1)} collective-permute-done((bf16[256,256]{1,0:T(8,128)(2,1)S(1)}, bf16[256,256]{1,0:T(8,128)(2,1)S(1)}, u32[]{:S(2)}, u32[]{:S(2)}) %collective-permute-start.12) | collective-permute-done | bytes 131104 | tf_op jit(solution)/shard_map/ppermute | solution.py:291
  41.5 2.3 %collective-permute-done.13.refs_14_ = bf16[256,256]{1,0:T(8,128)(2,1)S(1)} collective-permute-done((bf16[256,256]{1,0:T(8,128)(2,1)S(1)}, bf16[256,256]{1,0:T(8,128)(2,1)S(1)}, u32[]{:S(2)}, u32[]{:S(2)}) %collective-permute-start.13) | collective-permute-done | bytes 131104 | tf_op jit(solution)/shard_map/ppermute | solution.py:291
  43.8 1.9 %collective-permute-done.14.refs_15_ = bf16[256,256]{1,0:T(8,128)(2,1)S(1)} collective-permute-done((bf16[256,256]{1,0:T(8,128)(2,1)S(1)}, bf16[256,256]{1,0:T(8,128)(2,1)S(1)}, u32[]{:S(2)}, u32[]{:S(2)}) %collective-permute-start.14) | collective-permute-done | bytes 131104 | tf_op jit(solution)/shard_map/ppermute | solution.py:291
  46.3 8.7 %shard_map.111 = (bf16[1536,256]{1,0:T(8,128)(2,1)S(1)}, bf16[1536,256]{1,0:T(8,128)(2,1)S(1)}, bf16[256,1536]{1,0:T(8,128)(2,1)S(1)}, bf16[512,256]{1,0:T(8,128...) custom-call(s32[1,4]{1,0:T(1,128)S(1)} %copy-done.6, ...), custom_call_target="tpu_custom_call" | custom-call | flops 4294967296 | bytes 4194304 | tf_op jit(solution)/shard_map/pallas_call | solution.py:27
  55.1 1.2 collective-permute-start.16
  56.3 1.6 %shard_map.113 = (bf16[512,256]{1,0:T(8,128)(2,1)S(1)}, bf16[64,1024]{1,0:T(8,128)(2,1)S(1)}, bf16[64,1024]{1,0:T(8,128)(2,1)S(1)}, bf16[64,1024]{1,0:T(8,128)(2,1)S(1)}, bf16[64,1024]{1,0:T(8,128)(2,1)S(1)}) custom-call(s32[1,4]{1,0:T(1,128)S(1)} %copy-done.6, bf16[256,512]{1,0:T(8,128)(2,1)S(1)} %get-tuple-element.64.att_t, ...), custom_call_target="tpu_custom_call" | custom-call | flops 1073741824 | bytes 4194304 | tf_op jit(solution)/shard_map/pallas_call | solution.py:27
  57.9 0.8 collective-permute-start.33
  58.7 1.6 %collective-permute-start.32 = (bf16[64,1024]{1,0:T(8,128)(2,1)S(1)}, bf16[64,1024]{1,0:T(8,128)(2,1)S(1)}, u32[]{:S(2)}, u32[]{:S(2)}) collective-permute-start(bf16[64,1024]{1,0:T(8,128)(2,1)S(1)} %get-tuple-element.89), channel_id=1, source_target_pairs={{0,8},{1,9},{2,10},{3,11},{4,12},{5,13},{6,14},{7,15},{8,0},{9,1},... | collective-permute-start | bytes 393224 | tf_op jit(solution)/shard_map/ppermute | solution.py:287
  60.3 2.1 %collective-permute-start.31 = (bf16[64,1024]{1,0:T(8,128)(2,1)S(1)}, bf16[64,1024]{1,0:T(8,128)(2,1)S(1)}, u32[]{:S(2)}, u32[]{:S(2)}) collective-permute-start(bf16[64,1024]{1,0:T(8,128)(2,1)S(1)} %get-tuple-element.88), channel_id=1, source_target_pairs={{0,4},{1,5},{2,6},{3,7},{4,0},{5,1},{6,2},{7,3},{8,12},{9,13},{10,... | collective-permute-start | bytes 393224 | tf_op jit(solution)/shard_map/ppermute | solution.py:287
  62.4 4.9 %shard_map.114 = (bf16[1024,128]{1,0:T(8,128)(2,1)S(1)}, f32[1024,128]{1,0:T(8,128)S(1)}, bf16[1024,128]{1,0:T(8,128)(2,1)S(1)}, bf16[512,128]{1,0:T(8,128)(2,1)S(1)}) custom-call(s32[1,4]{1,0:T(1,128)S(1)} %copy-done.6, bf16[1536,256]{1,0:T(8,128)(2,1)S(1)} %get-tuple-element.60.keys, bf16[1536,256]{1,0:T(8,128)(2,1)S(1)} %get-tuple-element.61.vals, ...), custom_call_target="tpu_custom_call" | custom-call | flops 4294967296 | bytes 4194304 | tf_op jit(solution)/shard_map/pallas_call | solution.py:27
  67.4 5.0 %collective-permute-done.32 = bf16[64,1024]{1,0:T(8,128)(2,1)S(1)} collective-permute-done((bf16[64,1024]{1,0:T(8,128)(2,1)S(1)}, bf16[64,1024]{1,0:T(8,128)(2,1)S(1)}, u32[]{:S(2)}, u32[]{:S(2)}) %collective-permute-start.32) | collective-permute-done | bytes 131104 | tf_op jit(solution)/shard_map/ppermute | solution.py:287
  72.3 1.3 %collective-permute-start.21 = (bf16[1024,128]{1,0:T(8,128)(2,1)S(1)}, bf16[1024,128]{1,0:T(8,128)(2,1)S(1)}, u32[]{:S(2)}, u32[]{:S(2)}) collective-permute-start(bf16[1024,128]{1,0:T(8,128)(2,1)S(1)} %get-tuple-element.69), channel_id=1, source_target_pairs={{4,0},{5,1},{6,2},{7,3},{8,4},{9,5},{10,6},{11,7},{12,8},{13,9},{1... | collective-permute-start | bytes 786440 | tf_op jit(solution)/shard_map/ppermute | solution.py:291
  73.6 4.6 %collective-permute-start.22 = (bf16[1024,128]{1,0:T(8,128)(2,1)S(1)}, bf16[1024,128]{1,0:T(8,128)(2,1)S(1)}, u32[]{:S(2)}, u32[]{:S(2)}) collective-permute-start(bf16[1024,128]{1,0:T(8,128)(2,1)S(1)} %get-tuple-element.70), channel_id=1, source_target_pairs={{0,4},{1,5},{2,6},{3,7},{4,8},{5,9},{6,10},{7,11},{8,12},{9,13},{1... | collective-permute-start | bytes 786440 | tf_op jit(solution)/shard_map/ppermute | solution.py:291
  78.2 0.7 add_convert_fusion.1
  78.9 0.9 collective-permute-start.34
  79.8 1.3 %collective-permute-start.35 = (bf16[64,1024]{1,0:T(8,128)(2,1)}, bf16[64,1024]{1,0:T(8,128)(2,1)}, u32[]{:S(2)}, u32[]{:S(2)}) collective-permute-start(bf16[64,1024]{1,0:T(8,128)(2,1)} %add_convert_fusion.1), channel_id=1, source_target_pairs={{2,16},{3,17},{6,20},{7,21},{10,24},{11,25},{14,28},{15,29},{16,2}... | collective-permute-start | bytes 393224 | tf_op jit(solution)/shard_map/ppermute | solution.py:361
  81.1 5.4 %shard_map.116 = (bf16[1024,128]{1,0:T(8,128)(2,1)}, f32[1024,128]{1,0:T(8,128)S(1)}, bf16[1024,128]{1,0:T(8,128)(2,1)}, bf16[512,128]{1,0:T(8,128)(2,1)S(1)}) custom-call(s32[1,4]{1,0:T(1,128)S(1)} %copy-done.6, bf16[1536,256]{1,0:T(8,128)(2,1)S(1)} %get-tuple-element.60.keys, bf16[1536,256]{1,0:T(8,128)(2,1)S(1)} %get-tuple-element.61.vals, ...), custom_call_target="tpu_custom_call" | custom-call | flops 4294967296 | bytes 4194304 | tf_op jit(solution)/shard_map/pallas_call | solution.py:27
  86.5 1.3 %collective-permute-start.26 = (bf16[1024,128]{1,0:T(8,128)(2,1)}, bf16[1024,128]{1,0:T(8,128)(2,1)S(1)}, u32[]{:S(2)}, u32[]{:S(2)}) collective-permute-start(bf16[1024,128]{1,0:T(8,128)(2,1)} %get-tuple-element.77), channel_id=1, source_target_pairs={{4,0},{5,1},{6,2},{7,3},{8,4},{9,5},{10,6},{11,7},{12,8},{13,9},{1... | collective-permute-start | bytes 786440 | tf_op jit(solution)/shard_map/ppermute | solution.py:291
  87.8 4.6 %collective-permute-start.27 = (bf16[1024,128]{1,0:T(8,128)(2,1)}, bf16[1024,128]{1,0:T(8,128)(2,1)S(1)}, u32[]{:S(2)}, u32[]{:S(2)}) collective-permute-start(bf16[1024,128]{1,0:T(8,128)(2,1)} %get-tuple-element.78), channel_id=1, source_target_pairs={{0,4},{1,5},{2,6},{3,7},{4,8},{5,9},{6,10},{7,11},{8,12},{9,13},{1... | collective-permute-start | bytes 786440 | tf_op jit(solution)/shard_map/ppermute | solution.py:291
  92.6 3.3 %collective-permute-start.24 = (bf16[384,128]{1,0:T(8,128)(2,1)S(1)}, bf16[384,128]{1,0:T(8,128)(2,1)S(1)}, u32[]{:S(2)}, u32[]{:S(2)}) collective-permute-start(bf16[384,128]{1,0:T(8,128)(2,1)S(1)} %get-tuple-element.74), channel_id=1, source_target_pairs={{0,2},{1,3},{2,0},{3,1},{4,6},{5,7},{6,4},{7,5},{8,10},{9,11},{10,... | collective-permute-start | bytes 294920 | tf_op jit(solution)/shard_map/ppermute | solution.py:284
  96.0 1.0 add_convert_fusion.refs_0_
  97.1 1.6 %collective-permute-start.37 = (bf16[64,1024]{1,0:T(8,128)(2,1)S(1)}, bf16[64,1024]{1,0:T(8,128)(2,1)S(1)}, u32[]{:S(2)}, u32[]{:S(2)}) collective-permute-start(bf16[64,1024]{1,0:T(8,128)(2,1)S(1)} %add_convert_fusion.refs_0_), channel_id=1, source_target_pairs={{0,8},{1,9},{2,10},{3,11},{4,12},{5,13},{6,14},{7,15},{8,0},{9,1},... | collective-permute-start | bytes 393224 | tf_op jit(solution)/shard_map/ppermute | solution.py:287
  98.8 2.7 %collective-permute-start.38 = (bf16[64,1024]{1,0:T(8,128)(2,1)S(1)}, bf16[64,1024]{1,0:T(8,128)(2,1)S(1)}, u32[]{:S(2)}, u32[]{:S(2)}) collective-permute-start(bf16[64,1024]{1,0:T(8,128)(2,1)S(1)} %add_convert_fusion.refs_0_), channel_id=1, source_target_pairs={{0,12},{1,13},{2,14},{3,15},{4,8},{5,9},{6,10},{7,11},{8,4},{9,5},... | collective-permute-start | bytes 393224 | tf_op jit(solution)/shard_map/ppermute | solution.py:287
  101.7 3.1 %collective-permute-start.29 = (bf16[384,128]{1,0:T(8,128)(2,1)S(1)}, bf16[384,128]{1,0:T(8,128)(2,1)S(1)}, u32[]{:S(2)}, u32[]{:S(2)}) collective-permute-start(bf16[384,128]{1,0:T(8,128)(2,1)S(1)} %get-tuple-element.82), channel_id=1, source_target_pairs={{0,2},{1,3},{2,0},{3,1},{4,6},{5,7},{6,4},{7,5},{8,10},{9,11},{10,... | collective-permute-start | bytes 294920 | tf_op jit(solution)/shard_map/ppermute | solution.py:284
  105.3 4.8 %collective-permute-done.37.refs_2_ = bf16[64,1024]{1,0:T(8,128)(2,1)S(1)} collective-permute-done((bf16[64,1024]{1,0:T(8,128)(2,1)S(1)}, bf16[64,1024]{1,0:T(8,128)(2,1)S(1)}, u32[]{:S(2)}, u32[]{:S(2)}) %collective-permute-start.37) | collective-permute-done | bytes 131104 | tf_op jit(solution)/shard_map/ppermute | solution.py:287
  110.6 2.1 %collective-permute-start.30 = (bf16[384,128]{1,0:T(8,128)(2,1)S(1)}, bf16[384,128]{1,0:T(8,128)(2,1)S(1)}, u32[]{:S(2)}, u32[]{:S(2)}) collective-permute-start(bf16[384,128]{1,0:T(8,128)(2,1)S(1)} %get-tuple-element.83), channel_id=1, source_target_pairs={{0,3},{1,2},{2,1},{3,0},{4,7},{5,6},{6,5},{7,4},{8,11},{9,10},{10,... | collective-permute-start | bytes 294920 | tf_op jit(solution)/shard_map/ppermute | solution.py:284
  112.7 2.0 %shard_map.112 = bf16[128,1024]{1,0:T(8,128)(2,1)} custom-call(bf16[512,1024]{1,0:T(8,128)(2,1)S(1)} %copy-done.7, bf16[512,1024]{1,0:T(8,128)(2,1)S(1)} %copy-done.9, bf16[128,256]{1,0:T(8,128)(2,1)S(1)} %copy-done.11, bf16[128,256]{1,0:T(8,128)(2,1)S(1)} %collective-permute-done.15.refs_1_, bf16[128,256]{1,0:T(8,128)(2,1)S(1)} %collective-permute-done.16.refs_2_, ...), custom_call_target="tpu_custom_call" | custom-call | flops 1073741824 | bytes 4194304 | tf_op jit(solution)/shard_map/pallas_call | solution.py:27
  114.8 0.9 collective-permute-done.30.refs_7_
  115.7 1.1 shard_map.118
  116.8 1.5 %shard_map.119 = f32[512,1024]{1,0:T(8,128)} custom-call(bf16[64,1024]{1,0:T(8,128)(2,1)S(1)} %add_convert_fusion.refs_0_, bf16[64,1024]{1,0:T(8,128)(2,1)S(1)} %collective-permute-done.36.refs_1_, bf16[64,1024]{1,0:T(8,128)(2,1)S(1)} %collective-permute-done.37.refs_2_, bf16[64,1024]{1,0:T(8,128)(2,1)S(1)} %collective-permute-done.38.refs_3_, ...), custom_call_target="tpu_custom_call" | custom-call | flops 1048576 | bytes 4194304 | tf_op jit(solution)/shard_map/pallas_call | solution.py:27
  (74 shorter events, 6.1 us)
Async XLA Ops:
  0.6 55.6 %collective-permute-start = (bf16[512,1024]{1,0:T(8,128)(2,1)}, bf16[512,1024]{1,0:T(8,128)(2,1)S(1)}, u32[]{:S(2)}, u32[]{:S(2)}) collective-permute-start(bf16[512,1024]{1,0:T(8,128)(2,1)} %near.3), channel_id=1, source_target_pairs={{0,16},{16,0},{1,17},{17,1},{2,18},{18,2},{3,19},{19,3},{4,20},{20... | collective-permute-start | bytes 3145736 | tf_op jit(solution)/shard_map/ppermute | solution.py:314
  9.4 10.0 %collective-permute-start.4 = (bf16[256,256]{1,0:T(8,128)(2,1)S(1)}, bf16[256,256]{1,0:T(8,128)(2,1)S(1)}, u32[]{:S(2)}, u32[]{:S(2)}) collective-permute-start(bf16[256,256]{1,0:T(8,128)(2,1)S(1)} %get-tuple-element.53), channel_id=1, source_target_pairs={{0,1},{1,0},{2,3},{3,2},{4,5},{5,4},{6,7},{7,6},{8,9},{9,8},{10,11... | collective-permute-start | bytes 393224 | tf_op jit(solution)/shard_map/ppermute | solution.py:284
  9.5 2.0 %collective-permute-start.1 = (bf16[128,256]{1,0:T(8,128)(2,1)S(1)}, bf16[128,256]{1,0:T(8,128)(2,1)S(1)}, u32[]{:S(2)}, u32[]{:S(2)}) collective-permute-start(bf16[128,256]{1,0:T(8,128)(2,1)S(1)} %get-tuple-element.49), channel_id=1, source_target_pairs={{0,1},{1,0},{2,3},{3,2},{4,5},{5,4},{6,7},{7,6},{8,9},{9,8},{10,11... | collective-permute-start | bytes 196616 | tf_op jit(solution)/shard_map/ppermute | solution.py:284
  10.0 4.3 %collective-permute-start.2 = (bf16[128,256]{1,0:T(8,128)(2,1)S(1)}, bf16[128,256]{1,0:T(8,128)(2,1)S(1)}, u32[]{:S(2)}, u32[]{:S(2)}) collective-permute-start(bf16[128,256]{1,0:T(8,128)(2,1)S(1)} %get-tuple-element.50), channel_id=1, source_target_pairs={{0,2},{1,3},{2,0},{3,1},{4,6},{5,7},{6,4},{7,5},{8,10},{9,11},{10,... | collective-permute-start | bytes 196616 | tf_op jit(solution)/shard_map/ppermute | solution.py:284
  11.5 4.4 %collective-permute-start.3 = (bf16[128,256]{1,0:T(8,128)(2,1)S(1)}, bf16[128,256]{1,0:T(8,128)(2,1)S(1)}, u32[]{:S(2)}, u32[]{:S(2)}) collective-permute-start(bf16[128,256]{1,0:T(8,128)(2,1)S(1)} %get-tuple-element.51), channel_id=1, source_target_pairs={{0,3},{1,2},{2,1},{3,0},{4,7},{5,6},{6,5},{7,4},{8,11},{9,10},{10,... | collective-permute-start | bytes 196616 | tf_op jit(solution)/shard_map/ppermute | solution.py:284
  11.5 9.2 %collective-permute-start.5 = (bf16[256,256]{1,0:T(8,128)(2,1)S(1)}, bf16[256,256]{1,0:T(8,128)(2,1)S(1)}, u32[]{:S(2)}, u32[]{:S(2)}) collective-permute-start(bf16[256,256]{1,0:T(8,128)(2,1)S(1)} %get-tuple-element.54), channel_id=1, source_target_pairs={{0,2},{1,3},{2,0},{3,1},{4,6},{5,7},{6,4},{7,5},{8,10},{9,11},{10,... | collective-permute-start | bytes 393224 | tf_op jit(solution)/shard_map/ppermute | solution.py:284
  14.3 11.0 %collective-permute-start.6 = (bf16[256,256]{1,0:T(8,128)(2,1)S(1)}, bf16[256,256]{1,0:T(8,128)(2,1)S(1)}, u32[]{:S(2)}, u32[]{:S(2)}) collective-permute-start(bf16[256,256]{1,0:T(8,128)(2,1)S(1)} %get-tuple-element.55), channel_id=1, source_target_pairs={{0,3},{1,2},{2,1},{3,0},{4,7},{5,6},{6,5},{7,4},{8,11},{9,10},{10,... | collective-permute-start | bytes 393224 | tf_op jit(solution)/shard_map/ppermute | solution.py:284
  15.9 10.0 %collective-permute-start.7 = (bf16[256,256]{1,0:T(8,128)(2,1)S(1)}, bf16[256,256]{1,0:T(8,128)(2,1)S(1)}, u32[]{:S(2)}, u32[]{:S(2)}) collective-permute-start(bf16[256,256]{1,0:T(8,128)(2,1)S(1)} %get-tuple-element.52.refs_4_), channel_id=1, source_target_pairs={{0,4},{1,5},{2,6},{3,7},{4,8},{5,9},{6,10},{7,11},{8,12},{9,13},{1... | collective-permute-start | bytes 393224 | tf_op jit(solution)/shard_map/ppermute | solution.py:291
  19.4 10.0 %collective-permute-start.11 = (bf16[256,256]{1,0:T(8,128)(2,1)S(1)}, bf16[256,256]{1,0:T(8,128)(2,1)S(1)}, u32[]{:S(2)}, u32[]{:S(2)}) collective-permute-start(bf16[256,256]{1,0:T(8,128)(2,1)S(1)} %get-tuple-element.52.refs_4_), channel_id=1, source_target_pairs={{4,0},{5,1},{6,2},{7,3},{8,4},{9,5},{10,6},{11,7},{12,8},{13,9},{1... | collective-permute-start | bytes 393224 | tf_op jit(solution)/shard_map/ppermute | solution.py:291
  20.7 12.2 %collective-permute-start.8 = (bf16[256,256]{1,0:T(8,128)(2,1)S(1)}, bf16[256,256]{1,0:T(8,128)(2,1)S(1)}, u32[]{:S(2)}, u32[]{:S(2)}) collective-permute-start(bf16[256,256]{1,0:T(8,128)(2,1)S(1)} %collective-permute-done.4.refs_5_), channel_id=1, source_target_pairs={{0,4},{1,5},{2,6},{3,7},{4,8},{5,9},{6,10},{7,11},{8,12},{9,13},{1... | collective-permute-start | bytes 393224 | tf_op jit(solution)/shard_map/ppermute | solution.py:291
  25.3 15.7 %collective-permute-start.19 = (bf16[128,1024]{1,0:T(8,128)(2,1)S(1)}, bf16[128,1024]{1,0:T(8,128)(2,1)S(1)}, u32[]{:S(2)}, u32[]{:S(2)}) collective-permute-start(bf16[128,1024]{1,0:T(8,128)(2,1)S(1)} %get-tuple-element.65.refs_0_), channel_id=1, source_target_pairs={{0,2},{1,3},{2,0},{3,1},{4,6},{5,7},{6,4},{7,5},{8,10},{9,11},{10,... | collective-permute-start | bytes 786440 | tf_op jit(solution)/shard_map/ppermute | solution.py:284
  25.9 8.3 %collective-permute-start.9 = (bf16[256,256]{1,0:T(8,128)(2,1)S(1)}, bf16[256,256]{1,0:T(8,128)(2,1)S(1)}, u32[]{:S(2)}, u32[]{:S(2)}) collective-permute-start(bf16[256,256]{1,0:T(8,128)(2,1)S(1)} %collective-permute-done.5.refs_6_), channel_id=1, source_target_pairs={{0,4},{1,5},{2,6},{3,7},{4,8},{5,9},{6,10},{7,11},{8,12},{9,13},{1... | collective-permute-start | bytes 393224 | tf_op jit(solution)/shard_map/ppermute | solution.py:291
  29.5 6.5 %collective-permute-start.10 = (bf16[256,256]{1,0:T(8,128)(2,1)S(1)}, bf16[256,256]{1,0:T(8,128)(2,1)S(1)}, u32[]{:S(2)}, u32[]{:S(2)}) collective-permute-start(bf16[256,256]{1,0:T(8,128)(2,1)S(1)} %collective-permute-done.6.refs_7_), channel_id=1, source_target_pairs={{0,4},{1,5},{2,6},{3,7},{4,8},{5,9},{6,10},{7,11},{8,12},{9,13},{1... | collective-permute-start | bytes 393224 | tf_op jit(solution)/shard_map/ppermute | solution.py:291
  33.0 8.0 %collective-permute-start.12 = (bf16[256,256]{1,0:T(8,128)(2,1)S(1)}, bf16[256,256]{1,0:T(8,128)(2,1)S(1)}, u32[]{:S(2)}, u32[]{:S(2)}) collective-permute-start(bf16[256,256]{1,0:T(8,128)(2,1)S(1)} %collective-permute-done.4.refs_5_), channel_id=1, source_target_pairs={{4,0},{5,1},{6,2},{7,3},{8,4},{9,5},{10,6},{11,7},{12,8},{13,9},{1... | collective-permute-start | bytes 393224 | tf_op jit(solution)/shard_map/ppermute | solution.py:291
  34.3 9.5 %collective-permute-start.13 = (bf16[256,256]{1,0:T(8,128)(2,1)S(1)}, bf16[256,256]{1,0:T(8,128)(2,1)S(1)}, u32[]{:S(2)}, u32[]{:S(2)}) collective-permute-start(bf16[256,256]{1,0:T(8,128)(2,1)S(1)} %collective-permute-done.5.refs_6_), channel_id=1, source_target_pairs={{4,0},{5,1},{6,2},{7,3},{8,4},{9,5},{10,6},{11,7},{12,8},{13,9},{1... | collective-permute-start | bytes 393224 | tf_op jit(solution)/shard_map/ppermute | solution.py:291
  35.9 9.7 %collective-permute-start.14 = (bf16[256,256]{1,0:T(8,128)(2,1)S(1)}, bf16[256,256]{1,0:T(8,128)(2,1)S(1)}, u32[]{:S(2)}, u32[]{:S(2)}) collective-permute-start(bf16[256,256]{1,0:T(8,128)(2,1)S(1)} %collective-permute-done.6.refs_7_), channel_id=1, source_target_pairs={{4,0},{5,1},{6,2},{7,3},{8,4},{9,5},{10,6},{11,7},{12,8},{13,9},{1... | collective-permute-start | bytes 393224 | tf_op jit(solution)/shard_map/ppermute | solution.py:291
  41.0 15.3 %collective-permute-start.18 = (bf16[128,1024]{1,0:T(8,128)(2,1)S(1)}, bf16[128,1024]{1,0:T(8,128)(2,1)S(1)}, u32[]{:S(2)}, u32[]{:S(2)}) collective-permute-start(bf16[128,1024]{1,0:T(8,128)(2,1)S(1)} %get-tuple-element.65.refs_0_), channel_id=1, source_target_pairs={{0,1},{1,0},{2,3},{3,2},{4,5},{5,4},{6,7},{7,6},{8,9},{9,8},{10,11... | collective-permute-start | bytes 786440 | tf_op jit(solution)/shard_map/ppermute | solution.py:284
  41.0 15.3 %collective-permute-start.20 = (bf16[128,1024]{1,0:T(8,128)(2,1)S(1)}, bf16[128,1024]{1,0:T(8,128)(2,1)S(1)}, u32[]{:S(2)}, u32[]{:S(2)}) collective-permute-start(bf16[128,1024]{1,0:T(8,128)(2,1)S(1)} %collective-permute-done.19.refs_2_), channel_id=1, source_target_pairs={{0,1},{1,0},{2,3},{3,2},{4,5},{5,4},{6,7},{7,6},{8,9},{9,8},{10,11... | collective-permute-start | bytes 786440 | tf_op jit(solution)/shard_map/ppermute | solution.py:284
  46.3 10.0 %copy-start.7 = (bf16[512,1024]{1,0:T(8,128)(2,1)S(1)}, bf16[512,1024]{1,0:T(8,128)(2,1)}, u32[]{:S(2)}) copy-start(bf16[512,1024]{1,0:T(8,128)(2,1)} %near.3) | copy-start | bytes 3145732
  55.1 7.3 %copy-start.10 = (bf16[128,256]{1,0:T(8,128)(2,1)}, bf16[128,256]{1,0:T(8,128)(2,1)S(1)}, u32[]{:S(2)}) copy-start(bf16[128,256]{1,0:T(8,128)(2,1)S(1)} %get-tuple-element.56.refs_0_) | copy-start | bytes 196612
  55.1 23.8 %collective-permute-start.15 = (bf16[128,256]{1,0:T(8,128)(2,1)S(1)}, bf16[128,256]{1,0:T(8,128)(2,1)S(1)}, u32[]{:S(2)}, u32[]{:S(2)}) collective-permute-start(bf16[128,256]{1,0:T(8,128)(2,1)S(1)} %get-tuple-element.57), channel_id=1, source_target_pairs={{0,1},{1,0},{2,3},{3,2},{4,5},{5,4},{6,7},{7,6},{8,9},{9,8},{10,11... | collective-permute-start | bytes 196616 | tf_op jit(solution)/shard_map/ppermute | solution.py:284
  55.1 24.7 %collective-permute-start.16 = (bf16[128,256]{1,0:T(8,128)(2,1)S(1)}, bf16[128,256]{1,0:T(8,128)(2,1)S(1)}, u32[]{:S(2)}, u32[]{:S(2)}) collective-permute-start(bf16[128,256]{1,0:T(8,128)(2,1)S(1)} %get-tuple-element.58), channel_id=1, source_target_pairs={{0,2},{1,3},{2,0},{3,1},{4,6},{5,7},{6,4},{7,5},{8,10},{9,11},{10,... | collective-permute-start | bytes 196616 | tf_op jit(solution)/shard_map/ppermute | solution.py:284
  56.3 11.0 %copy-start.8 = (bf16[512,1024]{1,0:T(8,128)(2,1)}, bf16[512,1024]{1,0:T(8,128)(2,1)S(1)}, u32[]{:S(2)}) copy-start(bf16[512,1024]{1,0:T(8,128)(2,1)S(1)} %collective-permute-done.far) | copy-start | bytes 3145732
  57.9 9.4 %collective-permute-start.33 = (bf16[64,1024]{1,0:T(8,128)(2,1)S(1)}, bf16[64,1024]{1,0:T(8,128)(2,1)S(1)}, u32[]{:S(2)}, u32[]{:S(2)}) collective-permute-start(bf16[64,1024]{1,0:T(8,128)(2,1)S(1)} %get-tuple-element.90), channel_id=1, source_target_pairs={{0,12},{1,13},{2,14},{3,15},{4,8},{5,9},{6,10},{7,11},{8,4},{9,5},... | collective-permute-start | bytes 393224 | tf_op jit(solution)/shard_map/ppermute | solution.py:287
  58.7 13.6 %collective-permute-start.32 = (bf16[64,1024]{1,0:T(8,128)(2,1)S(1)}, bf16[64,1024]{1,0:T(8,128)(2,1)S(1)}, u32[]{:S(2)}, u32[]{:S(2)}) collective-permute-start(bf16[64,1024]{1,0:T(8,128)(2,1)S(1)} %get-tuple-element.89), channel_id=1, source_target_pairs={{0,8},{1,9},{2,10},{3,11},{4,12},{5,13},{6,14},{7,15},{8,0},{9,1},... | collective-permute-start | bytes 393224 | tf_op jit(solution)/shard_map/ppermute | solution.py:287
  60.3 13.3 %collective-permute-start.31 = (bf16[64,1024]{1,0:T(8,128)(2,1)S(1)}, bf16[64,1024]{1,0:T(8,128)(2,1)S(1)}, u32[]{:S(2)}, u32[]{:S(2)}) collective-permute-start(bf16[64,1024]{1,0:T(8,128)(2,1)S(1)} %get-tuple-element.88), channel_id=1, source_target_pairs={{0,4},{1,5},{2,6},{3,7},{4,0},{5,1},{6,2},{7,3},{8,12},{9,13},{10,... | collective-permute-start | bytes 393224 | tf_op jit(solution)/shard_map/ppermute | solution.py:287
  67.3 25.3 %collective-permute-start.17 = (bf16[128,256]{1,0:T(8,128)(2,1)}, bf16[128,256]{1,0:T(8,128)(2,1)}, u32[]{:S(2)}, u32[]{:S(2)}) collective-permute-start(bf16[128,256]{1,0:T(8,128)(2,1)} %get-tuple-element.59), channel_id=1, source_target_pairs={{0,3},{1,2},{2,1},{3,0},{4,7},{5,6},{6,5},{7,4},{8,11},{9,10},{10,... | collective-permute-start | bytes 196616 | tf_op jit(solution)/shard_map/ppermute | solution.py:284
  72.3 14.2 %collective-permute-start.21 = (bf16[1024,128]{1,0:T(8,128)(2,1)S(1)}, bf16[1024,128]{1,0:T(8,128)(2,1)S(1)}, u32[]{:S(2)}, u32[]{:S(2)}) collective-permute-start(bf16[1024,128]{1,0:T(8,128)(2,1)S(1)} %get-tuple-element.69), channel_id=1, source_target_pairs={{4,0},{5,1},{6,2},{7,3},{8,4},{9,5},{10,6},{11,7},{12,8},{13,9},{1... | collective-permute-start | bytes 786440 | tf_op jit(solution)/shard_map/ppermute | solution.py:291
  73.6 14.2 %collective-permute-start.22 = (bf16[1024,128]{1,0:T(8,128)(2,1)S(1)}, bf16[1024,128]{1,0:T(8,128)(2,1)S(1)}, u32[]{:S(2)}, u32[]{:S(2)}) collective-permute-start(bf16[1024,128]{1,0:T(8,128)(2,1)S(1)} %get-tuple-element.70), channel_id=1, source_target_pairs={{0,4},{1,5},{2,6},{3,7},{4,8},{5,9},{6,10},{7,11},{8,12},{9,13},{1... | collective-permute-start | bytes 786440 | tf_op jit(solution)/shard_map/ppermute | solution.py:291
  78.9 13.7 %collective-permute-start.34 = (bf16[64,1024]{1,0:T(8,128)(2,1)}, bf16[64,1024]{1,0:T(8,128)(2,1)}, u32[]{:S(2)}, u32[]{:S(2)}) collective-permute-start(bf16[64,1024]{1,0:T(8,128)(2,1)} %add_convert_fusion.1), channel_id=1, source_target_pairs={{0,2},{1,3},{2,18},{3,19},{4,6},{5,7},{6,22},{7,23},{8,10},{9,11},... | collective-permute-start | bytes 393224 | tf_op jit(solution)/shard_map/ppermute | solution.py:360
  79.8 16.1 %collective-permute-start.35 = (bf16[64,1024]{1,0:T(8,128)(2,1)}, bf16[64,1024]{1,0:T(8,128)(2,1)}, u32[]{:S(2)}, u32[]{:S(2)}) collective-permute-start(bf16[64,1024]{1,0:T(8,128)(2,1)} %add_convert_fusion.1), channel_id=1, source_target_pairs={{2,16},{3,17},{6,20},{7,21},{10,24},{11,25},{14,28},{15,29},{16,2}... | collective-permute-start | bytes 393224 | tf_op jit(solution)/shard_map/ppermute | solution.py:361
  86.5 10.5 %collective-permute-start.26 = (bf16[1024,128]{1,0:T(8,128)(2,1)}, bf16[1024,128]{1,0:T(8,128)(2,1)S(1)}, u32[]{:S(2)}, u32[]{:S(2)}) collective-permute-start(bf16[1024,128]{1,0:T(8,128)(2,1)} %get-tuple-element.77), channel_id=1, source_target_pairs={{4,0},{5,1},{6,2},{7,3},{8,4},{9,5},{10,6},{11,7},{12,8},{13,9},{1... | collective-permute-start | bytes 786440 | tf_op jit(solution)/shard_map/ppermute | solution.py:291
  87.8 9.3 %collective-permute-start.27 = (bf16[1024,128]{1,0:T(8,128)(2,1)}, bf16[1024,128]{1,0:T(8,128)(2,1)S(1)}, u32[]{:S(2)}, u32[]{:S(2)}) collective-permute-start(bf16[1024,128]{1,0:T(8,128)(2,1)} %get-tuple-element.78), channel_id=1, source_target_pairs={{0,4},{1,5},{2,6},{3,7},{4,8},{5,9},{6,10},{7,11},{8,12},{9,13},{1... | collective-permute-start | bytes 786440 | tf_op jit(solution)/shard_map/ppermute | solution.py:291
  92.4 20.3 %copy-start.9 = (bf16[512,1024]{1,0:T(8,128)(2,1)S(1)}, bf16[512,1024]{1,0:T(8,128)(2,1)}, u32[]{:S(2)}) copy-start(bf16[512,1024]{1,0:T(8,128)(2,1)} %copy-done.8) | copy-start | bytes 3145732
  92.4 20.3 %copy-start.11 = (bf16[128,256]{1,0:T(8,128)(2,1)S(1)}, bf16[128,256]{1,0:T(8,128)(2,1)}, u32[]{:S(2)}) copy-start(bf16[128,256]{1,0:T(8,128)(2,1)} %copy-done.10) | copy-start | bytes 196612
  92.5 6.2 %collective-permute-start.23 = (bf16[384,128]{1,0:T(8,128)(2,1)S(1)}, bf16[384,128]{1,0:T(8,128)(2,1)S(1)}, u32[]{:S(2)}, u32[]{:S(2)}) collective-permute-start(bf16[384,128]{1,0:T(8,128)(2,1)S(1)} %get-tuple-element.73), channel_id=1, source_target_pairs={{0,1},{1,0},{2,3},{3,2},{4,5},{5,4},{6,7},{7,6},{8,9},{9,8},{10,11... | collective-permute-start | bytes 294920 | tf_op jit(solution)/shard_map/ppermute | solution.py:284
  92.6 9.0 %collective-permute-start.24 = (bf16[384,128]{1,0:T(8,128)(2,1)S(1)}, bf16[384,128]{1,0:T(8,128)(2,1)S(1)}, u32[]{:S(2)}, u32[]{:S(2)}) collective-permute-start(bf16[384,128]{1,0:T(8,128)(2,1)S(1)} %get-tuple-element.74), channel_id=1, source_target_pairs={{0,2},{1,3},{2,0},{3,1},{4,6},{5,7},{6,4},{7,5},{8,10},{9,11},{10,... | collective-permute-start | bytes 294920 | tf_op jit(solution)/shard_map/ppermute | solution.py:284
  95.9 5.8 %collective-permute-start.25 = (bf16[384,128]{1,0:T(8,128)(2,1)S(1)}, bf16[384,128]{1,0:T(8,128)(2,1)S(1)}, u32[]{:S(2)}, u32[]{:S(2)}) collective-permute-start(bf16[384,128]{1,0:T(8,128)(2,1)S(1)} %get-tuple-element.75), channel_id=1, source_target_pairs={{0,3},{1,2},{2,1},{3,0},{4,7},{5,6},{6,5},{7,4},{8,11},{9,10},{10,... | collective-permute-start | bytes 294920 | tf_op jit(solution)/shard_map/ppermute | solution.py:284
  97.0 7.9 %collective-permute-start.36 = (bf16[64,1024]{1,0:T(8,128)(2,1)S(1)}, bf16[64,1024]{1,0:T(8,128)(2,1)S(1)}, u32[]{:S(2)}, u32[]{:S(2)}) collective-permute-start(bf16[64,1024]{1,0:T(8,128)(2,1)S(1)} %add_convert_fusion.refs_0_), channel_id=1, source_target_pairs={{0,4},{1,5},{2,6},{3,7},{4,0},{5,1},{6,2},{7,3},{8,12},{9,13},{10,... | collective-permute-start | bytes 393224 | tf_op jit(solution)/shard_map/ppermute | solution.py:287
  97.1 13.0 %collective-permute-start.37 = (bf16[64,1024]{1,0:T(8,128)(2,1)S(1)}, bf16[64,1024]{1,0:T(8,128)(2,1)S(1)}, u32[]{:S(2)}, u32[]{:S(2)}) collective-permute-start(bf16[64,1024]{1,0:T(8,128)(2,1)S(1)} %add_convert_fusion.refs_0_), channel_id=1, source_target_pairs={{0,8},{1,9},{2,10},{3,11},{4,12},{5,13},{6,14},{7,15},{8,0},{9,1},... | collective-permute-start | bytes 393224 | tf_op jit(solution)/shard_map/ppermute | solution.py:287
  98.8 11.3 %collective-permute-start.38 = (bf16[64,1024]{1,0:T(8,128)(2,1)S(1)}, bf16[64,1024]{1,0:T(8,128)(2,1)S(1)}, u32[]{:S(2)}, u32[]{:S(2)}) collective-permute-start(bf16[64,1024]{1,0:T(8,128)(2,1)S(1)} %add_convert_fusion.refs_0_), channel_id=1, source_target_pairs={{0,12},{1,13},{2,14},{3,15},{4,8},{5,9},{6,10},{7,11},{8,4},{9,5},... | collective-permute-start | bytes 393224 | tf_op jit(solution)/shard_map/ppermute | solution.py:287
  101.6 3.2 %collective-permute-start.28 = (bf16[384,128]{1,0:T(8,128)(2,1)S(1)}, bf16[384,128]{1,0:T(8,128)(2,1)S(1)}, u32[]{:S(2)}, u32[]{:S(2)}) collective-permute-start(bf16[384,128]{1,0:T(8,128)(2,1)S(1)} %get-tuple-element.81), channel_id=1, source_target_pairs={{0,1},{1,0},{2,3},{3,2},{4,5},{5,4},{6,7},{7,6},{8,9},{9,8},{10,11... | collective-permute-start | bytes 294920 | tf_op jit(solution)/shard_map/ppermute | solution.py:284
  101.7 8.9 %collective-permute-start.29 = (bf16[384,128]{1,0:T(8,128)(2,1)S(1)}, bf16[384,128]{1,0:T(8,128)(2,1)S(1)}, u32[]{:S(2)}, u32[]{:S(2)}) collective-permute-start(bf16[384,128]{1,0:T(8,128)(2,1)S(1)} %get-tuple-element.82), channel_id=1, source_target_pairs={{0,2},{1,3},{2,0},{3,1},{4,6},{5,7},{6,4},{7,5},{8,10},{9,11},{10,... | collective-permute-start | bytes 294920 | tf_op jit(solution)/shard_map/ppermute | solution.py:284
  104.8 12.0 %collective-permute-start.39 = (bf16[64,1024]{1,0:T(8,128)(2,1)S(1)}, bf16[64,1024]{1,0:T(8,128)(2,1)S(1)}, u32[]{:S(2)}, u32[]{:S(2)}) collective-permute-start(bf16[64,1024]{1,0:T(8,128)(2,1)S(1)} %add_convert_fusion.refs_0_), channel_id=1, source_target_pairs={{0,1},{1,0},{2,3},{3,2},{4,5},{5,4},{6,7},{7,6},{8,9},{9,8},{10,11... | collective-permute-start | bytes 393224 | tf_op jit(solution)/shard_map/ppermute | solution.py:284
  104.9 11.8 %collective-permute-start.40 = (bf16[64,1024]{1,0:T(8,128)(2,1)S(1)}, bf16[64,1024]{1,0:T(8,128)(2,1)S(1)}, u32[]{:S(2)}, u32[]{:S(2)}) collective-permute-start(bf16[64,1024]{1,0:T(8,128)(2,1)S(1)} %collective-permute-done.36.refs_1_), channel_id=1, source_target_pairs={{0,1},{1,0},{2,3},{3,2},{4,5},{5,4},{6,7},{7,6},{8,9},{9,8},{10,11... | collective-permute-start | bytes 393224 | tf_op jit(solution)/shard_map/ppermute | solution.py:284
  110.1 6.7 %collective-permute-start.41 = (bf16[64,1024]{1,0:T(8,128)(2,1)S(1)}, bf16[64,1024]{1,0:T(8,128)(2,1)S(1)}, u32[]{:S(2)}, u32[]{:S(2)}) collective-permute-start(bf16[64,1024]{1,0:T(8,128)(2,1)S(1)} %collective-permute-done.37.refs_2_), channel_id=1, source_target_pairs={{0,1},{1,0},{2,3},{3,2},{4,5},{5,4},{6,7},{7,6},{8,9},{9,8},{10,11... | collective-permute-start | bytes 393224 | tf_op jit(solution)/shard_map/ppermute | solution.py:284
  110.1 6.7 %collective-permute-start.42 = (bf16[64,1024]{1,0:T(8,128)(2,1)S(1)}, bf16[64,1024]{1,0:T(8,128)(2,1)S(1)}, u32[]{:S(2)}, u32[]{:S(2)}) collective-permute-start(bf16[64,1024]{1,0:T(8,128)(2,1)S(1)} %collective-permute-done.38.refs_3_), channel_id=1, source_target_pairs={{0,1},{1,0},{2,3},{3,2},{4,5},{5,4},{6,7},{7,6},{8,9},{9,8},{10,11... | collective-permute-start | bytes 393224 | tf_op jit(solution)/shard_map/ppermute | solution.py:284
  110.6 5.0 %collective-permute-start.30 = (bf16[384,128]{1,0:T(8,128)(2,1)S(1)}, bf16[384,128]{1,0:T(8,128)(2,1)S(1)}, u32[]{:S(2)}, u32[]{:S(2)}) collective-permute-start(bf16[384,128]{1,0:T(8,128)(2,1)S(1)} %get-tuple-element.83), channel_id=1, source_target_pairs={{0,3},{1,2},{2,1},{3,0},{4,7},{5,6},{6,5},{7,4},{8,11},{9,10},{10,... | collective-permute-start | bytes 294920 | tf_op jit(solution)/shard_map/ppermute | solution.py:284
  (7 other events, 5.8 us)

commit v2 on v1

v2 whole, which is shorter than its diff:
```python
import functools
import math

import jax
import jax.numpy as jnp
from jax import lax
from jax.experimental import pallas as pl
from jax.experimental.pallas import tpu as pltpu
from jax.sharding import PartitionSpec as P

HEADS = 16
HEAD_DIM = 64
WINDOW = 512
BLOCK = 64
DOCS = 4
PAIR = 2 * HEAD_DIM
MASKED = -1e30
BF16 = jnp.bfloat16
F32 = jnp.float32

VMEM = pl.BlockSpec(memory_space=pltpu.VMEM)
HBM = pl.BlockSpec(memory_space=pltpu.HBM)
ANY = pl.BlockSpec(memory_space=pl.ANY)
SMEM = pl.BlockSpec(memory_space=pltpu.SMEM)


def call(kernel, out_shape, operands, hbm=0, after=(), scratch=(), flops=0, moved=0, vmem=24):
    outs = [jax.ShapeDtypeStruct(shape, kind) for shape, kind in out_shape]
    operands = [
        pltpu.with_memory_space_constraint(value, pltpu.HBM) if i < hbm else value
        for i, value in enumerate(operands)
    ]
    count = len(operands)

    def run(*refs):
        kernel(*refs[:count], *refs[count + len(after) :])

    return pl.pallas_call(
        run,
        out_shape=outs,
        in_specs=[HBM] * hbm + [VMEM] * (count - hbm) + [ANY] * len(after),
        out_specs=[VMEM] * len(outs),
        scratch_shapes=list(scratch),
        compiler_params=pltpu.CompilerParams(vmem_limit_bytes=vmem << 20),
        cost_estimate=pl.CostEstimate(flops=flops, bytes_accessed=moved, transcendentals=0),
    )(*operands, *after)


def dot_nn(a, b):
    return lax.dot_general(a, b, (((1,), (0,)), ((), ())), preferred_element_type=F32)


def dot_nt(a, b):
    return lax.dot_general(a, b, (((1,), (1,)), ((), ())), preferred_element_type=F32)


def doc_bounds(len_ref):
    ends = []
    total = 0
    for d in range(DOCS):
        total = total + len_ref[0, d] * BLOCK
        ends.append(total)
    return ends


def query_limits(len_ref, first, count):
    ends = doc_bounds(len_ref)
    query = first + lax.broadcasted_iota(jnp.int32, (1, count), 1)
    low = jnp.zeros((1, count), jnp.int32)
    high = jnp.full((1, count), ends[DOCS - 1], jnp.int32)
    for d in range(DOCS - 1):
        low = jnp.where(query >= ends[d], ends[d], low)
        high = jnp.where(query < ends[DOCS - 2 - d], ends[DOCS - 2 - d], high)
    return jnp.maximum(low, query - WINDOW), jnp.minimum(high, query + WINDOW + 1)


def pack_kernel(group, fast, len_hbm, up_hbm, k_hbm, v_hbm, q_hbm, cot_hbm, weight_hbm, *refs):
    own_kv, far_kv, own_rest, near_all, far_rest = (
        refs[0], refs[1 : group - 1], refs[group - 1], refs[group], refs[group + 1 : 2 * group - 1]
    )
    limits = refs[2 * group - 1]
    k_ref, v_ref, q_ref, cot_ref, len_ref, up_ref, sems = refs[-7:]
    copies = [(len_hbm, len_ref), (up_hbm, up_ref), (k_hbm, k_ref), (v_hbm, v_ref)]
    copies += [(q_hbm, q_ref), (cot_hbm, cot_ref)]
    rows = q_ref.shape[0]
    cols = q_ref.shape[1] // group
    place = lax.axis_index("seq")
    inner = lax.rem(place, group)
    if fast:
        start = pl.multiple_of(lax.rem(inner, 2) * cols, 128)
        copies += [(weight_hbm.at[pl.ds(start, cols)], refs[2 * group])]
    loads = [
        pltpu.make_async_copy(source, target, sems.at[i])
        for i, (source, target) in enumerate(copies)
    ]
    for load in loads:
        load.start()
    starts = [pl.multiple_of((inner ^ m) * cols, 128) for m in range(group)]
    loads[2].wait()
    loads[3].wait()
    for m, target in ((0, own_kv), (1, near_all), *((m, far_kv[m - 2]) for m in range(2, group))):
        target[0:rows, :] = k_ref[:, pl.ds(starts[m], cols)]
        target[rows : 2 * rows, :] = v_ref[:, pl.ds(starts[m], cols)]
    loads[0].wait()
    loads[1].wait()
    ends = doc_bounds(len_ref)
    low, high = query_limits(len_ref, (place - inner) * rows, group * rows)
    limits[0:1, :] = low
    limits[1:2, :] = high
    pos = place * rows + lax.broadcasted_iota(jnp.int32, (rows, 1), 0)
    factor = jnp.full((rows, 1), up_ref[0, 0], jnp.int32)
    for d in range(1, DOCS):
        factor = jnp.where(pos >= ends[d - 1], up_ref[0, d], factor)
    loads[4].wait()
    own_rest[0:rows, :] = q_ref[:, pl.ds(starts[0], cols)]
    near_all[2 * rows : 3 * rows, :] = q_ref[:, pl.ds(starts[1], cols)]
    for m in range(2, group):
        far_rest[m - 2][0:rows, :] = q_ref[:, pl.ds(starts[m], cols)]
    loads[5].wait()
    weighted = (factor.astype(F32) * cot_ref[...].astype(F32)).astype(BF16)
    for j in range(group):
        part = weighted[:, j * cols : (j + 1) * cols]
        own_rest[(j + 1) * rows : (j + 2) * rows, :] = part
        near_all[(j + 3) * rows : (j + 4) * rows, :] = part
        far_rest[0][(j + 1) * rows : (j + 2) * rows, :] = part
    if fast:
        loads[6].wait()


def join_kernel(parts, *refs):
    passed = (len(refs) - parts - 1) // 2
    out = refs[parts + passed]
    size = out.shape[0] // parts
    for m, source in enumerate(refs[:parts]):
        out[m * size : (m + 1) * size, :] = source[0:size, :]
    for source, target in zip(refs[parts : parts + passed], refs[parts + passed + 1 :]):
        target[...] = source[...]


def key_bias(limits, plane_start, block, rows, span):
    at = slice(block * rows, (block + 1) * rows)
    first = plane_start + (block * rows - WINDOW)
    key = first + lax.broadcasted_iota(jnp.int32, (span, rows), 0)
    seen = (key >= limits[0:1, at]) & (key < limits[1:2, at])
    bias = jnp.where(seen, 0.0, MASKED).astype(F32)
    return jnp.concatenate([bias, bias], axis=1)


def stack_pair(block):
    lane = lax.broadcasted_iota(jnp.int32, block.shape, 1)
    zero = jnp.zeros_like(block)
    return jnp.concatenate(
        [jnp.where(lane < HEAD_DIM, block, zero), jnp.where(lane < HEAD_DIM, zero, block)], axis=0
    )


def unstack_pair(both, rows):
    return jnp.concatenate([both[:HEAD_DIM, :rows], both[HEAD_DIM:, rows:]], axis=0)


LOG2_SCALE = math.log2(math.e) * HEAD_DIM ** (-0.5)


def forward_kernel(group, limits, *refs):
    own_kv, near_all = refs[0], refs[1]
    far_kv = refs[2:group]
    own_rest = refs[group]
    far_rest = refs[group + 1 : 2 * group - 1]
    sides = refs[2 * group - 1 : 2 * group + 1]
    keys, vals, keys_t, queries, att_t, att, stats, vals_t = refs[2 * group + 1 :]
    rows, cols = far_rest[-1].shape
    plane = group * rows
    span = rows + 2 * WINDOW
    place = lax.axis_index("seq")
    inner = lax.rem(place, group)
    plane_start = (place - inner) * rows
    even = 1 - lax.rem(place // group, 2)
    for m in range(group):
        spot = (inner ^ m) * rows
        asked = (own_rest, 0) if m == 0 else (near_all, 2 * rows) if m == 1 else (far_rest[m - 2], 0)
        at = pl.ds(pl.multiple_of(spot, 128), rows)
        queries[at, :] = asked[0][asked[1] : asked[1] + rows, :]
        held = own_kv if m == 0 else near_all if m == 1 else far_kv[m - 2]
        base = m * 2 * rows
        sources = [(held, 0, 1), (sides[0], base, 2 * even), (sides[1], base, 2 - 2 * even)]
        for source, base, side in sources:
            at = pl.ds(pl.multiple_of(side * plane + spot, 128), rows)
            keys[at, :] = source[base : base + rows, :]
            vals[at, :] = source[base + rows : base + 2 * rows, :]
    keys_t[...] = keys[...].T
    vals_t[...] = vals[...].T
    for block in range(group):
        bias = key_bias(limits, plane_start, block, rows, span)
        at = slice(block * rows, (block + 1) * rows)
        seen = slice(block * rows, block * rows + span)
        for pair in range(cols // PAIR):
            lanes = slice(pair * PAIR, (pair + 1) * PAIR)
            score = dot_nt(keys[seen, lanes], stack_pair(queries[at, lanes])) + bias
            peak = jnp.max(score, axis=0, keepdims=True)
            power = jnp.exp2((score - peak) * LOG2_SCALE)
            share = 1.0 / jnp.sum(power, axis=0, keepdims=True)
            unit = block * (cols // PAIR) + pair
            stats[unit, 0:1, :] = peak
            stats[unit, 1:2, :] = share
            prob = (power * share).astype(BF16)
            mixed = unstack_pair(dot_nn(vals_t[lanes, seen], prob), rows).astype(BF16)
            att_t[lanes, at] = mixed
            att[at, lanes] = mixed.T


def middle_kernel(group, fast, att_t, near, far, *refs):
    grads = refs[:group]
    grad_att = refs[group]
    out = refs[group + 1 : -3]
    grad_all, weight, total = refs[-3:]
    rows = grad_all.shape[0] // group
    cols = att_t.shape[0]
    place = lax.axis_index("seq")
    inner = lax.rem(place, group)
    if fast:
        is_near = inner // 2 == lax.axis_index("doc")

        @pl.when(is_near)
        def _():
            weight[...] = near[...]

        @pl.when(jnp.logical_not(is_near))
        def _():
            weight[...] = far[...]

    else:
        weight[...] = near[...]
    for m in range(group):
        skipped = grads[m].shape[0] - group * rows
        for j in range(group):
            grad_all[
                pl.ds(pl.multiple_of((inner ^ m) * rows, 128), rows), j * cols : (j + 1) * cols
            ] = grads[m][skipped + j * rows : skipped + (j + 1) * rows, :]
    product = dot_nn(att_t[...], grad_all[...])
    if fast:
        total[...] = product.astype(BF16)
        count = len(out)
        part = cols // count
        outer = place // group
        for m in range(count):
            out[m][...] = total[pl.ds(pl.multiple_of((outer ^ m) * part, 16), part), :]
    else:
        out[0][...] = product
    grad_att[...] = dot_nt(grad_all[...], weight[...]).astype(BF16)


def backward_kernel(
    group, limits, keys, vals, keys_t, queries, grad_att, stats,
    to_first, own, to_second, grad_query, key_sum, value_sum,
):
    plane, cols = queries.shape
    rows = plane // group
    span = rows + 2 * WINDOW
    pairs = cols // PAIR
    place = lax.axis_index("seq")
    plane_start = (place - lax.rem(place, group)) * rows
    key_sum[...] = jnp.zeros_like(key_sum)
    value_sum[...] = jnp.zeros_like(value_sum)
    for block in range(group):
        bias = key_bias(limits, plane_start, block, rows, span)
        at = slice(block * rows, (block + 1) * rows)
        seen = slice(block * rows, block * rows + span)
        for pair in range(pairs):
            lanes = slice(pair * PAIR, (pair + 1) * PAIR)
            unit = block * pairs + pair
            query = stack_pair(queries[at, lanes])
            grad = stack_pair(grad_att[at, lanes])
            score = dot_nt(keys[seen, lanes], query) + bias
            prob = jnp.exp2((score - stats[unit, 0:1, :]) * LOG2_SCALE) * stats[unit, 1:2, :]
            grad_prob = dot_nt(vals[seen, lanes], grad)
            centre = jnp.sum(prob * grad_prob, axis=0, keepdims=True)
            grad_score = (prob * (grad_prob - centre) * HEAD_DIM ** (-0.5)).astype(BF16)
            value_sum[seen, lanes] += dot_nn(prob.astype(BF16), grad)
            key_sum[seen, lanes] += dot_nn(grad_score, query)
            turned = unstack_pair(dot_nn(keys_t[lanes, seen], grad_score), rows)
            grad_query[at, lanes] = turned.astype(BF16).T
    even = 1 - lax.rem(place // group, 2)
    for target, side in ((to_first, 2 * even), (own, 1), (to_second, 2 - 2 * even)):
        kept = pl.ds(pl.multiple_of(side * plane, 128), plane)
        target[0:plane, :] = key_sum[kept, :].astype(target.dtype)
        target[plane : 2 * plane, :] = value_sum[kept, :].astype(target.dtype)


def settle_kernel(group, own, from_first, from_second, grad_query, att, *pieces):
    plane = grad_query.shape[0]
    rows = plane // group
    inner = lax.rem(lax.axis_index("seq"), group)
    for m in range(group):
        spot = (inner ^ m) * rows
        mine = pl.ds(pl.multiple_of(spot, 128), rows)
        pieces[m][0:rows, :] = grad_query[mine, :]
        for part in range(2):
            at = pl.ds(pl.multiple_of(part * plane + spot, 128), rows)
            summed = own[at, :] + from_first[at, :].astype(F32) + from_second[at, :].astype(F32)
            pieces[m][(part + 1) * rows : (part + 2) * rows, :] = summed.astype(BF16)
        pieces[m][3 * rows : 4 * rows, :] = att[mine, :]


def unpack_kernel(group, fast, near, far, farther, *refs):
    pieces, outs, out, att = refs[:group], refs[group : group + 3], refs[group + 3], refs[group + 4]
    rows, width = out.shape
    cols = width // group
    half = width // 2
    inner = lax.rem(lax.axis_index("seq"), group)
    first = lax.axis_index("doc") if fast else 0
    for m in range(group):
        at = pl.ds(pl.multiple_of((inner ^ m) * cols, 128), cols)
        for part in range(3):
            outs[part][:, at] = pieces[m][part * rows : (part + 1) * rows, :]
        att[:, at] = pieces[m][3 * rows : 4 * rows, :]
    total = dot_nn(att[:, pl.ds(pl.multiple_of(first * half, 128), half)], near[...])
    for side, weight in ((0, far), (1, farther)):
        start = (1 - first) * half + (lax.rem(inner, 2) ^ side) * cols
        total += dot_nn(att[:, pl.ds(pl.multiple_of(start, 128), cols)], weight[...])
    out[...] = total.astype(BF16)


def finish_kernel(group, count, scale, *refs):
    out = refs[-1]
    near, far = refs[:count], refs[count : 2 * count]
    place = lax.axis_index("seq")
    side = lax.rem(place, 2)
    outer = place // group
    part = near[0].shape[0]
    for source, base in ((near, side), (far, 1 - side)):
        for m in range(count):
            start = (base * count + (outer ^ m)) * part
            out[pl.ds(pl.multiple_of(start, 8), part), :] = source[m][...].astype(F32) * scale


def body(queries, key_rows, value_rows, cotangent, out_weight, lengths, upweight):
    rows = queries.shape[1]
    width = queries.shape[2]
    seq_count = lax.axis_size("seq")
    doc_count = lax.axis_size("doc")
    group = WINDOW // rows
    plane = group * rows
    cols = width // group
    pairs = cols // PAIR
    outer_count = seq_count // group
    units = group * pairs
    span = rows + 2 * WINDOW
    fast = doc_count == 2 and outer_count == 4
    scale = 1.0 / math.sqrt(rows * seq_count * doc_count)

    def inner_swap(value, m):
        return lax.ppermute(value, "seq", [(i, i ^ m) for i in range(seq_count)])

    def outer_swap(value, m):
        return lax.ppermute(value, "seq", [(i, i ^ (m * group)) for i in range(seq_count)])

    def outer_first(value):
        return outer_swap(value, 1)

    def outer_second(value):
        pairs_of = [(i, (((i // group + 1) ^ 1) - 1) * group + i % group) for i in range(seq_count)]
        return lax.ppermute(value, "seq", [(a, b) for a, b in pairs_of if 0 <= b < seq_count])

    tokens = (rows, width)
    rest = [(((1 + group) * rows, cols), BF16), ((rows, cols), BF16)]
    chunk = [((cols, width), BF16)] if fast else []
    own_kv, *packed = call(
        functools.partial(pack_kernel, group, fast),
        [((2 * rows, cols), BF16)] * (group - 1)
        + [rest[0], (((3 + group) * rows, cols), BF16), *rest]
        + [((8, plane), jnp.int32), *chunk],
        (lengths, upweight, key_rows[0], value_rows[0], queries[0], cotangent[0], out_weight),
        hbm=7,
        scratch=[pltpu.VMEM(tokens, BF16)] * 4
        + [pltpu.SMEM((1, DOCS), jnp.int32)] * 2
        + [pltpu.SemaphoreType.DMA((7,))],
        flops=1 << 20, moved=4 << 20,
    )
    far_kv = [inner_swap(packed[m - 2], m) for m in range(2, group)]
    own_rest, near_all, rest_first, rest_last, limits, *weight = packed[group - 2 :]
    near_all = inner_swap(near_all, 1)
    joined, rest_first, rest_last, *weight = call(
        functools.partial(join_kernel, group),
        [((2 * group * rows, cols), BF16), *rest, *chunk],
        (own_kv, near_all, *far_kv, rest_first, rest_last, *weight),
        flops=1 << 20, moved=1 << 20,
    )
    sides = [outer_first(joined), outer_second(joined)]
    far_rest = [inner_swap(rest_first, 2), inner_swap(rest_last, 3)]
    grads = [own_rest, near_all, far_rest[0], inner_swap(far_rest[0], 1)]
    inner = lax.axis_index("seq") % group
    if fast:
        near, half_near = weight[0], out_weight
        far = lax.ppermute(near, "doc", [(0, 1), (1, 0)])
        half_far = [far, inner_swap(far, 1)]
    else:
        whole = lax.all_gather(out_weight, "doc", axis=0, tiled=True)
        chunks = [lax.dynamic_slice_in_dim(whole, at * cols, cols, 0) for at in (
            inner, 2 + inner % 2, 2 + (inner + 1) % 2
        )]
        near = far = chunks[0]
        half_near, half_far = whole[: width // 2], chunks[1:]

    keys, vals, keys_t, query_all, att_t, att, stats = call(
        functools.partial(forward_kernel, group),
        [((3 * plane, cols), BF16)] * 2
        + [((cols, 3 * plane), BF16), ((plane, cols), BF16), ((cols, plane), BF16)]
        + [((plane, cols), BF16), ((units, 8, 2 * rows), F32)],
        (limits, own_kv, near_all, *far_kv, own_rest, *far_rest, *sides),
        scratch=[pltpu.VMEM((cols, 3 * plane), BF16)],
        flops=4 << 30, moved=4 << 20, vmem=32,
    )
    middle_out = (
        [((cols // outer_count, width), BF16)] * outer_count if fast else [((cols, width), F32)]
    )
    grad_att, *weight_parts = call(
        functools.partial(middle_kernel, group, fast),
        [((plane, cols), BF16)] + middle_out,
        (att_t, near, far, *grads),
        scratch=[
            pltpu.VMEM((plane, width), BF16),
            pltpu.VMEM((cols, width), BF16),
            pltpu.VMEM((cols, width), BF16),
        ],
        flops=1 << 30, moved=4 << 20,
    )

    if fast:
        swapped = [weight_parts[0]] + [outer_swap(weight_parts[m], m) for m in range(1, outer_count)]
        line = sum(part.astype(F32) for part in swapped).astype(BF16)
        flat = [(d, i) for d in range(doc_count) for i in range(seq_count)]
        first_pairs, second_pairs = [], []
        for d, i in flat:
            owner = (i % group) // 2
            source = d * seq_count + i
            if d == owner:
                first_pairs.append((source, d * seq_count + (i ^ 2)))
            else:
                first_pairs.append((source, owner * seq_count + i))
                second_pairs.append((source, owner * seq_count + (i ^ 2)))
        got_first = lax.ppermute(line, ("doc", "seq"), first_pairs)
        got_second = lax.ppermute(line, ("doc", "seq"), second_pairs)
        is_owner = inner // 2 == lax.axis_index("doc")
        final = (
            got_first.astype(F32) + jnp.where(is_owner, line, got_second).astype(F32)
        ).astype(BF16)
        before_settle = (final,)
        near_parts = [final] + [outer_swap(final, m) for m in range(1, outer_count)]
        far_parts = [inner_swap(part, 1) for part in near_parts]
        (grad_weight,) = call(
            functools.partial(finish_kernel, group, outer_count, scale),
            [((width // doc_count, width), F32)],
            (*near_parts, *far_parts), flops=1 << 20, moved=4 << 20,
        )
    else:
        placed = lax.dynamic_update_slice_in_dim(
            jnp.zeros((width, width), F32), weight_parts[0], inner * cols, 0
        )
        block = lax.psum_scatter(placed, "doc", scatter_dimension=0, tiled=True)
        grad_weight = lax.psum(block, "seq") * scale
        before_settle = ()

    to_first, own, to_second, grad_query = call(
        functools.partial(backward_kernel, group),
        [((2 * plane, cols), BF16), ((2 * plane, cols), F32), ((2 * plane, cols), BF16)]
        + [((plane, cols), BF16)],
        (limits, keys, vals, keys_t, query_all, grad_att, stats),
        after=half_far[1:],
        scratch=[pltpu.VMEM((3 * plane, cols), F32)] * 2,
        flops=8 << 30, moved=4 << 20, vmem=32,
    )
    pieces = call(
        functools.partial(settle_kernel, group),
        [((4 * rows, cols), BF16)] * group,
        (own, outer_first(to_first), outer_second(to_second), grad_query, att),
        after=before_settle, flops=1 << 20, moved=2 << 20,
    )
    pieces = [pieces[0]] + [inner_swap(pieces[m], m) for m in range(1, group)]
    grad_query, grad_key, grad_value, layer_out = call(
        functools.partial(unpack_kernel, group, fast),
        [((rows, width), BF16)] * 4,
        (half_near, *half_far, *pieces),
        scratch=[pltpu.VMEM((rows, width), BF16)],
        flops=1 << 30, moved=4 << 20,
    )
    return (layer_out[None], grad_query[None], grad_key[None], grad_value[None], grad_weight)


def solution(mesh):
    spec = P("doc", "seq", None)
    return jax.shard_map(
        body,
        mesh=mesh,
        in_specs=(spec, spec, spec, spec, P("doc", None), P("doc", None), P("doc", None)),
        out_specs=(spec, spec, spec, spec, P("doc", None)),
        check_vma=False,
    )
```

time: 119 us -> 89.4 us (0.75)
  starting transfers between devices: 62 us -> 28.4 us
  waiting for transfers between devices: 21.7 us -> 37.3 us
  local copies, waits for them, and re-layouts: 5.79 us -> 0.01 us
  Pallas kernels: 26 us -> 22 us
  other arithmetic: 1.75 us -> 0.13 us
    ppermute x13 -> x3, starting transfers between devices: 34.9 us -> 2.97 us  [the longest x1 1.6 us: body(): far = lax.ppermute(near, 'doc', [(0, 1), (1, 0)])]
    ppermute x22 -> x14, waiting for transfers between devices: 3.58 us -> 13.7 us  [inner_swap(): return lax.ppermute(value, 'seq', [(i, i ^ m) for i in range(seq_count)])]
    ppermute x22 -> x14, starting transfers between devices: 16 us -> 8.08 us  [inner_swap(): return lax.ppermute(value, 'seq', [(i, i ^ m) for i in range(seq_count)])]
    ppermute x6 -> x8, starting transfers between devices: 8.89 us -> 15.1 us  [outer_swap(): lax.ppermute(value, 'seq', [(i, i ^ m * group) for i in range(seq_count)])]
    unnamed x24 -> x6, local copies, waits for them, and re-layouts: 5.79 us -> 0.01 us
    pallas_call x10 -> x8, Pallas kernels: 26 us -> 22 us  [call(): pl.pallas_call(run, out_shape=outs, in_specs=[HBM] * hbm + [VMEM] * (coun...]
    ppermute x1, waiting for transfers between devices: 0.01 us -> 3.89 us  [body(): got_first = lax.ppermute(line, ('doc', 'seq'), first_pairs)]
    ppermute x6 -> x8, waiting for transfers between devices: 9.8 us -> 11.2 us  [outer_swap(): lax.ppermute(value, 'seq', [(i, i ^ m * group) for i in range(seq_count)])]
  transfers between devices with their start and end apart: 43 -> 27, of which waited for: 9 -> 11; matrix products, arithmetic and copies ran while one was open for 1% -> 0% of each run, Pallas kernels for 21% -> 22%
where the time goes in v2:
time: 89.4 us; the launch traced here: 88.7 us
  waiting for transfers between devices  37.3 us (42%)
  starting transfers between devices  28.4 us (32%)
  Pallas kernels  22 us (25%)
    pallas_call x8, Pallas kernels, call(): pl.pallas_call(run, out_shape=outs, in_specs=[HBM] * hbm + [VMEM] * (coun...  22 us
    ppermute x8, starting transfers between devices, outer_swap(): lax.ppermute(value, 'seq', [(i, i ^ m * group) for i in range(seq_count)])  15.1 us
    ppermute x14, waiting for transfers between devices, inner_swap(): return lax.ppermute(value, 'seq', [(i, i ^ m) for i in range(seq_count)])  13.7 us
    ppermute x8, waiting for transfers between devices, outer_swap(): lax.ppermute(value, 'seq', [(i, i ^ m * group) for i in range(seq_count)])  11.2 us
    ppermute x1, waiting for transfers between devices, body(): far = lax.ppermute(near, 'doc', [(0, 1), (1, 0)])  8.55 us
    ppermute x14, starting transfers between devices, inner_swap(): return lax.ppermute(value, 'seq', [(i, i ^ m) for i in range(seq_count)])  8.08 us
    ppermute x1, waiting for transfers between devices, body(): got_first = lax.ppermute(line, ('doc', 'seq'), first_pairs)  3.89 us
  transfers between devices with their start and end apart: 27, of which 11 were waited for; matrix products, arithmetic and copies ran while one was open for 0% of the time, Pallas kernels for 22%

profile of v2, /device:TPU:0, one launch (start us, length us, event | category | flops | bytes accessed | tf_op | source)
XLA Modules:
  0.0 88.7 jit_solution(2726217655498830631)
XLA Ops:
  0.6 1.4 %shard_map.110 = (bf16[256,256]{1,0:T(8,128)(2,1)S(1)}, bf16[256,256]{1,0:T(8,128)(2,1)S(1)}, bf16[256,256]{1,0:T(8,128)(2,1)S(1)}, bf16[640,256]{1,0:T(8,128)(2...) custom-call(s32[1,4]{1,0:T(1,128)} %refs_0_.2, ...), custom_call_target="tpu_custom_call" | custom-call | flops 1048576 | bytes 4194304 | tf_op jit(solution)/shard_map/pallas_call | solution.py:38
  2.1 0.5 collective-permute-start
  2.6 2.6 %collective-permute-start.1 = (bf16[256,256]{1,0:T(8,128)(2,1)S(1)}, bf16[256,256]{1,0:T(8,128)(2,1)S(1)}, u32[]{:S(2)}, u32[]{:S(2)}) collective-permute-start(bf16[256,256]{1,0:T(8,128)(2,1)S(1)} %get-tuple-element.44), channel_id=1, source_target_pairs={{0,2},{1,3},{2,0},{3,1},{4,6},{5,7},{6,4},{7,5},{8,10},{9,11},{10,... | collective-permute-start | bytes 393224 | tf_op jit(solution)/shard_map/ppermute | solution.py:352
  5.2 0.1 collective-permute-start.2
  5.3 4.3 %collective-permute-done.1.refs_2_.refs_3_ = bf16[256,256]{1,0:T(8,128)(2,1)S(1)} collective-permute-done((bf16[256,256]{1,0:T(8,128)(2,1)S(1)}, bf16[256,256]{1,0:T(8,128)(2,1)S(1)}, u32[]{:S(2)}, u32[]{:S(2)}) %collective-permute-start.1) | collective-permute-done | bytes 131104 | tf_op jit(solution)/shard_map/ppermute | solution.py:352
  9.5 2.3 %collective-permute-done.2.refs_3_.refs_4_ = bf16[256,256]{1,0:T(8,128)(2,1)S(1)} collective-permute-done((bf16[256,256]{1,0:T(8,128)(2,1)S(1)}, bf16[256,256]{1,0:T(8,128)(2,1)S(1)}, u32[]{:S(2)}, u32[]{:S(2)}) %collective-permute-start.2) | collective-permute-done | bytes 131104 | tf_op jit(solution)/shard_map/ppermute | solution.py:352
  11.8 0.1 shard_map.111
  11.9 1.6 %collective-permute-start.3 = (bf16[256,1024]{1,0:T(8,128)(2,1)S(1)}, bf16[256,1024]{1,0:T(8,128)(2,1)S(1)}, u32[]{:S(2)}, u32[]{:S(2)}) collective-permute-start(bf16[256,1024]{1,0:T(8,128)(2,1)S(1)} %get-tuple-element.49.refs_1_), channel_id=1, source_target_pairs={{0,16},{16,0},{1,17},{17,1},{2,18},{18,2},{3,19},{19,3},{4,20},{20... | collective-permute-start | bytes 1572872 | tf_op jit(solution)/shard_map/ppermute | solution.py:394
  13.5 1.6 %collective-permute-start.7 = (bf16[1024,256]{1,0:T(8,128)(2,1)S(1)}, bf16[1024,256]{1,0:T(8,128)(2,1)S(1)}, u32[]{:S(2)}, u32[]{:S(2)}) collective-permute-start(bf16[1024,256]{1,0:T(8,128)(2,1)S(1)} %get-tuple-element.54), channel_id=1, source_target_pairs={{0,4},{1,5},{2,6},{3,7},{4,0},{5,1},{6,2},{7,3},{8,12},{9,13},{10,... | collective-permute-start | bytes 1572872 | tf_op jit(solution)/shard_map/ppermute | solution.py:355
  15.1 0.7 collective-permute-start.8
  15.8 1.6 %collective-permute-start.5 = (bf16[640,256]{1,0:T(8,128)(2,1)S(1)}, bf16[640,256]{1,0:T(8,128)(2,1)S(1)}, u32[]{:S(2)}, u32[]{:S(2)}) collective-permute-start(bf16[640,256]{1,0:T(8,128)(2,1)S(1)} %get-tuple-element.52), channel_id=1, source_target_pairs={{0,2},{1,3},{2,0},{3,1},{4,6},{5,7},{6,4},{7,5},{8,10},{9,11},{10,... | collective-permute-start | bytes 983048 | tf_op jit(solution)/shard_map/ppermute | solution.py:352
  17.4 0.0 collective-permute-start.6
  17.4 8.6 %collective-permute-done.3.refs_2_.refs_1_ = bf16[256,1024]{1,0:T(8,128)(2,1)S(1)} collective-permute-done((bf16[256,1024]{1,0:T(8,128)(2,1)S(1)}, bf16[256,1024]{1,0:T(8,128)(2,1)S(1)}, u32[]{:S(2)}, u32[]{:S(2)}) %collective-permute-start.3) | collective-permute-done | bytes 524320 | tf_op jit(solution)/shard_map/ppermute | solution.py:394
  25.9 0.0 collective-permute-done.5.refs_6_.refs_5_
  25.9 0.5 collective-permute-start.9
  26.4 0.0 collective-permute-done.6.refs_7_
  26.4 0.9 %collective-permute-done.7.refs_8_ = bf16[1024,256]{1,0:T(8,128)(2,1)S(1)} collective-permute-done((bf16[1024,256]{1,0:T(8,128)(2,1)S(1)}, bf16[1024,256]{1,0:T(8,128)(2,1)S(1)}, u32[]{:S(2)}, u32[]{:S(2)}) %collective-permute-start.7) | collective-permute-done | bytes 524320 | tf_op jit(solution)/shard_map/ppermute | solution.py:355
  27.4 7.5 %shard_map.112 = (bf16[1536,256]{1,0:T(8,128)(2,1)S(1)}, bf16[1536,256]{1,0:T(8,128)(2,1)S(1)}, bf16[256,1536]{1,0:T(8,128)(2,1)S(1)}, bf16[512,256]{1,0:T(8,128...) custom-call(s32[8,512]{1,0:T(8,128)S(1)} %get-tuple-element.50.refs_0_, ...), custom_call_target="tpu_custom_call" | custom-call | flops 4294967296 | bytes 4194304 | tf_op jit(solution)/shard_map/pallas_call | solution.py:38
  34.9 1.1 %shard_map.113 = (bf16[512,256]{1,0:T(8,128)(2,1)S(1)}, bf16[64,1024]{1,0:T(8,128)(2,1)S(1)}, bf16[64,1024]{1,0:T(8,128)(2,1)S(1)}, bf16[64,1024]{1,0:T(8,128)(2,1)S(1)}, bf16[64,1024]{1,0:T(8,128)(2,1)S(1)}) custom-call(bf16[256,512]{1,0:T(8,128)(2,1)S(1)} %get-tuple-element.59.refs_0_, bf16[256,1024]{1,0:T(8,128)(2,1)S(1)} %get-tuple-element.49.refs_1_, ...), custom_call_target="tpu_custom_call" | custom-call | flops 1073741824 | bytes 4194304 | tf_op jit(solution)/shard_map/pallas_call | solution.py:38
  35.9 3.7 %collective-permute-start.14 = (bf16[64,1024]{1,0:T(8,128)(2,1)S(1)}, bf16[64,1024]{1,0:T(8,128)(2,1)S(1)}, u32[]{:S(2)}, u32[]{:S(2)}) collective-permute-start(bf16[64,1024]{1,0:T(8,128)(2,1)S(1)} %get-tuple-element.70), channel_id=1, source_target_pairs={{0,12},{1,13},{2,14},{3,15},{4,8},{5,9},{6,10},{7,11},{8,4},{9,5},... | collective-permute-start | bytes 393224 | tf_op jit(solution)/shard_map/ppermute | solution.py:355
  39.6 2.4 %collective-permute-start.13 = (bf16[64,1024]{1,0:T(8,128)(2,1)S(1)}, bf16[64,1024]{1,0:T(8,128)(2,1)S(1)}, u32[]{:S(2)}, u32[]{:S(2)}) collective-permute-start(bf16[64,1024]{1,0:T(8,128)(2,1)S(1)} %get-tuple-element.69), channel_id=1, source_target_pairs={{0,8},{1,9},{2,10},{3,11},{4,12},{5,13},{6,14},{7,15},{8,0},{9,1},... | collective-permute-start | bytes 393224 | tf_op jit(solution)/shard_map/ppermute | solution.py:355
  42.1 0.3 collective-permute-start.12
  42.3 9.0 %shard_map.114 = (bf16[1024,256]{1,0:T(8,128)(2,1)}, f32[1024,256]{1,0:T(8,128)S(1)}, bf16[1024,256]{1,0:T(8,128)(2,1)}, bf16[512,256]{1,0:T(8,128)(2,1)S(1)}) custom-call(s32[8,512]{1,0:T(8,128)S(1)} %get-tuple-element.50.refs_0_, bf16[1536,256]{1,0:T(8,128)(2,1)S(1)} %get-tuple-element.55.refs_1_, bf16[1536,256]{1,0:T(8,128)(2,1)S(1)} %get-tuple-element.56.refs_2_, ...), custom_call_target="tpu_custom_call" | custom-call | flops 8589934592 | bytes 4194304 | tf_op jit(solution)/shard_map/pallas_call | solution.py:38
  51.3 1.7 %collective-permute-start.10 = (bf16[1024,256]{1,0:T(8,128)(2,1)}, bf16[1024,256]{1,0:T(8,128)(2,1)S(1)}, u32[]{:S(2)}, u32[]{:S(2)}) collective-permute-start(bf16[1024,256]{1,0:T(8,128)(2,1)} %get-tuple-element.63), channel_id=1, source_target_pairs={{0,4},{1,5},{2,6},{3,7},{4,0},{5,1},{6,2},{7,3},{8,12},{9,13},{10,... | collective-permute-start | bytes 1572872 | tf_op jit(solution)/shard_map/ppermute | solution.py:355
  53.1 0.7 collective-permute-start.11
  53.8 0.1 add_convert_fusion.1
  53.9 1.6 %collective-permute-start.15 = (bf16[64,1024]{1,0:T(8,128)(2,1)S(1)}, bf16[64,1024]{1,0:T(8,128)(2,1)S(1)}, u32[]{:S(2)}, u32[]{:S(2)}) collective-permute-start(bf16[64,1024]{1,0:T(8,128)(2,1)S(1)} %add_convert_fusion.1), channel_id=1, source_target_pairs={{0,2},{1,3},{2,18},{3,19},{4,6},{5,7},{6,22},{7,23},{8,10},{9,11},... | collective-permute-start | bytes 393224 | tf_op jit(solution)/shard_map/ppermute | solution.py:441
  55.4 0.7 collective-permute-start.16
  56.1 3.9 %collective-permute-done.15 = bf16[64,1024]{1,0:T(8,128)(2,1)S(1)} collective-permute-done((bf16[64,1024]{1,0:T(8,128)(2,1)S(1)}, bf16[64,1024]{1,0:T(8,128)(2,1)S(1)}, u32[]{:S(2)}, u32[]{:S(2)}) %collective-permute-start.15) | collective-permute-done | bytes 131104 | tf_op jit(solution)/shard_map/ppermute | solution.py:441
  60.0 0.1 add_convert_fusion.refs_5_.refs_0_
  60.1 3.0 %collective-permute-start.20 = (bf16[64,1024]{1,0:T(8,128)(2,1)S(1)}, bf16[64,1024]{1,0:T(8,128)(2,1)S(1)}, u32[]{:S(2)}, u32[]{:S(2)}) collective-permute-start(bf16[64,1024]{1,0:T(8,128)(2,1)S(1)} %add_convert_fusion.refs_5_.refs_0_), channel_id=1, source_target_pairs={{0,4},{1,5},{2,6},{3,7},{4,0},{5,1},{6,2},{7,3},{8,12},{9,13},{10,... | collective-permute-start | bytes 393224 | tf_op jit(solution)/shard_map/ppermute | solution.py:355
  63.1 0.3 collective-permute-start.21
  63.4 2.1 %collective-permute-start.22 = (bf16[64,1024]{1,0:T(8,128)(2,1)S(1)}, bf16[64,1024]{1,0:T(8,128)(2,1)S(1)}, u32[]{:S(2)}, u32[]{:S(2)}) collective-permute-start(bf16[64,1024]{1,0:T(8,128)(2,1)S(1)} %add_convert_fusion.refs_5_.refs_0_), channel_id=1, source_target_pairs={{0,12},{1,13},{2,14},{3,15},{4,8},{5,9},{6,10},{7,11},{8,4},{9,5},... | collective-permute-start | bytes 393224 | tf_op jit(solution)/shard_map/ppermute | solution.py:355
  65.5 2.9 %collective-permute-done.20.refs_1_ = bf16[64,1024]{1,0:T(8,128)(2,1)S(1)} collective-permute-done((bf16[64,1024]{1,0:T(8,128)(2,1)S(1)}, bf16[64,1024]{1,0:T(8,128)(2,1)S(1)}, u32[]{:S(2)}, u32[]{:S(2)}) %collective-permute-start.20) | collective-permute-done | bytes 131104 | tf_op jit(solution)/shard_map/ppermute | solution.py:355
  68.5 0.5 collective-permute-start.24
  69.0 0.2 shard_map.115
  69.1 0.0 copy-start
  69.2 0.1 collective-permute-start.17
  69.3 7.3 %collective-permute-done.21.refs_2_ = bf16[64,1024]{1,0:T(8,128)(2,1)S(1)} collective-permute-done((bf16[64,1024]{1,0:T(8,128)(2,1)S(1)}, bf16[64,1024]{1,0:T(8,128)(2,1)S(1)}, u32[]{:S(2)}, u32[]{:S(2)}) %collective-permute-start.21) | collective-permute-done | bytes 131104 | tf_op jit(solution)/shard_map/ppermute | solution.py:355
  76.6 1.3 %collective-permute-start.18 = (bf16[512,256]{1,0:T(8,128)(2,1)S(1)}, bf16[512,256]{1,0:T(8,128)(2,1)S(1)}, u32[]{:S(2)}, u32[]{:S(2)}) collective-permute-start(bf16[512,256]{1,0:T(8,128)(2,1)S(1)} %get-tuple-element.73), channel_id=1, source_target_pairs={{0,2},{1,3},{2,0},{3,1},{4,6},{5,7},{6,4},{7,5},{8,10},{9,11},{10,... | collective-permute-start | bytes 786440 | tf_op jit(solution)/shard_map/ppermute | solution.py:352
  77.9 0.9 collective-permute-start.25
  78.7 0.1 collective-permute-start.26
  78.8 0.9 %collective-permute-done.25.refs_6_ = bf16[64,1024]{1,0:T(8,128)(2,1)S(1)} collective-permute-done((bf16[64,1024]{1,0:T(8,128)(2,1)S(1)}, bf16[64,1024]{1,0:T(8,128)(2,1)S(1)}, u32[]{:S(2)}, u32[]{:S(2)}) %collective-permute-start.25) | collective-permute-done | bytes 131104 | tf_op jit(solution)/shard_map/ppermute | solution.py:352
  79.7 0.4 collective-permute-done.26.refs_7_
  80.1 1.5 %shard_map.117 = f32[512,1024]{1,0:T(8,128)} custom-call(bf16[64,1024]{1,0:T(8,128)(2,1)S(1)} %add_convert_fusion.refs_5_.refs_0_, bf16[64,1024]{1,0:T(8,128)(2,1)S(1)} %collective-permute-done.20.refs_1_, bf16[64,1024]{1,0:T(8,128)(2,1)S(1)} %collective-permute-done.21.refs_2_, bf16[64,1024]{1,0:T(8,128)(2,1)S(1)} %collective-permute-done.22.refs_3_, ...), custom_call_target="tpu_custom_call" | custom-call | flops 1048576 | bytes 4194304 | tf_op jit(solution)/shard_map/pallas_call | solution.py:38
  81.5 3.5 %collective-permute-done.18.refs_5_ = bf16[512,256]{1,0:T(8,128)(2,1)S(1)} collective-permute-done((bf16[512,256]{1,0:T(8,128)(2,1)S(1)}, bf16[512,256]{1,0:T(8,128)(2,1)S(1)}, u32[]{:S(2)}, u32[]{:S(2)}) %collective-permute-start.18) | collective-permute-done | bytes 262176 | tf_op jit(solution)/shard_map/ppermute | solution.py:352
  85.1 2.3 %collective-permute-done.19.refs_6_ = bf16[512,256]{1,0:T(8,128)(2,1)S(1)} collective-permute-done((bf16[512,256]{1,0:T(8,128)(2,1)S(1)}, bf16[512,256]{1,0:T(8,128)(2,1)S(1)}, u32[]{:S(2)}, u32[]{:S(2)}) %collective-permute-start.19) | collective-permute-done | bytes 262176 | tf_op jit(solution)/shard_map/ppermute | solution.py:352
  87.4 1.3 %shard_map.116 = (bf16[128,1024]{1,0:T(8,128)(2,1)}, bf16[128,1024]{1,0:T(8,128)(2,1)}, bf16[128,1024]{1,0:T(8,128)(2,1)}, bf16[128,1024]{1,0:T(8,128)(2,1)}) custom-call(bf16[512,1024]{1,0:T(8,128)(2,1)S(1)} %copy-done, bf16[256,1024]{1,0:T(8,128)(2,1)S(1)} %collective-permute-done.3.refs_2_.refs_1_, bf16[256,1024]{1,0:T(8,128)(2,1)S(1)} %copy-done.2, ...), custom_call_target="tpu_custom_call" | custom-call | flops 1073741824 | bytes 4194304 | tf_op jit(solution)/shard_map/pallas_call | solution.py:38
  (22 shorter events, 0.1 us)
Async XLA Ops:
  2.1 9.8 %collective-permute-start = (bf16[896,256]{1,0:T(8,128)(2,1)S(1)}, bf16[896,256]{1,0:T(8,128)(2,1)S(1)}, u32[]{:S(2)}, u32[]{:S(2)}) collective-permute-start(bf16[896,256]{1,0:T(8,128)(2,1)S(1)} %get-tuple-element.43), channel_id=1, source_target_pairs={{0,1},{1,0},{2,3},{3,2},{4,5},{5,4},{6,7},{7,6},{8,9},{9,8},{10,11... | collective-permute-start | bytes 1376264 | tf_op jit(solution)/shard_map/ppermute | solution.py:352
  2.6 6.9 %collective-permute-start.1 = (bf16[256,256]{1,0:T(8,128)(2,1)S(1)}, bf16[256,256]{1,0:T(8,128)(2,1)S(1)}, u32[]{:S(2)}, u32[]{:S(2)}) collective-permute-start(bf16[256,256]{1,0:T(8,128)(2,1)S(1)} %get-tuple-element.44), channel_id=1, source_target_pairs={{0,2},{1,3},{2,0},{3,1},{4,6},{5,7},{6,4},{7,5},{8,10},{9,11},{10,... | collective-permute-start | bytes 393224 | tf_op jit(solution)/shard_map/ppermute | solution.py:352
  5.2 6.6 %collective-permute-start.2 = (bf16[256,256]{1,0:T(8,128)(2,1)S(1)}, bf16[256,256]{1,0:T(8,128)(2,1)S(1)}, u32[]{:S(2)}, u32[]{:S(2)}) collective-permute-start(bf16[256,256]{1,0:T(8,128)(2,1)S(1)} %get-tuple-element.45), channel_id=1, source_target_pairs={{0,3},{1,2},{2,1},{3,0},{4,7},{5,6},{6,5},{7,4},{8,11},{9,10},{10,... | collective-permute-start | bytes 393224 | tf_op jit(solution)/shard_map/ppermute | solution.py:352
  11.9 14.0 %collective-permute-start.3 = (bf16[256,1024]{1,0:T(8,128)(2,1)S(1)}, bf16[256,1024]{1,0:T(8,128)(2,1)S(1)}, u32[]{:S(2)}, u32[]{:S(2)}) collective-permute-start(bf16[256,1024]{1,0:T(8,128)(2,1)S(1)} %get-tuple-element.49.refs_1_), channel_id=1, source_target_pairs={{0,16},{16,0},{1,17},{17,1},{2,18},{18,2},{3,19},{19,3},{4,20},{20... | collective-permute-start | bytes 1572872 | tf_op jit(solution)/shard_map/ppermute | solution.py:394
  13.5 13.8 %collective-permute-start.7 = (bf16[1024,256]{1,0:T(8,128)(2,1)S(1)}, bf16[1024,256]{1,0:T(8,128)(2,1)S(1)}, u32[]{:S(2)}, u32[]{:S(2)}) collective-permute-start(bf16[1024,256]{1,0:T(8,128)(2,1)S(1)} %get-tuple-element.54), channel_id=1, source_target_pairs={{0,4},{1,5},{2,6},{3,7},{4,0},{5,1},{6,2},{7,3},{8,12},{9,13},{10,... | collective-permute-start | bytes 1572872 | tf_op jit(solution)/shard_map/ppermute | solution.py:355
  15.1 12.3 %collective-permute-start.8 = (bf16[1024,256]{1,0:T(8,128)(2,1)S(1)}, bf16[1024,256]{1,0:T(8,128)(2,1)S(1)}, u32[]{:S(2)}, u32[]{:S(2)}) collective-permute-start(bf16[1024,256]{1,0:T(8,128)(2,1)S(1)} %get-tuple-element.54), channel_id=1, source_target_pairs={{4,8},{5,9},{6,10},{7,11},{8,4},{9,5},{10,6},{11,7},{20,24},{21,25... | collective-permute-start | bytes 1572872 | tf_op jit(solution)/shard_map/ppermute | solution.py:362
  15.8 10.1 %collective-permute-start.5 = (bf16[640,256]{1,0:T(8,128)(2,1)S(1)}, bf16[640,256]{1,0:T(8,128)(2,1)S(1)}, u32[]{:S(2)}, u32[]{:S(2)}) collective-permute-start(bf16[640,256]{1,0:T(8,128)(2,1)S(1)} %get-tuple-element.52), channel_id=1, source_target_pairs={{0,2},{1,3},{2,0},{3,1},{4,6},{5,7},{6,4},{7,5},{8,10},{9,11},{10,... | collective-permute-start | bytes 983048 | tf_op jit(solution)/shard_map/ppermute | solution.py:352
  17.4 9.1 %collective-permute-start.6 = (bf16[128,256]{1,0:T(8,128)(2,1)S(1)}, bf16[128,256]{1,0:T(8,128)(2,1)S(1)}, u32[]{:S(2)}, u32[]{:S(2)}) collective-permute-start(bf16[128,256]{1,0:T(8,128)(2,1)S(1)} %get-tuple-element.53), channel_id=1, source_target_pairs={{0,3},{1,2},{2,1},{3,0},{4,7},{5,6},{6,5},{7,4},{8,11},{9,10},{10,... | collective-permute-start | bytes 196616 | tf_op jit(solution)/shard_map/ppermute | solution.py:352
  25.9 16.4 %collective-permute-start.4 = (bf16[256,1024]{1,0:T(8,128)(2,1)S(1)}, bf16[256,1024]{1,0:T(8,128)(2,1)S(1)}, u32[]{:S(2)}, u32[]{:S(2)}) collective-permute-start(bf16[256,1024]{1,0:T(8,128)(2,1)S(1)} %collective-permute-done.3.refs_2_.refs_1_), channel_id=1, source_target_pairs={{0,1},{1,0},{2,3},{3,2},{4,5},{5,4},{6,7},{7,6},{8,9},{9,8},{10,11... | collective-permute-start | bytes 1572872 | tf_op jit(solution)/shard_map/ppermute | solution.py:352
  25.9 8.9 %collective-permute-start.9 = (bf16[640,256]{1,0:T(8,128)(2,1)S(1)}, bf16[640,256]{1,0:T(8,128)(2,1)S(1)}, u32[]{:S(2)}, u32[]{:S(2)}) collective-permute-start(bf16[640,256]{1,0:T(8,128)(2,1)S(1)} %collective-permute-done.5.refs_6_.refs_5_), channel_id=1, source_target_pairs={{0,1},{1,0},{2,3},{3,2},{4,5},{5,4},{6,7},{7,6},{8,9},{9,8},{10,11... | collective-permute-start | bytes 983048 | tf_op jit(solution)/shard_map/ppermute | solution.py:352
  35.9 17.8 %collective-permute-start.14 = (bf16[64,1024]{1,0:T(8,128)(2,1)S(1)}, bf16[64,1024]{1,0:T(8,128)(2,1)S(1)}, u32[]{:S(2)}, u32[]{:S(2)}) collective-permute-start(bf16[64,1024]{1,0:T(8,128)(2,1)S(1)} %get-tuple-element.70), channel_id=1, source_target_pairs={{0,12},{1,13},{2,14},{3,15},{4,8},{5,9},{6,10},{7,11},{8,4},{9,5},... | collective-permute-start | bytes 393224 | tf_op jit(solution)/shard_map/ppermute | solution.py:355
  39.6 14.2 %collective-permute-start.13 = (bf16[64,1024]{1,0:T(8,128)(2,1)S(1)}, bf16[64,1024]{1,0:T(8,128)(2,1)S(1)}, u32[]{:S(2)}, u32[]{:S(2)}) collective-permute-start(bf16[64,1024]{1,0:T(8,128)(2,1)S(1)} %get-tuple-element.69), channel_id=1, source_target_pairs={{0,8},{1,9},{2,10},{3,11},{4,12},{5,13},{6,14},{7,15},{8,0},{9,1},... | collective-permute-start | bytes 393224 | tf_op jit(solution)/shard_map/ppermute | solution.py:355
  42.1 11.7 %collective-permute-start.12 = (bf16[64,1024]{1,0:T(8,128)(2,1)S(1)}, bf16[64,1024]{1,0:T(8,128)(2,1)S(1)}, u32[]{:S(2)}, u32[]{:S(2)}) collective-permute-start(bf16[64,1024]{1,0:T(8,128)(2,1)S(1)} %get-tuple-element.68), channel_id=1, source_target_pairs={{0,4},{1,5},{2,6},{3,7},{4,0},{5,1},{6,2},{7,3},{8,12},{9,13},{10,... | collective-permute-start | bytes 393224 | tf_op jit(solution)/shard_map/ppermute | solution.py:355
  42.3 9.0 %copy-start.1 = (bf16[256,1024]{1,0:T(8,128)(2,1)}, bf16[256,1024]{1,0:T(8,128)(2,1)S(1)}, u32[]{:S(2)}) copy-start(bf16[256,1024]{1,0:T(8,128)(2,1)S(1)} %collective-permute-done.4.refs_7_.refs_2_) | copy-start | bytes 1572868
  51.3 17.1 %collective-permute-start.10 = (bf16[1024,256]{1,0:T(8,128)(2,1)}, bf16[1024,256]{1,0:T(8,128)(2,1)S(1)}, u32[]{:S(2)}, u32[]{:S(2)}) collective-permute-start(bf16[1024,256]{1,0:T(8,128)(2,1)} %get-tuple-element.63), channel_id=1, source_target_pairs={{0,4},{1,5},{2,6},{3,7},{4,0},{5,1},{6,2},{7,3},{8,12},{9,13},{10,... | collective-permute-start | bytes 1572872 | tf_op jit(solution)/shard_map/ppermute | solution.py:355
  53.1 15.9 %collective-permute-start.11 = (bf16[1024,256]{1,0:T(8,128)(2,1)}, bf16[1024,256]{1,0:T(8,128)(2,1)S(1)}, u32[]{:S(2)}, u32[]{:S(2)}) collective-permute-start(bf16[1024,256]{1,0:T(8,128)(2,1)} %get-tuple-element.64), channel_id=1, source_target_pairs={{4,8},{5,9},{6,10},{7,11},{8,4},{9,5},{10,6},{11,7},{20,24},{21,25... | collective-permute-start | bytes 1572872 | tf_op jit(solution)/shard_map/ppermute | solution.py:362
  53.9 6.2 %collective-permute-start.15 = (bf16[64,1024]{1,0:T(8,128)(2,1)S(1)}, bf16[64,1024]{1,0:T(8,128)(2,1)S(1)}, u32[]{:S(2)}, u32[]{:S(2)}) collective-permute-start(bf16[64,1024]{1,0:T(8,128)(2,1)S(1)} %add_convert_fusion.1), channel_id=1, source_target_pairs={{0,2},{1,3},{2,18},{3,19},{4,6},{5,7},{6,22},{7,23},{8,10},{9,11},... | collective-permute-start | bytes 393224 | tf_op jit(solution)/shard_map/ppermute | solution.py:441
  55.4 4.6 %collective-permute-start.16 = (bf16[64,1024]{1,0:T(8,128)(2,1)S(1)}, bf16[64,1024]{1,0:T(8,128)(2,1)S(1)}, u32[]{:S(2)}, u32[]{:S(2)}) collective-permute-start(bf16[64,1024]{1,0:T(8,128)(2,1)S(1)} %add_convert_fusion.1), channel_id=1, source_target_pairs={{2,16},{3,17},{6,20},{7,21},{10,24},{11,25},{14,28},{15,29},{16,2}... | collective-permute-start | bytes 393224 | tf_op jit(solution)/shard_map/ppermute | solution.py:442
  60.1 8.4 %collective-permute-start.20 = (bf16[64,1024]{1,0:T(8,128)(2,1)S(1)}, bf16[64,1024]{1,0:T(8,128)(2,1)S(1)}, u32[]{:S(2)}, u32[]{:S(2)}) collective-permute-start(bf16[64,1024]{1,0:T(8,128)(2,1)S(1)} %add_convert_fusion.refs_5_.refs_0_), channel_id=1, source_target_pairs={{0,4},{1,5},{2,6},{3,7},{4,0},{5,1},{6,2},{7,3},{8,12},{9,13},{10,... | collective-permute-start | bytes 393224 | tf_op jit(solution)/shard_map/ppermute | solution.py:355
  63.1 13.5 %collective-permute-start.21 = (bf16[64,1024]{1,0:T(8,128)(2,1)S(1)}, bf16[64,1024]{1,0:T(8,128)(2,1)S(1)}, u32[]{:S(2)}, u32[]{:S(2)}) collective-permute-start(bf16[64,1024]{1,0:T(8,128)(2,1)S(1)} %add_convert_fusion.refs_5_.refs_0_), channel_id=1, source_target_pairs={{0,8},{1,9},{2,10},{3,11},{4,12},{5,13},{6,14},{7,15},{8,0},{9,1},... | collective-permute-start | bytes 393224 | tf_op jit(solution)/shard_map/ppermute | solution.py:355
  63.4 14.4 %collective-permute-start.22 = (bf16[64,1024]{1,0:T(8,128)(2,1)S(1)}, bf16[64,1024]{1,0:T(8,128)(2,1)S(1)}, u32[]{:S(2)}, u32[]{:S(2)}) collective-permute-start(bf16[64,1024]{1,0:T(8,128)(2,1)S(1)} %add_convert_fusion.refs_5_.refs_0_), channel_id=1, source_target_pairs={{0,12},{1,13},{2,14},{3,15},{4,8},{5,9},{6,10},{7,11},{8,4},{9,5},... | collective-permute-start | bytes 393224 | tf_op jit(solution)/shard_map/ppermute | solution.py:355
  68.5 9.4 %collective-permute-start.23 = (bf16[64,1024]{1,0:T(8,128)(2,1)S(1)}, bf16[64,1024]{1,0:T(8,128)(2,1)S(1)}, u32[]{:S(2)}, u32[]{:S(2)}) collective-permute-start(bf16[64,1024]{1,0:T(8,128)(2,1)S(1)} %add_convert_fusion.refs_5_.refs_0_), channel_id=1, source_target_pairs={{0,1},{1,0},{2,3},{3,2},{4,5},{5,4},{6,7},{7,6},{8,9},{9,8},{10,11... | collective-permute-start | bytes 393224 | tf_op jit(solution)/shard_map/ppermute | solution.py:352
  68.5 10.3 %collective-permute-start.24 = (bf16[64,1024]{1,0:T(8,128)(2,1)S(1)}, bf16[64,1024]{1,0:T(8,128)(2,1)S(1)}, u32[]{:S(2)}, u32[]{:S(2)}) collective-permute-start(bf16[64,1024]{1,0:T(8,128)(2,1)S(1)} %collective-permute-done.20.refs_1_), channel_id=1, source_target_pairs={{0,1},{1,0},{2,3},{3,2},{4,5},{5,4},{6,7},{7,6},{8,9},{9,8},{10,11... | collective-permute-start | bytes 393224 | tf_op jit(solution)/shard_map/ppermute | solution.py:352
  69.1 18.2 %copy-start = (bf16[512,1024]{1,0:T(8,128)(2,1)S(1)}, bf16[512,1024]{1,0:T(8,128)(2,1)}, u32[]{:S(2)}) copy-start(bf16[512,1024]{1,0:T(8,128)(2,1)} %refs_0_.3) | copy-start | bytes 3145732
  69.2 18.2 %copy-start.2 = (bf16[256,1024]{1,0:T(8,128)(2,1)S(1)}, bf16[256,1024]{1,0:T(8,128)(2,1)}, u32[]{:S(2)}) copy-start(bf16[256,1024]{1,0:T(8,128)(2,1)} %copy-done.1) | copy-start | bytes 1572868
  69.2 12.4 %collective-permute-start.17 = (bf16[512,256]{1,0:T(8,128)(2,1)S(1)}, bf16[512,256]{1,0:T(8,128)(2,1)S(1)}, u32[]{:S(2)}, u32[]{:S(2)}) collective-permute-start(bf16[512,256]{1,0:T(8,128)(2,1)S(1)} %get-tuple-element.72), channel_id=1, source_target_pairs={{0,1},{1,0},{2,3},{3,2},{4,5},{5,4},{6,7},{7,6},{8,9},{9,8},{10,11... | collective-permute-start | bytes 786440 | tf_op jit(solution)/shard_map/ppermute | solution.py:352
  76.6 8.5 %collective-permute-start.18 = (bf16[512,256]{1,0:T(8,128)(2,1)S(1)}, bf16[512,256]{1,0:T(8,128)(2,1)S(1)}, u32[]{:S(2)}, u32[]{:S(2)}) collective-permute-start(bf16[512,256]{1,0:T(8,128)(2,1)S(1)} %get-tuple-element.73), channel_id=1, source_target_pairs={{0,2},{1,3},{2,0},{3,1},{4,6},{5,7},{6,4},{7,5},{8,10},{9,11},{10,... | collective-permute-start | bytes 786440 | tf_op jit(solution)/shard_map/ppermute | solution.py:352
  77.9 9.5 %collective-permute-start.19 = (bf16[512,256]{1,0:T(8,128)(2,1)S(1)}, bf16[512,256]{1,0:T(8,128)(2,1)S(1)}, u32[]{:S(2)}, u32[]{:S(2)}) collective-permute-start(bf16[512,256]{1,0:T(8,128)(2,1)S(1)} %get-tuple-element.74), channel_id=1, source_target_pairs={{0,3},{1,2},{2,1},{3,0},{4,7},{5,6},{6,5},{7,4},{8,11},{9,10},{10,... | collective-permute-start | bytes 786440 | tf_op jit(solution)/shard_map/ppermute | solution.py:352
  77.9 1.8 %collective-permute-start.25 = (bf16[64,1024]{1,0:T(8,128)(2,1)S(1)}, bf16[64,1024]{1,0:T(8,128)(2,1)S(1)}, u32[]{:S(2)}, u32[]{:S(2)}) collective-permute-start(bf16[64,1024]{1,0:T(8,128)(2,1)S(1)} %collective-permute-done.21.refs_2_), channel_id=1, source_target_pairs={{0,1},{1,0},{2,3},{3,2},{4,5},{5,4},{6,7},{7,6},{8,9},{9,8},{10,11... | collective-permute-start | bytes 393224 | tf_op jit(solution)/shard_map/ppermute | solution.py:352
  78.7 1.3 %collective-permute-start.26 = (bf16[64,1024]{1,0:T(8,128)(2,1)S(1)}, bf16[64,1024]{1,0:T(8,128)(2,1)S(1)}, u32[]{:S(2)}, u32[]{:S(2)}) collective-permute-start(bf16[64,1024]{1,0:T(8,128)(2,1)S(1)} %collective-permute-done.22.refs_3_), channel_id=1, source_target_pairs={{0,1},{1,0},{2,3},{3,2},{4,5},{5,4},{6,7},{7,6},{8,9},{9,8},{10,11... | collective-permute-start | bytes 393224 | tf_op jit(solution)/shard_map/ppermute | solution.py:352

commit v3 on v2

--- a/solution.py
+++ b/solution.py
@@ -158,6 +158,15 @@
     return jnp.concatenate([both[:HEAD_DIM, :rows], both[HEAD_DIM:, rows:]], axis=0)
 
 
+def unit_slices(unit, pairs, rows, span):
+    block, pair = unit // pairs, unit % pairs
+    return (
+        slice(block * rows, (block + 1) * rows),
+        slice(block * rows, block * rows + span),
+        slice(pair * PAIR, (pair + 1) * PAIR),
+    )
+
+
 LOG2_SCALE = math.log2(math.e) * HEAD_DIM ** (-0.5)
 
 
@@ -189,23 +198,37 @@
             vals[at, :] = source[base + rows : base + 2 * rows, :]
     keys_t[...] = keys[...].T
     vals_t[...] = vals[...].T
-    for block in range(group):
-        bias = key_bias(limits, plane_start, block, rows, span)
-        at = slice(block * rows, (block + 1) * rows)
-        seen = slice(block * rows, block * rows + span)
-        for pair in range(cols // PAIR):
-            lanes = slice(pair * PAIR, (pair + 1) * PAIR)
-            score = dot_nt(keys[seen, lanes], stack_pair(queries[at, lanes])) + bias
-            peak = jnp.max(score, axis=0, keepdims=True)
-            power = jnp.exp2((score - peak) * LOG2_SCALE)
-            share = 1.0 / jnp.sum(power, axis=0, keepdims=True)
-            unit = block * (cols // PAIR) + pair
-            stats[unit, 0:1, :] = peak
-            stats[unit, 1:2, :] = share
-            prob = (power * share).astype(BF16)
-            mixed = unstack_pair(dot_nn(vals_t[lanes, seen], prob), rows).astype(BF16)
-            att_t[lanes, at] = mixed
-            att[at, lanes] = mixed.T
+    pairs = cols // PAIR
+    count = group * pairs
+
+    def scored(unit, bias):
+        at, seen, lanes = unit_slices(unit, pairs, rows, span)
+        return dot_nt(keys[seen, lanes], stack_pair(queries[at, lanes])) + bias
+
+    def mix(unit, prob):
+        at, seen, lanes = unit_slices(unit, pairs, rows, span)
+        mixed = unstack_pair(dot_nn(vals_t[lanes, seen], prob), rows).astype(BF16)
+        att_t[lanes, at] = mixed
+        att[at, lanes] = mixed.T
+
+    bias = key_bias(limits, plane_start, 0, rows, span)
+    ahead = scored(0, bias)
+    prob = None
+    for unit in range(count):
+        score = ahead
+        if unit + 1 < count:
+            if (unit + 1) % pairs == 0:
+                bias = key_bias(limits, plane_start, (unit + 1) // pairs, rows, span)
+            ahead = scored(unit + 1, bias)
+        if unit > 0:
+            mix(unit - 1, prob)
+        peak = jnp.max(score, axis=0, keepdims=True)
+        power = jnp.exp2((score - peak) * LOG2_SCALE)
+        share = 1.0 / jnp.sum(power, axis=0, keepdims=True)
+        stats[unit, 0:1, :] = peak
+        stats[unit, 1:2, :] = share
+        prob = (power * share).astype(BF16)
+    mix(count - 1, prob)
 
 
 def middle_kernel(group, fast, att_t, near, far, *refs):
@@ -250,35 +273,55 @@
 
 
 def backward_kernel(
-    group, limits, keys, vals, keys_t, queries, grad_att, stats,
-    to_first, own, to_second, grad_query, key_sum, value_sum,
+    group, limits, keys, vals, keys_t, queries, grad_att, stats, att,
+    to_first, own, to_second, *refs,
 ):
+    mine, near, far, key_sum, value_sum, grad_query = refs
     plane, cols = queries.shape
     rows = plane // group
     span = rows + 2 * WINDOW
     pairs = cols // PAIR
+    count = group * pairs
     place = lax.axis_index("seq")
-    plane_start = (place - lax.rem(place, group)) * rows
+    inner = lax.rem(place, group)
+    plane_start = (place - inner) * rows
     key_sum[...] = jnp.zeros_like(key_sum)
     value_sum[...] = jnp.zeros_like(value_sum)
-    for block in range(group):
-        bias = key_bias(limits, plane_start, block, rows, span)
-        at = slice(block * rows, (block + 1) * rows)
-        seen = slice(block * rows, block * rows + span)
-        for pair in range(pairs):
-            lanes = slice(pair * PAIR, (pair + 1) * PAIR)
-            unit = block * pairs + pair
-            query = stack_pair(queries[at, lanes])
-            grad = stack_pair(grad_att[at, lanes])
-            score = dot_nt(keys[seen, lanes], query) + bias
-            prob = jnp.exp2((score - stats[unit, 0:1, :]) * LOG2_SCALE) * stats[unit, 1:2, :]
-            grad_prob = dot_nt(vals[seen, lanes], grad)
-            centre = jnp.sum(prob * grad_prob, axis=0, keepdims=True)
-            grad_score = (prob * (grad_prob - centre) * HEAD_DIM ** (-0.5)).astype(BF16)
-            value_sum[seen, lanes] += dot_nn(prob.astype(BF16), grad)
-            key_sum[seen, lanes] += dot_nn(grad_score, query)
-            turned = unstack_pair(dot_nn(keys_t[lanes, seen], grad_score), rows)
-            grad_query[at, lanes] = turned.astype(BF16).T
+
+    def begin(unit, bias):
+        at, seen, lanes = unit_slices(unit, pairs, rows, span)
+        query = stack_pair(queries[at, lanes])
+        grad = stack_pair(grad_att[at, lanes])
+        score = dot_nt(keys[seen, lanes], query) + bias
+        return query, grad, score, dot_nt(vals[seen, lanes], grad)
+
+    def end(unit, query, grad, prob, grad_score):
+        at, seen, lanes = unit_slices(unit, pairs, rows, span)
+        value_sum[seen, lanes] += dot_nn(prob, grad)
+        key_sum[seen, lanes] += dot_nn(grad_score, query)
+        turned = unstack_pair(dot_nn(keys_t[lanes, seen], grad_score), rows)
+        grad_query[at, lanes] = turned.astype(BF16).T
+
+    bias = key_bias(limits, plane_start, 0, rows, span)
+    ahead = begin(0, bias)
+    behind = None
+    for unit in range(count):
+        query, grad, score, grad_prob = ahead
+        if unit + 1 < count:
+            if (unit + 1) % pairs == 0:
+                bias = key_bias(limits, plane_start, (unit + 1) // pairs, rows, span)
+            ahead = begin(unit + 1, bias)
+        if unit > 0:
+            end(unit - 1, *behind)
+        prob = jnp.exp2((score - stats[unit, 0:1, :]) * LOG2_SCALE) * stats[unit, 1:2, :]
+        centre = jnp.sum(prob * grad_prob, axis=0, keepdims=True)
+        grad_score = (prob * (grad_prob - centre) * HEAD_DIM ** (-0.5)).astype(BF16)
+        behind = (query, grad, prob.astype(BF16), grad_score)
+    end(count - 1, *behind)
+    for m, (target, base) in enumerate(((mine, 0), (near, 0), (far, 0), (far, 2 * rows))):
+        taken = pl.ds(pl.multiple_of((inner ^ m) * rows, 128), rows)
+        target[base : base + rows, :] = grad_query[taken, :]
+        target[base + rows : base + 2 * rows, :] = att[taken, :]
     even = 1 - lax.rem(place // group, 2)
     for target, side in ((to_first, 2 * even), (own, 1), (to_second, 2 - 2 * even)):
         kept = pl.ds(pl.multiple_of(side * plane, 128), plane)
@@ -286,33 +329,36 @@
         target[plane : 2 * plane, :] = value_sum[kept, :].astype(target.dtype)
 
 
-def settle_kernel(group, own, from_first, from_second, grad_query, att, *pieces):
-    plane = grad_query.shape[0]
-    rows = plane // group
+def settle_kernel(group, own, from_first, from_second, near, far, *pieces):
+    rows = pieces[0].shape[0] // 2
+    plane = group * rows
     inner = lax.rem(lax.axis_index("seq"), group)
     for m in range(group):
         spot = (inner ^ m) * rows
-        mine = pl.ds(pl.multiple_of(spot, 128), rows)
-        pieces[m][0:rows, :] = grad_query[mine, :]
         for part in range(2):
             at = pl.ds(pl.multiple_of(part * plane + spot, 128), rows)
             summed = own[at, :] + from_first[at, :].astype(F32) + from_second[at, :].astype(F32)
-            pieces[m][(part + 1) * rows : (part + 2) * rows, :] = summed.astype(BF16)
-        pieces[m][3 * rows : 4 * rows, :] = att[mine, :]
+            pieces[m][part * rows : (part + 1) * rows, :] = summed.astype(BF16)
+    pieces[1][2 * rows : 4 * rows, :] = near[...]
+    pieces[1][4 * rows : 6 * rows, :] = far[2 * rows : 4 * rows, :]
 
 
 def unpack_kernel(group, fast, near, far, farther, *refs):
-    pieces, outs, out, att = refs[:group], refs[group : group + 3], refs[group + 3], refs[group + 4]
+    sums, mine, early = refs[:group], refs[group], refs[group + 1]
+    outs, out, att = refs[group + 2 : group + 5], refs[group + 5], refs[group + 6]
     rows, width = out.shape
     cols = width // group
     half = width // 2
     inner = lax.rem(lax.axis_index("seq"), group)
     first = lax.axis_index("doc") if fast else 0
+    held = ((mine, 0), (sums[1], 2 * rows), (early, 0), (sums[1], 4 * rows))
     for m in range(group):
         at = pl.ds(pl.multiple_of((inner ^ m) * cols, 128), cols)
-        for part in range(3):
-            outs[part][:, at] = pieces[m][part * rows : (part + 1) * rows, :]
-        att[:, at] = pieces[m][3 * rows : 4 * rows, :]
+        outs[1][:, at] = sums[m][0:rows, :]
+        outs[2][:, at] = sums[m][rows : 2 * rows, :]
+        source, base = held[m]
+        outs[0][:, at] = source[base : base + rows, :]
+        att[:, at] = source[base + rows : base + 2 * rows, :]
     total = dot_nn(att[:, pl.ds(pl.multiple_of(first * half, 128), half)], near[...])
     for side, weight in ((0, far), (1, farther)):
         start = (1 - first) * half + (lax.rem(inner, 2) ^ side) * cols
@@ -320,17 +366,44 @@
     out[...] = total.astype(BF16)
 
 
-def finish_kernel(group, count, scale, *refs):
+def add_kernel(*refs):
+    total = refs[0][...].astype(F32)
+    for ref in refs[1:-1]:
+        total += ref[...].astype(F32)
+    refs[-1][...] = total.astype(BF16)
+
+
+def pass_kernel(source, target):
+    target[...] = source[...]
+
+
+def cross_kernel(group, own, first, second, out):
+    inner = lax.rem(lax.axis_index("seq"), group)
+    owner = inner // 2 == lax.axis_index("doc")
+
+    @pl.when(owner)
+    def _():
+        out[...] = (first[...].astype(F32) + own[...].astype(F32)).astype(BF16)
+
+    @pl.when(jnp.logical_not(owner))
+    def _():
+        out[...] = (first[...].astype(F32) + second[...].astype(F32)).astype(BF16)
+
+
+def gather_kernel(group, *refs):
     out = refs[-1]
-    near, far = refs[:count], refs[count : 2 * count]
-    place = lax.axis_index("seq")
-    side = lax.rem(place, 2)
-    outer = place // group
-    part = near[0].shape[0]
+    outer = lax.axis_index("seq") // group
+    part = refs[0].shape[0]
+    for m, source in enumerate(refs[:-1]):
+        out[pl.ds(pl.multiple_of((outer ^ m) * part, 16), part), :] = source[...]
+
+
+def finish_kernel(scale, near, far, out):
+    side = lax.rem(lax.axis_index("seq"), 2)
+    size = near.shape[0]
     for source, base in ((near, side), (far, 1 - side)):
-        for m in range(count):
-            start = (base * count + (outer ^ m)) * part
-            out[pl.ds(pl.multiple_of(start, 8), part), :] = source[m][...].astype(F32) * scale
+        at = pl.ds(pl.multiple_of(base * size, 128), size)
+        out[at, :] = source[...].astype(F32) * scale
 
 
 def body(queries, key_rows, value_rows, cotangent, out_weight, lengths, upweight):
@@ -379,10 +452,10 @@
     far_kv = [inner_swap(packed[m - 2], m) for m in range(2, group)]
     own_rest, near_all, rest_first, rest_last, limits, *weight = packed[group - 2 :]
     near_all = inner_swap(near_all, 1)
-    joined, rest_first, rest_last, *weight = call(
+    joined, rest_first, rest_last = call(
         functools.partial(join_kernel, group),
-        [((2 * group * rows, cols), BF16), *rest, *chunk],
-        (own_kv, near_all, *far_kv, rest_first, rest_last, *weight),
+        [((2 * group * rows, cols), BF16), *rest],
+        (own_kv, near_all, *far_kv, rest_first, rest_last),
         flops=1 << 20, moved=1 << 20,
     )
     sides = [outer_first(joined), outer_second(joined)]
@@ -425,9 +498,26 @@
         flops=1 << 30, moved=4 << 20,
     )
 
+    to_first, own, to_second, early_own, early_near, early_far = call(
+        functools.partial(backward_kernel, group),
+        [((2 * plane, cols), BF16), ((2 * plane, cols), F32), ((2 * plane, cols), BF16)]
+        + [((2 * rows, cols), BF16)] * 2
+        + [((4 * rows, cols), BF16)],
+        (limits, keys, vals, keys_t, query_all, grad_att, stats, att),
+        after=half_far[1:],
+        scratch=[pltpu.VMEM((3 * plane, cols), F32)] * 2 + [pltpu.VMEM((plane, cols), BF16)],
+        flops=8 << 30, moved=4 << 20, vmem=32,
+    )
     if fast:
         swapped = [weight_parts[0]] + [outer_swap(weight_parts[m], m) for m in range(1, outer_count)]
-        line = sum(part.astype(F32) for part in swapped).astype(BF16)
+        part_shape = [(swapped[0].shape, BF16)]
+        (line,) = call(
+            add_kernel, part_shape, swapped, after=(early_near,), flops=1 << 18, moved=1 << 19
+        )
+        (early_far,) = call(
+            pass_kernel, [(early_far.shape, BF16)], (early_far,), after=(line,),
+            flops=1 << 18, moved=1 << 19,
+        )
         flat = [(d, i) for d in range(doc_count) for i in range(seq_count)]
         first_pairs, second_pairs = [], []
         for d, i in flat:
@@ -440,18 +530,13 @@
                 second_pairs.append((source, owner * seq_count + (i ^ 2)))
         got_first = lax.ppermute(line, ("doc", "seq"), first_pairs)
         got_second = lax.ppermute(line, ("doc", "seq"), second_pairs)
-        is_owner = inner // 2 == lax.axis_index("doc")
-        final = (
-            got_first.astype(F32) + jnp.where(is_owner, line, got_second).astype(F32)
-        ).astype(BF16)
-        before_settle = (final,)
-        near_parts = [final] + [outer_swap(final, m) for m in range(1, outer_count)]
-        far_parts = [inner_swap(part, 1) for part in near_parts]
-        (grad_weight,) = call(
-            functools.partial(finish_kernel, group, outer_count, scale),
-            [((width // doc_count, width), F32)],
-            (*near_parts, *far_parts), flops=1 << 20, moved=4 << 20,
+        early = inner_swap(early_far, 2)
+        (final,) = call(
+            functools.partial(cross_kernel, group), part_shape, (line, got_first, got_second), after=(early,),
+            flops=2 << 30, moved=1 << 19,
         )
+        gathered = [final] + [outer_swap(final, m) for m in range(1, outer_count)]
+        before_settle = gathered[:1]
     else:
         placed = lax.dynamic_update_slice_in_dim(
             jnp.zeros((width, width), F32), weight_parts[0], inner * cols, 0
@@ -459,27 +544,28 @@
         block = lax.psum_scatter(placed, "doc", scatter_dimension=0, tiled=True)
         grad_weight = lax.psum(block, "seq") * scale
         before_settle = ()
-
-    to_first, own, to_second, grad_query = call(
-        functools.partial(backward_kernel, group),
-        [((2 * plane, cols), BF16), ((2 * plane, cols), F32), ((2 * plane, cols), BF16)]
-        + [((plane, cols), BF16)],
-        (limits, keys, vals, keys_t, query_all, grad_att, stats),
-        after=half_far[1:],
-        scratch=[pltpu.VMEM((3 * plane, cols), F32)] * 2,
-        flops=8 << 30, moved=4 << 20, vmem=32,
-    )
-    pieces = call(
+        early = inner_swap(early_far, 2)
+
+    sums = call(
         functools.partial(settle_kernel, group),
-        [((4 * rows, cols), BF16)] * group,
-        (own, outer_first(to_first), outer_second(to_second), grad_query, att),
-        after=before_settle, flops=1 << 20, moved=2 << 20,
-    )
-    pieces = [pieces[0]] + [inner_swap(pieces[m], m) for m in range(1, group)]
+        [(((6 if m == 1 else 2) * rows, cols), BF16) for m in range(group)],
+        (own, outer_first(to_first), outer_second(to_second), early_near, early),
+        after=before_settle, flops=10 << 30, moved=2 << 20,
+    )
+    sums = [sums[0]] + [inner_swap(sums[m], m) for m in range(1, group)]
+    if fast:
+        (gathered,) = call(
+            functools.partial(gather_kernel, group), [((cols, width), BF16)], gathered,
+            after=sums[2:], flops=1 << 18, moved=1 << 20,
+        )
+        (grad_weight,) = call(
+            functools.partial(finish_kernel, scale), [((width // doc_count, width), F32)],
+            (gathered, inner_swap(gathered, 1)), flops=1 << 20, moved=4 << 20,
+        )
     grad_query, grad_key, grad_value, layer_out = call(
         functools.partial(unpack_kernel, group, fast),
         [((rows, width), BF16)] * 4,
-        (half_near, *half_far, *pieces),
+        (half_near, *half_far, *sums, early_own, early),
         scratch=[pltpu.VMEM((rows, width), BF16)],
         flops=1 << 30, moved=4 << 20,
     )

time: 89.4 us -> 80 us (0.89)
  waiting for transfers between devices: 37.3 us -> 31.8 us
  Pallas kernels: 22 us -> 17.3 us
  starting transfers between devices: 28.4 us -> 30 us
    ppermute x1, waiting for transfers between devices: 8.55 us -> 3.41 us  [body(): far = lax.ppermute(near, 'doc', [(0, 1), (1, 0)])]
    pallas_call x8 -> x12, Pallas kernels: 22 us -> 17.3 us  [call(): pl.pallas_call(run, out_shape=outs, in_specs=[HBM] * hbm + [VMEM] * (coun...]
    ppermute x1, waiting for transfers between devices: 3.89 us -> 7.8 us  [body(): got_first = lax.ppermute(line, ('doc', 'seq'), first_pairs)]
    ppermute x8, waiting for transfers between devices: 11.2 us -> 7.51 us  [outer_swap(): lax.ppermute(value, 'seq', [(i, i ^ m * group) for i in range(seq_count)])]
    ppermute x14 -> x12, starting transfers between devices: 8.08 us -> 9.59 us  [inner_swap(): return lax.ppermute(value, 'seq', [(i, i ^ m) for i in range(seq_count)])]
    ppermute x1, starting transfers between devices: 1.58 us -> 0.51 us  [body(): got_first = lax.ppermute(line, ('doc', 'seq'), first_pairs)]
    ppermute x8, starting transfers between devices: 15.1 us -> 16.2 us  [outer_swap(): lax.ppermute(value, 'seq', [(i, i ^ m * group) for i in range(seq_count)])]
    ppermute x14 -> x12, waiting for transfers between devices: 13.7 us -> 13 us  [inner_swap(): return lax.ppermute(value, 'seq', [(i, i ^ m) for i in range(seq_count)])]
  transfers between devices with their start and end apart: 27 -> 25, of which waited for: 11 -> 11; matrix products, arithmetic and copies ran while one was open for 0% -> 0% of each run, Pallas kernels for 22% -> 18%
where the time goes in v3:
time: 80 us; the launch traced here: 79.8 us
  waiting for transfers between devices  31.8 us (40%)
  starting transfers between devices  30 us (38%)
  Pallas kernels  17.3 us (22%)
    pallas_call x12, Pallas kernels, call(): pl.pallas_call(run, out_shape=outs, in_specs=[HBM] * hbm + [VMEM] * (coun...  17.3 us
    ppermute x8, starting transfers between devices, outer_swap(): lax.ppermute(value, 'seq', [(i, i ^ m * group) for i in range(seq_count)])  16.2 us
    ppermute x12, waiting for transfers between devices, inner_swap(): return lax.ppermute(value, 'seq', [(i, i ^ m) for i in range(seq_count)])  13 us
    ppermute x12, starting transfers between devices, inner_swap(): return lax.ppermute(value, 'seq', [(i, i ^ m) for i in range(seq_count)])  9.59 us
    ppermute x1, waiting for transfers between devices, body(): got_first = lax.ppermute(line, ('doc', 'seq'), first_pairs)  7.8 us
    ppermute x8, waiting for transfers between devices, outer_swap(): lax.ppermute(value, 'seq', [(i, i ^ m * group) for i in range(seq_count)])  7.51 us
    ppermute x1, waiting for transfers between devices, body(): far = lax.ppermute(near, 'doc', [(0, 1), (1, 0)])  3.41 us
    ppermute x1, starting transfers between devices, body(): far = lax.ppermute(near, 'doc', [(0, 1), (1, 0)])  1.7 us
  transfers between devices with their start and end apart: 25, of which 11 were waited for; matrix products, arithmetic and copies ran while one was open for 0% of the time, Pallas kernels for 18%

profile of v3, /device:TPU:0, one launch (start us, length us, event | category | flops | bytes accessed | tf_op | source)
XLA Modules:
  0.0 79.8 jit_solution(12022053971513006478)
XLA Ops:
  0.6 1.4 %shard_map.110 = (bf16[256,256]{1,0:T(8,128)(2,1)S(1)}, bf16[256,256]{1,0:T(8,128)(2,1)S(1)}, bf16[256,256]{1,0:T(8,128)(2,1)S(1)}, bf16[640,256]{1,0:T(8,128)(2...) custom-call(s32[1,4]{1,0:T(1,128)} %refs_0_.2, ...), custom_call_target="tpu_custom_call" | custom-call | flops 1048576 | bytes 4194304 | tf_op jit(solution)/shard_map/pallas_call | solution.py:38
  2.1 0.5 collective-permute-start.2
  2.6 2.6 %collective-permute-start.3 = (bf16[256,256]{1,0:T(8,128)(2,1)S(1)}, bf16[256,256]{1,0:T(8,128)(2,1)S(1)}, u32[]{:S(2)}, u32[]{:S(2)}) collective-permute-start(bf16[256,256]{1,0:T(8,128)(2,1)S(1)} %get-tuple-element.47), channel_id=1, source_target_pairs={{0,2},{1,3},{2,0},{3,1},{4,6},{5,7},{6,4},{7,5},{8,10},{9,11},{10,... | collective-permute-start | bytes 393224 | tf_op jit(solution)/shard_map/ppermute | solution.py:425
  5.2 0.1 collective-permute-start.4
  5.3 1.7 %collective-permute-start = (bf16[256,1024]{1,0:T(8,128)(2,1)S(1)}, bf16[256,1024]{1,0:T(8,128)(2,1)S(1)}, u32[]{:S(2)}, u32[]{:S(2)}) collective-permute-start(bf16[256,1024]{1,0:T(8,128)(2,1)S(1)} %get-tuple-element.43.refs_1_), channel_id=1, source_target_pairs={{0,16},{16,0},{1,17},{17,1},{2,18},{18,2},{3,19},{19,3},{4,20},{20... | collective-permute-start | bytes 1572872 | tf_op jit(solution)/shard_map/ppermute | solution.py:467
  7.0 2.6 %collective-permute-done.3.refs_2_.refs_3_ = bf16[256,256]{1,0:T(8,128)(2,1)S(1)} collective-permute-done((bf16[256,256]{1,0:T(8,128)(2,1)S(1)}, bf16[256,256]{1,0:T(8,128)(2,1)S(1)}, u32[]{:S(2)}, u32[]{:S(2)}) %collective-permute-start.3) | collective-permute-done | bytes 131104 | tf_op jit(solution)/shard_map/ppermute | solution.py:425
  9.5 2.3 %collective-permute-done.4.refs_3_.refs_4_ = bf16[256,256]{1,0:T(8,128)(2,1)S(1)} collective-permute-done((bf16[256,256]{1,0:T(8,128)(2,1)S(1)}, bf16[256,256]{1,0:T(8,128)(2,1)S(1)}, u32[]{:S(2)}, u32[]{:S(2)}) %collective-permute-start.4) | collective-permute-done | bytes 131104 | tf_op jit(solution)/shard_map/ppermute | solution.py:425
  11.8 0.0 collective-permute-done.2.refs_1_.refs_2_.refs_4_
  11.8 0.1 shard_map.111
  11.9 1.7 %collective-permute-start.7 = (bf16[1024,256]{1,0:T(8,128)(2,1)S(1)}, bf16[1024,256]{1,0:T(8,128)(2,1)S(1)}, u32[]{:S(2)}, u32[]{:S(2)}) collective-permute-start(bf16[1024,256]{1,0:T(8,128)(2,1)S(1)} %get-tuple-element.54), channel_id=1, source_target_pairs={{0,4},{1,5},{2,6},{3,7},{4,0},{5,1},{6,2},{7,3},{8,12},{9,13},{10,... | collective-permute-start | bytes 1572872 | tf_op jit(solution)/shard_map/ppermute | solution.py:428
  13.6 0.7 collective-permute-start.8
  14.3 1.6 %collective-permute-start.5 = (bf16[640,256]{1,0:T(8,128)(2,1)S(1)}, bf16[640,256]{1,0:T(8,128)(2,1)S(1)}, u32[]{:S(2)}, u32[]{:S(2)}) collective-permute-start(bf16[640,256]{1,0:T(8,128)(2,1)S(1)} %get-tuple-element.52), channel_id=1, source_target_pairs={{0,2},{1,3},{2,0},{3,1},{4,6},{5,7},{6,4},{7,5},{8,10},{9,11},{10,... | collective-permute-start | bytes 983048 | tf_op jit(solution)/shard_map/ppermute | solution.py:425
  15.8 0.1 collective-permute-start.6
  16.0 3.4 %collective-permute-done.refs_2_.refs_1_ = bf16[256,1024]{1,0:T(8,128)(2,1)S(1)} collective-permute-done((bf16[256,1024]{1,0:T(8,128)(2,1)S(1)}, bf16[256,1024]{1,0:T(8,128)(2,1)S(1)}, u32[]{:S(2)}, u32[]{:S(2)}) %collective-permute-start) | collective-permute-done | bytes 524320 | tf_op jit(solution)/shard_map/ppermute | solution.py:467
  19.4 5.5 %collective-permute-done.5.refs_6_.refs_5_ = bf16[640,256]{1,0:T(8,128)(2,1)S(1)} collective-permute-done((bf16[640,256]{1,0:T(8,128)(2,1)S(1)}, bf16[640,256]{1,0:T(8,128)(2,1)S(1)}, u32[]{:S(2)}, u32[]{:S(2)}) %collective-permute-start.5) | collective-permute-done | bytes 327712 | tf_op jit(solution)/shard_map/ppermute | solution.py:425
  24.9 0.1 collective-permute-done.6.refs_7_
  25.0 1.2 %collective-permute-done.7.refs_8_ = bf16[1024,256]{1,0:T(8,128)(2,1)S(1)} collective-permute-done((bf16[1024,256]{1,0:T(8,128)(2,1)S(1)}, bf16[1024,256]{1,0:T(8,128)(2,1)S(1)}, u32[]{:S(2)}, u32[]{:S(2)}) %collective-permute-start.7) | collective-permute-done | bytes 524320 | tf_op jit(solution)/shard_map/ppermute | solution.py:428
  26.2 0.0 collective-permute-done.8.refs_9_
  26.2 4.3 %shard_map.112 = (bf16[1536,256]{1,0:T(8,128)(2,1)S(1)}, bf16[1536,256]{1,0:T(8,128)(2,1)S(1)}, bf16[256,1536]{1,0:T(8,128)(2,1)S(1)}, bf16[512,256]{1,0:T(8,128...) custom-call(s32[8,512]{1,0:T(8,128)S(1)} %get-tuple-element.44.refs_0_, ...), custom_call_target="tpu_custom_call" | custom-call | flops 4294967296 | bytes 4194304 | tf_op jit(solution)/shard_map/pallas_call | solution.py:38
  30.6 1.1 %shard_map.113 = (bf16[512,256]{1,0:T(8,128)(2,1)S(1)}, bf16[64,1024]{1,0:T(8,128)(2,1)S(1)}, bf16[64,1024]{1,0:T(8,128)(2,1)S(1)}, bf16[64,1024]{1,0:T(8,128)(2,1)S(1)}, bf16[64,1024]{1,0:T(8,128)(2,1)S(1)}) custom-call(bf16[256,512]{1,0:T(8,128)(2,1)S(1)} %get-tuple-element.59.refs_0_, bf16[256,1024]{1,0:T(8,128)(2,1)S(1)} %get-tuple-element.43.refs_1_, ...), custom_call_target="tpu_custom_call" | custom-call | flops 1073741824 | bytes 4194304 | tf_op jit(solution)/shard_map/pallas_call | solution.py:38
  31.6 4.8 %collective-permute-start.12 = (bf16[64,1024]{1,0:T(8,128)(2,1)S(1)}, bf16[64,1024]{1,0:T(8,128)(2,1)S(1)}, u32[]{:S(2)}, u32[]{:S(2)}) collective-permute-start(bf16[64,1024]{1,0:T(8,128)(2,1)S(1)} %get-tuple-element.69), channel_id=1, source_target_pairs={{0,4},{1,5},{2,6},{3,7},{4,0},{5,1},{6,2},{7,3},{8,12},{9,13},{10,... | collective-permute-start | bytes 393224 | tf_op jit(solution)/shard_map/ppermute | solution.py:428
  36.5 1.2 %collective-permute-start.13 = (bf16[64,1024]{1,0:T(8,128)(2,1)S(1)}, bf16[64,1024]{1,0:T(8,128)(2,1)S(1)}, u32[]{:S(2)}, u32[]{:S(2)}) collective-permute-start(bf16[64,1024]{1,0:T(8,128)(2,1)S(1)} %get-tuple-element.70), channel_id=1, source_target_pairs={{0,8},{1,9},{2,10},{3,11},{4,12},{5,13},{6,14},{7,15},{8,0},{9,1},... | collective-permute-start | bytes 393224 | tf_op jit(solution)/shard_map/ppermute | solution.py:428
  37.7 1.4 %collective-permute-start.14 = (bf16[64,1024]{1,0:T(8,128)(2,1)S(1)}, bf16[64,1024]{1,0:T(8,128)(2,1)S(1)}, u32[]{:S(2)}, u32[]{:S(2)}) collective-permute-start(bf16[64,1024]{1,0:T(8,128)(2,1)S(1)} %get-tuple-element.71), channel_id=1, source_target_pairs={{0,12},{1,13},{2,14},{3,15},{4,8},{5,9},{6,10},{7,11},{8,4},{9,5},... | collective-permute-start | bytes 393224 | tf_op jit(solution)/shard_map/ppermute | solution.py:428
  39.1 7.3 %shard_map.114 = (bf16[1024,256]{1,0:T(8,128)(2,1)S(1)}, f32[1024,256]{1,0:T(8,128)S(1)}, bf16[1024,256]{1,0:T(8,128)(2,1)S(1)}, bf16[256,256]{1,0:T(8,128)(2,1)...) custom-call(s32[8,512]{1,0:T(8,128)S(1)} %get-tuple-element.44.refs_0_, ...), custom_call_target="tpu_custom_call" | custom-call | flops 8589934592 | bytes 4194304 | tf_op jit(solution)/shard_map/pallas_call | solution.py:38
  46.4 0.9 %collective-permute-start.10 = (bf16[1024,256]{1,0:T(8,128)(2,1)S(1)}, bf16[1024,256]{1,0:T(8,128)(2,1)S(1)}, u32[]{:S(2)}, u32[]{:S(2)}) collective-permute-start(bf16[1024,256]{1,0:T(8,128)(2,1)S(1)} %get-tuple-element.64), channel_id=1, source_target_pairs={{0,4},{1,5},{2,6},{3,7},{4,0},{5,1},{6,2},{7,3},{8,12},{9,13},{10,... | collective-permute-start | bytes 1572872 | tf_op jit(solution)/shard_map/ppermute | solution.py:428
  47.4 0.7 collective-permute-start.11
  48.1 1.1 %collective-permute-done.13.refs_2_ = bf16[64,1024]{1,0:T(8,128)(2,1)S(1)} collective-permute-done((bf16[64,1024]{1,0:T(8,128)(2,1)S(1)}, bf16[64,1024]{1,0:T(8,128)(2,1)S(1)}, u32[]{:S(2)}, u32[]{:S(2)}) %collective-permute-start.13) | collective-permute-done | bytes 131104 | tf_op jit(solution)/shard_map/ppermute | solution.py:428
  49.2 0.1 shard_map.115.refs_1_.refs_0_
  49.3 1.6 %collective-permute-start.15 = (bf16[512,256]{1,0:T(8,128)(2,1)S(1)}, bf16[512,256]{1,0:T(8,128)(2,1)S(1)}, u32[]{:S(2)}, u32[]{:S(2)}) collective-permute-start(bf16[512,256]{1,0:T(8,128)(2,1)S(1)} %shard_map.116), channel_id=1, source_target_pairs={{0,2},{1,3},{2,0},{3,1},{4,6},{5,7},{6,4},{7,5},{8,10},{9,11},{10,... | collective-permute-start | bytes 786440 | tf_op jit(solution)/shard_map/ppermute | solution.py:425
  50.8 0.5 collective-permute-start.16
  51.4 0.7 collective-permute-start.17
  52.0 7.8 %collective-permute-done.16.refs_1_ = bf16[64,1024]{1,0:T(8,128)(2,1)S(1)} collective-permute-done((bf16[64,1024]{1,0:T(8,128)(2,1)S(1)}, bf16[64,1024]{1,0:T(8,128)(2,1)S(1)}, u32[]{:S(2)}, u32[]{:S(2)}) %collective-permute-start.16) | collective-permute-done | bytes 131104 | tf_op jit(solution)/shard_map/ppermute | solution.py:531
  59.8 0.0 collective-permute-done.17.refs_2_
  59.8 0.0 collective-permute-done.15.refs_3_.refs_4_.refs_8_
  59.9 3.6 %collective-permute-start.21 = (bf16[64,1024]{1,0:T(8,128)(2,1)S(1)}, bf16[64,1024]{1,0:T(8,128)(2,1)S(1)}, u32[]{:S(2)}, u32[]{:S(2)}) collective-permute-start(bf16[64,1024]{1,0:T(8,128)(2,1)S(1)} %shard_map.117.refs_5_.refs_0_), channel_id=1, source_target_pairs={{0,4},{1,5},{2,6},{3,7},{4,0},{5,1},{6,2},{7,3},{8,12},{9,13},{10,... | collective-permute-start | bytes 393224 | tf_op jit(solution)/shard_map/ppermute | solution.py:428
  63.5 0.7 collective-permute-start.22
  64.3 1.7 %collective-permute-start.23 = (bf16[64,1024]{1,0:T(8,128)(2,1)S(1)}, bf16[64,1024]{1,0:T(8,128)(2,1)S(1)}, u32[]{:S(2)}, u32[]{:S(2)}) collective-permute-start(bf16[64,1024]{1,0:T(8,128)(2,1)S(1)} %shard_map.117.refs_5_.refs_0_), channel_id=1, source_target_pairs={{0,12},{1,13},{2,14},{3,15},{4,8},{5,9},{6,10},{7,11},{8,4},{9,5},... | collective-permute-start | bytes 393224 | tf_op jit(solution)/shard_map/ppermute | solution.py:428
  66.0 0.0 collective-permute-done.10.refs_1_
  66.0 0.0 collective-permute-done.11.refs_2_
  66.0 0.2 shard_map.118
  66.2 2.5 %collective-permute-start.19 = (bf16[256,256]{1,0:T(8,128)(2,1)S(1)}, bf16[256,256]{1,0:T(8,128)(2,1)S(1)}, u32[]{:S(2)}, u32[]{:S(2)}) collective-permute-start(bf16[256,256]{1,0:T(8,128)(2,1)S(1)} %get-tuple-element.74), channel_id=1, source_target_pairs={{0,2},{1,3},{2,0},{3,1},{4,6},{5,7},{6,4},{7,5},{8,10},{9,11},{10,... | collective-permute-start | bytes 393224 | tf_op jit(solution)/shard_map/ppermute | solution.py:425
  68.7 5.2 %collective-permute-done.22.refs_2_ = bf16[64,1024]{1,0:T(8,128)(2,1)S(1)} collective-permute-done((bf16[64,1024]{1,0:T(8,128)(2,1)S(1)}, bf16[64,1024]{1,0:T(8,128)(2,1)S(1)}, u32[]{:S(2)}, u32[]{:S(2)}) %collective-permute-start.22) | collective-permute-done | bytes 131104 | tf_op jit(solution)/shard_map/ppermute | solution.py:428
  73.9 0.6 collective-permute-done.20.refs_6_.refs_5_
  74.5 0.1 collective-permute-start.24
  74.6 0.5 collective-permute-start.18
  75.1 2.0 %collective-permute-done.18.refs_4_ = bf16[768,256]{1,0:T(8,128)(2,1)S(1)} collective-permute-done((bf16[768,256]{1,0:T(8,128)(2,1)S(1)}, bf16[768,256]{1,0:T(8,128)(2,1)S(1)}, u32[]{:S(2)}, u32[]{:S(2)}) %collective-permute-start.18) | collective-permute-done | bytes 393248 | tf_op jit(solution)/shard_map/ppermute | solution.py:425
  77.1 1.3 %shard_map.119 = (bf16[128,1024]{1,0:T(8,128)(2,1)}, bf16[128,1024]{1,0:T(8,128)(2,1)}, bf16[128,1024]{1,0:T(8,128)(2,1)}, bf16[128,1024]{1,0:T(8,128)(2,1)}) custom-call(bf16[512,1024]{1,0:T(8,128)(2,1)S(1)} %copy-done, bf16[256,1024]{1,0:T(8,128)(2,1)S(1)} %collective-permute-done.refs_2_.refs_1_, ...), custom_call_target="tpu_custom_call" | custom-call | flops 1073741824 | bytes 4194304 | tf_op jit(solution)/shard_map/pallas_call | solution.py:38
  78.3 1.5 %shard_map.121 = f32[512,1024]{1,0:T(8,128)} custom-call(bf16[256,1024]{1,0:T(8,128)(2,1)S(1)} %shard_map.120.refs_0_, bf16[256,1024]{1,0:T(8,128)(2,1)S(1)} %collective-permute-done.24.refs_1_), custom_call_target="tpu_custom_call" | custom-call | flops 1048576 | bytes 4194304 | tf_op jit(solution)/shard_map/pallas_call | solution.py:38
  (16 shorter events, 0.1 us)
Async XLA Ops:
  2.1 9.8 %collective-permute-start.2 = (bf16[896,256]{1,0:T(8,128)(2,1)S(1)}, bf16[896,256]{1,0:T(8,128)(2,1)S(1)}, u32[]{:S(2)}, u32[]{:S(2)}) collective-permute-start(bf16[896,256]{1,0:T(8,128)(2,1)S(1)} %get-tuple-element.46), channel_id=1, source_target_pairs={{0,1},{1,0},{2,3},{3,2},{4,5},{5,4},{6,7},{7,6},{8,9},{9,8},{10,11... | collective-permute-start | bytes 1376264 | tf_op jit(solution)/shard_map/ppermute | solution.py:425
  2.6 6.9 %collective-permute-start.3 = (bf16[256,256]{1,0:T(8,128)(2,1)S(1)}, bf16[256,256]{1,0:T(8,128)(2,1)S(1)}, u32[]{:S(2)}, u32[]{:S(2)}) collective-permute-start(bf16[256,256]{1,0:T(8,128)(2,1)S(1)} %get-tuple-element.47), channel_id=1, source_target_pairs={{0,2},{1,3},{2,0},{3,1},{4,6},{5,7},{6,4},{7,5},{8,10},{9,11},{10,... | collective-permute-start | bytes 393224 | tf_op jit(solution)/shard_map/ppermute | solution.py:425
  5.2 6.6 %collective-permute-start.4 = (bf16[256,256]{1,0:T(8,128)(2,1)S(1)}, bf16[256,256]{1,0:T(8,128)(2,1)S(1)}, u32[]{:S(2)}, u32[]{:S(2)}) collective-permute-start(bf16[256,256]{1,0:T(8,128)(2,1)S(1)} %get-tuple-element.48), channel_id=1, source_target_pairs={{0,3},{1,2},{2,1},{3,0},{4,7},{5,6},{6,5},{7,4},{8,11},{9,10},{10,... | collective-permute-start | bytes 393224 | tf_op jit(solution)/shard_map/ppermute | solution.py:425
  5.3 14.1 %collective-permute-start = (bf16[256,1024]{1,0:T(8,128)(2,1)S(1)}, bf16[256,1024]{1,0:T(8,128)(2,1)S(1)}, u32[]{:S(2)}, u32[]{:S(2)}) collective-permute-start(bf16[256,1024]{1,0:T(8,128)(2,1)S(1)} %get-tuple-element.43.refs_1_), channel_id=1, source_target_pairs={{0,16},{16,0},{1,17},{17,1},{2,18},{18,2},{3,19},{19,3},{4,20},{20... | collective-permute-start | bytes 1572872 | tf_op jit(solution)/shard_map/ppermute | solution.py:467
  11.9 14.3 %collective-permute-start.7 = (bf16[1024,256]{1,0:T(8,128)(2,1)S(1)}, bf16[1024,256]{1,0:T(8,128)(2,1)S(1)}, u32[]{:S(2)}, u32[]{:S(2)}) collective-permute-start(bf16[1024,256]{1,0:T(8,128)(2,1)S(1)} %get-tuple-element.54), channel_id=1, source_target_pairs={{0,4},{1,5},{2,6},{3,7},{4,0},{5,1},{6,2},{7,3},{8,12},{9,13},{10,... | collective-permute-start | bytes 1572872 | tf_op jit(solution)/shard_map/ppermute | solution.py:428
  13.6 12.7 %collective-permute-start.8 = (bf16[1024,256]{1,0:T(8,128)(2,1)S(1)}, bf16[1024,256]{1,0:T(8,128)(2,1)S(1)}, u32[]{:S(2)}, u32[]{:S(2)}) collective-permute-start(bf16[1024,256]{1,0:T(8,128)(2,1)S(1)} %get-tuple-element.54), channel_id=1, source_target_pairs={{4,8},{5,9},{6,10},{7,11},{8,4},{9,5},{10,6},{11,7},{20,24},{21,25... | collective-permute-start | bytes 1572872 | tf_op jit(solution)/shard_map/ppermute | solution.py:435
  14.3 10.6 %collective-permute-start.5 = (bf16[640,256]{1,0:T(8,128)(2,1)S(1)}, bf16[640,256]{1,0:T(8,128)(2,1)S(1)}, u32[]{:S(2)}, u32[]{:S(2)}) collective-permute-start(bf16[640,256]{1,0:T(8,128)(2,1)S(1)} %get-tuple-element.52), channel_id=1, source_target_pairs={{0,2},{1,3},{2,0},{3,1},{4,6},{5,7},{6,4},{7,5},{8,10},{9,11},{10,... | collective-permute-start | bytes 983048 | tf_op jit(solution)/shard_map/ppermute | solution.py:425
  15.8 9.2 %collective-permute-start.6 = (bf16[128,256]{1,0:T(8,128)(2,1)S(1)}, bf16[128,256]{1,0:T(8,128)(2,1)S(1)}, u32[]{:S(2)}, u32[]{:S(2)}) collective-permute-start(bf16[128,256]{1,0:T(8,128)(2,1)S(1)} %get-tuple-element.53), channel_id=1, source_target_pairs={{0,3},{1,2},{2,1},{3,0},{4,7},{5,6},{6,5},{7,4},{8,11},{9,10},{10,... | collective-permute-start | bytes 196616 | tf_op jit(solution)/shard_map/ppermute | solution.py:425
  19.4 19.7 %collective-permute-start.1 = (bf16[256,1024]{1,0:T(8,128)(2,1)S(1)}, bf16[256,1024]{1,0:T(8,128)(2,1)S(1)}, u32[]{:S(2)}, u32[]{:S(2)}) collective-permute-start(bf16[256,1024]{1,0:T(8,128)(2,1)S(1)} %collective-permute-done.refs_2_.refs_1_), channel_id=1, source_target_pairs={{0,1},{1,0},{2,3},{3,2},{4,5},{5,4},{6,7},{7,6},{8,9},{9,8},{10,11... | collective-permute-start | bytes 1572872 | tf_op jit(solution)/shard_map/ppermute | solution.py:425
  24.9 5.7 %collective-permute-start.9 = (bf16[640,256]{1,0:T(8,128)(2,1)S(1)}, bf16[640,256]{1,0:T(8,128)(2,1)S(1)}, u32[]{:S(2)}, u32[]{:S(2)}) collective-permute-start(bf16[640,256]{1,0:T(8,128)(2,1)S(1)} %collective-permute-done.5.refs_6_.refs_5_), channel_id=1, source_target_pairs={{0,1},{1,0},{2,3},{3,2},{4,5},{5,4},{6,7},{7,6},{8,9},{9,8},{10,11... | collective-permute-start | bytes 983048 | tf_op jit(solution)/shard_map/ppermute | solution.py:425
  31.6 16.4 %collective-permute-start.12 = (bf16[64,1024]{1,0:T(8,128)(2,1)S(1)}, bf16[64,1024]{1,0:T(8,128)(2,1)S(1)}, u32[]{:S(2)}, u32[]{:S(2)}) collective-permute-start(bf16[64,1024]{1,0:T(8,128)(2,1)S(1)} %get-tuple-element.69), channel_id=1, source_target_pairs={{0,4},{1,5},{2,6},{3,7},{4,0},{5,1},{6,2},{7,3},{8,12},{9,13},{10,... | collective-permute-start | bytes 393224 | tf_op jit(solution)/shard_map/ppermute | solution.py:428
  36.5 12.7 %collective-permute-start.13 = (bf16[64,1024]{1,0:T(8,128)(2,1)S(1)}, bf16[64,1024]{1,0:T(8,128)(2,1)S(1)}, u32[]{:S(2)}, u32[]{:S(2)}) collective-permute-start(bf16[64,1024]{1,0:T(8,128)(2,1)S(1)} %get-tuple-element.70), channel_id=1, source_target_pairs={{0,8},{1,9},{2,10},{3,11},{4,12},{5,13},{6,14},{7,15},{8,0},{9,1},... | collective-permute-start | bytes 393224 | tf_op jit(solution)/shard_map/ppermute | solution.py:428
  37.7 11.4 %collective-permute-start.14 = (bf16[64,1024]{1,0:T(8,128)(2,1)S(1)}, bf16[64,1024]{1,0:T(8,128)(2,1)S(1)}, u32[]{:S(2)}, u32[]{:S(2)}) collective-permute-start(bf16[64,1024]{1,0:T(8,128)(2,1)S(1)} %get-tuple-element.71), channel_id=1, source_target_pairs={{0,12},{1,13},{2,14},{3,15},{4,8},{5,9},{6,10},{7,11},{8,4},{9,5},... | collective-permute-start | bytes 393224 | tf_op jit(solution)/shard_map/ppermute | solution.py:428
  46.4 19.5 %collective-permute-start.10 = (bf16[1024,256]{1,0:T(8,128)(2,1)S(1)}, bf16[1024,256]{1,0:T(8,128)(2,1)S(1)}, u32[]{:S(2)}, u32[]{:S(2)}) collective-permute-start(bf16[1024,256]{1,0:T(8,128)(2,1)S(1)} %get-tuple-element.64), channel_id=1, source_target_pairs={{0,4},{1,5},{2,6},{3,7},{4,0},{5,1},{6,2},{7,3},{8,12},{9,13},{10,... | collective-permute-start | bytes 1572872 | tf_op jit(solution)/shard_map/ppermute | solution.py:428
  47.4 18.6 %collective-permute-start.11 = (bf16[1024,256]{1,0:T(8,128)(2,1)S(1)}, bf16[1024,256]{1,0:T(8,128)(2,1)S(1)}, u32[]{:S(2)}, u32[]{:S(2)}) collective-permute-start(bf16[1024,256]{1,0:T(8,128)(2,1)S(1)} %get-tuple-element.65), channel_id=1, source_target_pairs={{4,8},{5,9},{6,10},{7,11},{8,4},{9,5},{10,6},{11,7},{20,24},{21,25... | collective-permute-start | bytes 1572872 | tf_op jit(solution)/shard_map/ppermute | solution.py:435
  49.3 10.6 %collective-permute-start.15 = (bf16[512,256]{1,0:T(8,128)(2,1)S(1)}, bf16[512,256]{1,0:T(8,128)(2,1)S(1)}, u32[]{:S(2)}, u32[]{:S(2)}) collective-permute-start(bf16[512,256]{1,0:T(8,128)(2,1)S(1)} %shard_map.116), channel_id=1, source_target_pairs={{0,2},{1,3},{2,0},{3,1},{4,6},{5,7},{6,4},{7,5},{8,10},{9,11},{10,... | collective-permute-start | bytes 786440 | tf_op jit(solution)/shard_map/ppermute | solution.py:425
  50.8 9.0 %collective-permute-start.16 = (bf16[64,1024]{1,0:T(8,128)(2,1)S(1)}, bf16[64,1024]{1,0:T(8,128)(2,1)S(1)}, u32[]{:S(2)}, u32[]{:S(2)}) collective-permute-start(bf16[64,1024]{1,0:T(8,128)(2,1)S(1)} %shard_map.115.refs_1_.refs_0_), channel_id=1, source_target_pairs={{0,2},{1,3},{2,18},{3,19},{4,6},{5,7},{6,22},{7,23},{8,10},{9,11},... | collective-permute-start | bytes 393224 | tf_op jit(solution)/shard_map/ppermute | solution.py:531
  51.4 8.5 %collective-permute-start.17 = (bf16[64,1024]{1,0:T(8,128)(2,1)S(1)}, bf16[64,1024]{1,0:T(8,128)(2,1)S(1)}, u32[]{:S(2)}, u32[]{:S(2)}) collective-permute-start(bf16[64,1024]{1,0:T(8,128)(2,1)S(1)} %shard_map.115.refs_1_.refs_0_), channel_id=1, source_target_pairs={{2,16},{3,17},{6,20},{7,21},{10,24},{11,25},{14,28},{15,29},{16,2}... | collective-permute-start | bytes 393224 | tf_op jit(solution)/shard_map/ppermute | solution.py:532
  59.9 8.8 %collective-permute-start.21 = (bf16[64,1024]{1,0:T(8,128)(2,1)S(1)}, bf16[64,1024]{1,0:T(8,128)(2,1)S(1)}, u32[]{:S(2)}, u32[]{:S(2)}) collective-permute-start(bf16[64,1024]{1,0:T(8,128)(2,1)S(1)} %shard_map.117.refs_5_.refs_0_), channel_id=1, source_target_pairs={{0,4},{1,5},{2,6},{3,7},{4,0},{5,1},{6,2},{7,3},{8,12},{9,13},{10,... | collective-permute-start | bytes 393224 | tf_op jit(solution)/shard_map/ppermute | solution.py:428
  63.5 10.4 %collective-permute-start.22 = (bf16[64,1024]{1,0:T(8,128)(2,1)S(1)}, bf16[64,1024]{1,0:T(8,128)(2,1)S(1)}, u32[]{:S(2)}, u32[]{:S(2)}) collective-permute-start(bf16[64,1024]{1,0:T(8,128)(2,1)S(1)} %shard_map.117.refs_5_.refs_0_), channel_id=1, source_target_pairs={{0,8},{1,9},{2,10},{3,11},{4,12},{5,13},{6,14},{7,15},{8,0},{9,1},... | collective-permute-start | bytes 393224 | tf_op jit(solution)/shard_map/ppermute | solution.py:428
  64.3 9.6 %collective-permute-start.23 = (bf16[64,1024]{1,0:T(8,128)(2,1)S(1)}, bf16[64,1024]{1,0:T(8,128)(2,1)S(1)}, u32[]{:S(2)}, u32[]{:S(2)}) collective-permute-start(bf16[64,1024]{1,0:T(8,128)(2,1)S(1)} %shard_map.117.refs_5_.refs_0_), channel_id=1, source_target_pairs={{0,12},{1,13},{2,14},{3,15},{4,8},{5,9},{6,10},{7,11},{8,4},{9,5},... | collective-permute-start | bytes 393224 | tf_op jit(solution)/shard_map/ppermute | solution.py:428
  66.0 11.1 %copy-start = (bf16[512,1024]{1,0:T(8,128)(2,1)S(1)}, bf16[512,1024]{1,0:T(8,128)(2,1)}, u32[]{:S(2)}) copy-start(bf16[512,1024]{1,0:T(8,128)(2,1)} %refs_0_.3) | copy-start | bytes 3145732
  66.2 7.7 %collective-permute-start.19 = (bf16[256,256]{1,0:T(8,128)(2,1)S(1)}, bf16[256,256]{1,0:T(8,128)(2,1)S(1)}, u32[]{:S(2)}, u32[]{:S(2)}) collective-permute-start(bf16[256,256]{1,0:T(8,128)(2,1)S(1)} %get-tuple-element.74), channel_id=1, source_target_pairs={{0,2},{1,3},{2,0},{3,1},{4,6},{5,7},{6,4},{7,5},{8,10},{9,11},{10,... | collective-permute-start | bytes 393224 | tf_op jit(solution)/shard_map/ppermute | solution.py:425
  68.7 5.8 %collective-permute-start.20 = (bf16[256,256]{1,0:T(8,128)(2,1)S(1)}, bf16[256,256]{1,0:T(8,128)(2,1)S(1)}, u32[]{:S(2)}, u32[]{:S(2)}) collective-permute-start(bf16[256,256]{1,0:T(8,128)(2,1)S(1)} %get-tuple-element.75), channel_id=1, source_target_pairs={{0,3},{1,2},{2,1},{3,0},{4,7},{5,6},{6,5},{7,4},{8,11},{9,10},{10,... | collective-permute-start | bytes 393224 | tf_op jit(solution)/shard_map/ppermute | solution.py:425
  74.5 3.8 %collective-permute-start.24 = (bf16[256,1024]{1,0:T(8,128)(2,1)S(1)}, bf16[256,1024]{1,0:T(8,128)(2,1)S(1)}, u32[]{:S(2)}, u32[]{:S(2)}) collective-permute-start(bf16[256,1024]{1,0:T(8,128)(2,1)S(1)} %shard_map.120.refs_0_), channel_id=1, source_target_pairs={{0,1},{1,0},{2,3},{3,2},{4,5},{5,4},{6,7},{7,6},{8,9},{9,8},{10,11... | collective-permute-start | bytes 1572872 | tf_op jit(solution)/shard_map/ppermute | solution.py:425
  74.6 2.5 %collective-permute-start.18 = (bf16[768,256]{1,0:T(8,128)(2,1)S(1)}, bf16[768,256]{1,0:T(8,128)(2,1)S(1)}, u32[]{:S(2)}, u32[]{:S(2)}) collective-permute-start(bf16[768,256]{1,0:T(8,128)(2,1)S(1)} %get-tuple-element.73), channel_id=1, source_target_pairs={{0,1},{1,0},{2,3},{3,2},{4,5},{5,4},{6,7},{7,6},{8,9},{9,8},{10,11... | collective-permute-start | bytes 1179656 | tf_op jit(solution)/shard_map/ppermute | solution.py:425

commit v4 on v3

--- a/solution.py
+++ b/solution.py
@@ -127,13 +127,16 @@
         loads[6].wait()
 
 
-def join_kernel(parts, *refs):
-    passed = (len(refs) - parts - 1) // 2
-    out = refs[parts + passed]
-    size = out.shape[0] // parts
-    for m, source in enumerate(refs[:parts]):
+def join_kernel(*refs):
+    out = refs[-1]
+    size = out.shape[0] // (len(refs) - 1)
+    for m, source in enumerate(refs[:-1]):
         out[m * size : (m + 1) * size, :] = source[0:size, :]
-    for source, target in zip(refs[parts : parts + passed], refs[parts + passed + 1 :]):
+
+
+def pass_kernel(*refs):
+    half = len(refs) // 2
+    for source, target in zip(refs[:half], refs[half:]):
         target[...] = source[...]
 
 
@@ -175,8 +178,8 @@
     far_kv = refs[2:group]
     own_rest = refs[group]
     far_rest = refs[group + 1 : 2 * group - 1]
-    sides = refs[2 * group - 1 : 2 * group + 1]
-    keys, vals, keys_t, queries, att_t, att, stats, vals_t = refs[2 * group + 1 :]
+    sides = refs[2 * group - 1 : 2 * group + 3]
+    keys, vals, keys_t, queries, att_t, att, stats, vals_t = refs[2 * group + 3 :]
     rows, cols = far_rest[-1].shape
     plane = group * rows
     span = rows + 2 * WINDOW
@@ -190,8 +193,9 @@
         at = pl.ds(pl.multiple_of(spot, 128), rows)
         queries[at, :] = asked[0][asked[1] : asked[1] + rows, :]
         held = own_kv if m == 0 else near_all if m == 1 else far_kv[m - 2]
-        base = m * 2 * rows
-        sources = [(held, 0, 1), (sides[0], base, 2 * even), (sides[1], base, 2 - 2 * even)]
+        first, second = sides[0:2] if m == 0 else sides[2:4]
+        base = max(m - 1, 0) * 2 * rows
+        sources = [(held, 0, 1), (first, base, 2 * even), (second, base, 2 - 2 * even)]
         for source, base, side in sources:
             at = pl.ds(pl.multiple_of(side * plane + spot, 128), rows)
             keys[at, :] = source[base : base + rows, :]
@@ -329,7 +333,7 @@
         target[plane : 2 * plane, :] = value_sum[kept, :].astype(target.dtype)
 
 
-def settle_kernel(group, own, from_first, from_second, near, far, *pieces):
+def settle_kernel(group, own, from_first, from_second, *pieces):
     rows = pieces[0].shape[0] // 2
     plane = group * rows
     inner = lax.rem(lax.axis_index("seq"), group)
@@ -339,31 +343,43 @@
             at = pl.ds(pl.multiple_of(part * plane + spot, 128), rows)
             summed = own[at, :] + from_first[at, :].astype(F32) + from_second[at, :].astype(F32)
             pieces[m][part * rows : (part + 1) * rows, :] = summed.astype(BF16)
-    pieces[1][2 * rows : 4 * rows, :] = near[...]
-    pieces[1][4 * rows : 6 * rows, :] = far[2 * rows : 4 * rows, :]
-
-
-def unpack_kernel(group, fast, near, far, farther, *refs):
-    sums, mine, early = refs[:group], refs[group], refs[group + 1]
-    outs, out, att = refs[group + 2 : group + 5], refs[group + 5], refs[group + 6]
+
+
+def relay_kernel(near, far, out):
+    size = near.shape[0]
+    out[0:size, :] = near[...]
+    out[size : 2 * size, :] = far[size : 2 * size, :]
+
+
+def unpack_kernel(group, *refs):
+    pieces, outs = refs[:group], refs[group:]
+    rows, width = outs[0].shape
+    cols = width // group
+    inner = lax.rem(lax.axis_index("seq"), group)
+    for m in range(group):
+        at = pl.ds(pl.multiple_of((inner ^ m) * cols, 128), cols)
+        for part in range(2):
+            outs[part][:, at] = pieces[m][part * rows : (part + 1) * rows, :]
+
+
+def project_kernel(group, fast, near, far, farther, mine, early, relayed, grad_query, out, done, att):
     rows, width = out.shape
     cols = width // group
     half = width // 2
     inner = lax.rem(lax.axis_index("seq"), group)
     first = lax.axis_index("doc") if fast else 0
-    held = ((mine, 0), (sums[1], 2 * rows), (early, 0), (sums[1], 4 * rows))
+    held = ((mine, 0), (relayed, 0), (early, 0), (relayed, 2 * rows))
     for m in range(group):
         at = pl.ds(pl.multiple_of((inner ^ m) * cols, 128), cols)
-        outs[1][:, at] = sums[m][0:rows, :]
-        outs[2][:, at] = sums[m][rows : 2 * rows, :]
         source, base = held[m]
-        outs[0][:, at] = source[base : base + rows, :]
+        grad_query[:, at] = source[base : base + rows, :]
         att[:, at] = source[base + rows : base + 2 * rows, :]
     total = dot_nn(att[:, pl.ds(pl.multiple_of(first * half, 128), half)], near[...])
     for side, weight in ((0, far), (1, farther)):
         start = (1 - first) * half + (lax.rem(inner, 2) ^ side) * cols
         total += dot_nn(att[:, pl.ds(pl.multiple_of(start, 128), cols)], weight[...])
     out[...] = total.astype(BF16)
+    done[...] = jnp.zeros_like(done)
 
 
 def add_kernel(*refs):
@@ -371,10 +387,6 @@
     for ref in refs[1:-1]:
         total += ref[...].astype(F32)
     refs[-1][...] = total.astype(BF16)
-
-
-def pass_kernel(source, target):
-    target[...] = source[...]
 
 
 def cross_kernel(group, own, first, second, out):
@@ -452,14 +464,20 @@
     far_kv = [inner_swap(packed[m - 2], m) for m in range(2, group)]
     own_rest, near_all, rest_first, rest_last, limits, *weight = packed[group - 2 :]
     near_all = inner_swap(near_all, 1)
-    joined, rest_first, rest_last = call(
-        functools.partial(join_kernel, group),
-        [((2 * group * rows, cols), BF16), *rest],
-        (own_kv, near_all, *far_kv, rest_first, rest_last),
-        flops=1 << 20, moved=1 << 20,
-    )
-    sides = [outer_first(joined), outer_second(joined)]
+    (sent_kv,) = call(
+        pass_kernel, [((2 * rows, cols), BF16)], (own_kv,), flops=3 << 30, moved=1 << 18
+    )
+    sides = [outer_first(sent_kv), outer_second(sent_kv)]
+    rest_first, rest_last = call(
+        pass_kernel, rest, (rest_first, rest_last),
+        after=(near_all, *far_kv), flops=1 << 18, moved=1 << 20,
+    )
     far_rest = [inner_swap(rest_first, 2), inner_swap(rest_last, 3)]
+    (joined,) = call(
+        join_kernel, [((2 * (group - 1) * rows, cols), BF16)], (near_all, *far_kv),
+        after=(rest_last, *sides), flops=3 << 30, moved=1 << 20,
+    )
+    sides += [outer_first(joined), outer_second(joined)]
     grads = [own_rest, near_all, far_rest[0], inner_swap(far_rest[0], 1)]
     inner = lax.axis_index("seq") % group
     if fast:
@@ -515,8 +533,8 @@
             add_kernel, part_shape, swapped, after=(early_near,), flops=1 << 18, moved=1 << 19
         )
         (early_far,) = call(
-            pass_kernel, [(early_far.shape, BF16)], (early_far,), after=(line,),
-            flops=1 << 18, moved=1 << 19,
+            pass_kernel, [(early_far.shape, BF16)], (early_far,), after=(swapped[1],),
+            flops=2 << 30, moved=1 << 19,
         )
         flat = [(d, i) for d in range(doc_count) for i in range(seq_count)]
         first_pairs, second_pairs = [], []
@@ -546,28 +564,37 @@
         before_settle = ()
         early = inner_swap(early_far, 2)
 
+    (relayed,) = call(
+        relay_kernel, [((4 * rows, cols), BF16)], (early_near, early),
+        after=(), flops=1 << 18, moved=1 << 20,
+    )
+    relayed = inner_swap(relayed, 1)
+    grad_query, layer_out, projected = call(
+        functools.partial(project_kernel, group, fast),
+        [((rows, width), BF16)] * 2 + [((8, 128), F32)],
+        (half_near, *half_far, early_own, early, relayed),
+        scratch=[pltpu.VMEM((rows, width), BF16)],
+        flops=1 << 30, moved=4 << 20,
+    )
     sums = call(
         functools.partial(settle_kernel, group),
-        [(((6 if m == 1 else 2) * rows, cols), BF16) for m in range(group)],
-        (own, outer_first(to_first), outer_second(to_second), early_near, early),
+        [((2 * rows, cols), BF16)] * group,
+        (own, outer_first(to_first), outer_second(to_second)),
         after=before_settle, flops=10 << 30, moved=2 << 20,
     )
     sums = [sums[0]] + [inner_swap(sums[m], m) for m in range(1, group)]
     if fast:
         (gathered,) = call(
             functools.partial(gather_kernel, group), [((cols, width), BF16)], gathered,
-            after=sums[2:], flops=1 << 18, moved=1 << 20,
+            after=(*sums[1:], projected), flops=1 << 18, moved=1 << 20,
         )
         (grad_weight,) = call(
             functools.partial(finish_kernel, scale), [((width // doc_count, width), F32)],
             (gathered, inner_swap(gathered, 1)), flops=1 << 20, moved=4 << 20,
         )
-    grad_query, grad_key, grad_value, layer_out = call(
-        functools.partial(unpack_kernel, group, fast),
-        [((rows, width), BF16)] * 4,
-        (half_near, *half_far, *sums, early_own, early),
-        scratch=[pltpu.VMEM((rows, width), BF16)],
-        flops=1 << 30, moved=4 << 20,
+    grad_key, grad_value = call(
+        functools.partial(unpack_kernel, group), [((rows, width), BF16)] * 2, sums,
+        flops=1 << 20, moved=1 << 20,
     )
     return (layer_out[None], grad_query[None], grad_key[None], grad_value[None], grad_weight)
 

time: 80 us -> 78.7 us (0.984)
  waiting for transfers between devices: 31.8 us -> 25 us
  starting transfers between devices: 30 us -> 34.5 us
  Pallas kernels: 17.3 us -> 18.1 us
    ppermute x8 -> x9, waiting for transfers between devices: 7.51 us -> 4.27 us  [outer_swap(): lax.ppermute(value, 'seq', [(i, i ^ m * group) for i in range(seq_count)])]
    ppermute x12 -> x13, waiting for transfers between devices: 13 us -> 9.81 us  [inner_swap(): return lax.ppermute(value, 'seq', [(i, i ^ m) for i in range(seq_count)])]
    ppermute x8 -> x9, starting transfers between devices: 16.2 us -> 19.2 us  [outer_swap(): lax.ppermute(value, 'seq', [(i, i ^ m * group) for i in range(seq_count)])]
    ppermute x1, waiting for transfers between devices: 3.41 us -> 1.8 us  [body(): far = lax.ppermute(near, 'doc', [(0, 1), (1, 0)])]
    ppermute x1, waiting for transfers between devices: 7.8 us -> 9.1 us  [body(): got_first = lax.ppermute(line, ('doc', 'seq'), first_pairs)]
    pallas_call x12 -> x16, Pallas kernels: 17.3 us -> 18.1 us  [call(): pl.pallas_call(run, out_shape=outs, in_specs=[HBM] * hbm + [VMEM] * (coun...]
    ppermute x2 -> x3, starting transfers between devices: 1.36 us -> 2.02 us  [outer_second(): lax.ppermute(value, 'seq', [(a, b) for a, b in pairs_of if 0 <= b < seq_c...]
    ppermute x12 -> x13, starting transfers between devices: 9.59 us -> 9.55 us  [inner_swap(): return lax.ppermute(value, 'seq', [(i, i ^ m) for i in range(seq_count)])]
  transfers between devices with their start and end apart: 25 -> 28, of which waited for: 11 -> 9; matrix products, arithmetic and copies ran while one was open for 0% -> 0% of each run, Pallas kernels for 18% -> 19%
where the time goes in v4:
time: 78.7 us; the launch traced here: 78.5 us
  starting transfers between devices  34.5 us (44%)
  waiting for transfers between devices  25 us (32%)
  Pallas kernels  18.1 us (23%)
  between operations  0.85 us (1%)
    ppermute x9, starting transfers between devices, outer_swap(): lax.ppermute(value, 'seq', [(i, i ^ m * group) for i in range(seq_count)])  19.2 us
    pallas_call x16, Pallas kernels, call(): pl.pallas_call(run, out_shape=outs, in_specs=[HBM] * hbm + [VMEM] * (coun...  18.1 us
    ppermute x13, waiting for transfers between devices, inner_swap(): return lax.ppermute(value, 'seq', [(i, i ^ m) for i in range(seq_count)])  9.81 us
    ppermute x13, starting transfers between devices, inner_swap(): return lax.ppermute(value, 'seq', [(i, i ^ m) for i in range(seq_count)])  9.55 us
    ppermute x1, waiting for transfers between devices, body(): got_first = lax.ppermute(line, ('doc', 'seq'), first_pairs)  9.1 us
    ppermute x9, waiting for transfers between devices, outer_swap(): lax.ppermute(value, 'seq', [(i, i ^ m * group) for i in range(seq_count)])  4.27 us
    ppermute x3, starting transfers between devices, outer_second(): lax.ppermute(value, 'seq', [(a, b) for a, b in pairs_of if 0 <= b < seq_c...  2.02 us
    ppermute x1, starting transfers between devices, body(): far = lax.ppermute(near, 'doc', [(0, 1), (1, 0)])  1.92 us
  transfers between devices with their start and end apart: 28, of which 9 were waited for; matrix products, arithmetic and copies ran while one was open for 0% of the time, Pallas kernels for 19%

profile of v4, /device:TPU:0, one launch (start us, length us, event | category | flops | bytes accessed | tf_op | source)
XLA Modules:
  0.0 78.5 jit_solution(4616032671218583781)
XLA Ops:
  0.6 1.4 %shard_map.110 = (bf16[256,256]{1,0:T(8,128)(2,1)S(1)}, bf16[256,256]{1,0:T(8,128)(2,1)S(1)}, bf16[256,256]{1,0:T(8,128)(2,1)S(1)}, bf16[640,256]{1,0:T(8,128)(2...) custom-call(s32[1,4]{1,0:T(1,128)} %refs_0_.2, ...), custom_call_target="tpu_custom_call" | custom-call | flops 1048576 | bytes 4194304 | tf_op jit(solution)/shard_map/pallas_call | solution.py:38
  2.1 0.5 collective-permute-start.2
  2.6 2.6 %collective-permute-start.3 = (bf16[256,256]{1,0:T(8,128)(2,1)S(1)}, bf16[256,256]{1,0:T(8,128)(2,1)S(1)}, u32[]{:S(2)}, u32[]{:S(2)}) collective-permute-start(bf16[256,256]{1,0:T(8,128)(2,1)S(1)} %get-tuple-element.47), channel_id=1, source_target_pairs={{0,2},{1,3},{2,0},{3,1},{4,6},{5,7},{6,4},{7,5},{8,10},{9,11},{10,... | collective-permute-start | bytes 393224 | tf_op jit(solution)/shard_map/ppermute | solution.py:437
  5.2 0.1 collective-permute-start.4
  5.3 1.8 %collective-permute-start.7 = (bf16[256,256]{1,0:T(8,128)(2,1)S(1)}, bf16[256,256]{1,0:T(8,128)(2,1)S(1)}, u32[]{:S(2)}, u32[]{:S(2)}) collective-permute-start(bf16[256,256]{1,0:T(8,128)(2,1)S(1)} %shard_map.112), channel_id=1, source_target_pairs={{0,4},{1,5},{2,6},{3,7},{4,0},{5,1},{6,2},{7,3},{8,12},{9,13},{10,... | collective-permute-start | bytes 393224 | tf_op jit(solution)/shard_map/ppermute | solution.py:440
  7.1 0.7 collective-permute-start.8
  7.8 1.8 %collective-permute-done.3.refs_3_.refs_1_ = bf16[256,256]{1,0:T(8,128)(2,1)S(1)} collective-permute-done((bf16[256,256]{1,0:T(8,128)(2,1)S(1)}, bf16[256,256]{1,0:T(8,128)(2,1)S(1)}, u32[]{:S(2)}, u32[]{:S(2)}) %collective-permute-start.3) | collective-permute-done | bytes 131104 | tf_op jit(solution)/shard_map/ppermute | solution.py:437
  9.5 1.9 %collective-permute-start = (bf16[256,1024]{1,0:T(8,128)(2,1)S(1)}, bf16[256,1024]{1,0:T(8,128)(2,1)S(1)}, u32[]{:S(2)}, u32[]{:S(2)}) collective-permute-start(bf16[256,1024]{1,0:T(8,128)(2,1)S(1)} %get-tuple-element.43.refs_1_), channel_id=1, source_target_pairs={{0,16},{16,0},{1,17},{17,1},{2,18},{18,2},{3,19},{19,3},{4,20},{20... | collective-permute-start | bytes 1572872 | tf_op jit(solution)/shard_map/ppermute | solution.py:485
  11.5 0.4 collective-permute-done.4.refs_4_.refs_2_
  11.8 0.0 collective-permute-done.2.refs_2_.refs_0_.refs_4_
  11.9 0.7 collective-permute-start.10
  12.6 7.0 %collective-permute-start.9 = (bf16[768,256]{1,0:T(8,128)(2,1)S(1)}, bf16[768,256]{1,0:T(8,128)(2,1)S(1)}, u32[]{:S(2)}, u32[]{:S(2)}) collective-permute-start(bf16[768,256]{1,0:T(8,128)(2,1)S(1)} %shard_map.113), channel_id=1, source_target_pairs={{0,4},{1,5},{2,6},{3,7},{4,0},{5,1},{6,2},{7,3},{8,12},{9,13},{10,... | collective-permute-start | bytes 1179656 | tf_op jit(solution)/shard_map/ppermute | solution.py:440
  19.6 1.5 %collective-permute-start.5 = (bf16[640,256]{1,0:T(8,128)(2,1)S(1)}, bf16[640,256]{1,0:T(8,128)(2,1)S(1)}, u32[]{:S(2)}, u32[]{:S(2)}) collective-permute-start(bf16[640,256]{1,0:T(8,128)(2,1)S(1)} %get-tuple-element.52), channel_id=1, source_target_pairs={{0,2},{1,3},{2,0},{3,1},{4,6},{5,7},{6,4},{7,5},{8,10},{9,11},{10,... | collective-permute-start | bytes 983048 | tf_op jit(solution)/shard_map/ppermute | solution.py:437
  21.2 1.8 %collective-permute-done.refs_2_.refs_1_ = bf16[256,1024]{1,0:T(8,128)(2,1)S(1)} collective-permute-done((bf16[256,1024]{1,0:T(8,128)(2,1)S(1)}, bf16[256,1024]{1,0:T(8,128)(2,1)S(1)}, u32[]{:S(2)}, u32[]{:S(2)}) %collective-permute-start) | collective-permute-done | bytes 524320 | tf_op jit(solution)/shard_map/ppermute | solution.py:485
  23.0 0.0 collective-permute-start.1
  23.0 5.6 %collective-permute-done.5.refs_6_.refs_5_ = bf16[640,256]{1,0:T(8,128)(2,1)S(1)} collective-permute-done((bf16[640,256]{1,0:T(8,128)(2,1)S(1)}, bf16[640,256]{1,0:T(8,128)(2,1)S(1)}, u32[]{:S(2)}, u32[]{:S(2)}) %collective-permute-start.5) | collective-permute-done | bytes 327712 | tf_op jit(solution)/shard_map/ppermute | solution.py:437
  28.6 0.0 collective-permute-start.11
  28.6 0.0 collective-permute-done.6.refs_7_
  28.6 0.0 collective-permute-done.10.refs_11_
  28.6 4.3 %shard_map.114 = (bf16[1536,256]{1,0:T(8,128)(2,1)S(1)}, bf16[1536,256]{1,0:T(8,128)(2,1)S(1)}, bf16[256,1536]{1,0:T(8,128)(2,1)S(1)}, bf16[512,256]{1,0:T(8,128...) custom-call(s32[8,512]{1,0:T(8,128)S(1)} %get-tuple-element.44.refs_0_, ...), custom_call_target="tpu_custom_call" | custom-call | flops 4294967296 | bytes 4194304 | tf_op jit(solution)/shard_map/pallas_call | solution.py:38
  33.0 1.1 %shard_map.115 = (bf16[512,256]{1,0:T(8,128)(2,1)S(1)}, bf16[64,1024]{1,0:T(8,128)(2,1)S(1)}, bf16[64,1024]{1,0:T(8,128)(2,1)S(1)}, bf16[64,1024]{1,0:T(8,128)(2,1)S(1)}, bf16[64,1024]{1,0:T(8,128)(2,1)S(1)}) custom-call(bf16[256,512]{1,0:T(8,128)(2,1)S(1)} %get-tuple-element.58.refs_0_, bf16[256,1024]{1,0:T(8,128)(2,1)S(1)} %get-tuple-element.43.refs_1_, ...), custom_call_target="tpu_custom_call" | custom-call | flops 1073741824 | bytes 4194304 | tf_op jit(solution)/shard_map/pallas_call | solution.py:38
  34.1 1.0 %collective-permute-start.12 = (bf16[64,1024]{1,0:T(8,128)(2,1)S(1)}, bf16[64,1024]{1,0:T(8,128)(2,1)S(1)}, u32[]{:S(2)}, u32[]{:S(2)}) collective-permute-start(bf16[64,1024]{1,0:T(8,128)(2,1)S(1)} %get-tuple-element.64), channel_id=1, source_target_pairs={{0,4},{1,5},{2,6},{3,7},{4,0},{5,1},{6,2},{7,3},{8,12},{9,13},{10,... | collective-permute-start | bytes 393224 | tf_op jit(solution)/shard_map/ppermute | solution.py:440
  35.1 1.1 %collective-permute-start.17 = (bf16[64,1024]{1,0:T(8,128)(2,1)S(1)}, bf16[64,1024]{1,0:T(8,128)(2,1)S(1)}, u32[]{:S(2)}, u32[]{:S(2)}) collective-permute-start(bf16[64,1024]{1,0:T(8,128)(2,1)S(1)} %get-tuple-element.72), channel_id=1, source_target_pairs={{0,8},{1,9},{2,10},{3,11},{4,12},{5,13},{6,14},{7,15},{8,0},{9,1},... | collective-permute-start | bytes 393224 | tf_op jit(solution)/shard_map/ppermute | solution.py:440
  36.2 2.3 %collective-permute-start.18 = (bf16[64,1024]{1,0:T(8,128)(2,1)S(1)}, bf16[64,1024]{1,0:T(8,128)(2,1)S(1)}, u32[]{:S(2)}, u32[]{:S(2)}) collective-permute-start(bf16[64,1024]{1,0:T(8,128)(2,1)S(1)} %get-tuple-element.73), channel_id=1, source_target_pairs={{0,12},{1,13},{2,14},{3,15},{4,8},{5,9},{6,10},{7,11},{8,4},{9,5},... | collective-permute-start | bytes 393224 | tf_op jit(solution)/shard_map/ppermute | solution.py:440
  38.5 7.3 %shard_map.116 = (bf16[1024,256]{1,0:T(8,128)(2,1)S(1)}, f32[1024,256]{1,0:T(8,128)S(1)}, bf16[1024,256]{1,0:T(8,128)(2,1)S(1)}, bf16[256,256]{1,0:T(8,128)(2,1)...) custom-call(s32[8,512]{1,0:T(8,128)S(1)} %get-tuple-element.44.refs_0_, ...), custom_call_target="tpu_custom_call" | custom-call | flops 8589934592 | bytes 4194304 | tf_op jit(solution)/shard_map/pallas_call | solution.py:38
  45.8 0.1 collective-permute-start.15
  46.0 0.7 collective-permute-start.16
  46.7 1.6 %collective-permute-start.13 = (bf16[512,256]{1,0:T(8,128)(2,1)S(1)}, bf16[512,256]{1,0:T(8,128)(2,1)S(1)}, u32[]{:S(2)}, u32[]{:S(2)}) collective-permute-start(bf16[512,256]{1,0:T(8,128)(2,1)S(1)} %shard_map.117), channel_id=1, source_target_pairs={{0,2},{1,3},{2,0},{3,1},{4,6},{5,7},{6,4},{7,5},{8,10},{9,11},{10,... | collective-permute-start | bytes 786440 | tf_op jit(solution)/shard_map/ppermute | solution.py:437
  48.3 0.1 shard_map.120.refs_0_
  48.4 1.2 %collective-permute-start.19 = (bf16[64,1024]{1,0:T(8,128)(2,1)S(1)}, bf16[64,1024]{1,0:T(8,128)(2,1)S(1)}, u32[]{:S(2)}, u32[]{:S(2)}) collective-permute-start(bf16[64,1024]{1,0:T(8,128)(2,1)S(1)} %shard_map.120.refs_0_), channel_id=1, source_target_pairs={{0,2},{1,3},{2,18},{3,19},{4,6},{5,7},{6,22},{7,23},{8,10},{9,11},... | collective-permute-start | bytes 393224 | tf_op jit(solution)/shard_map/ppermute | solution.py:549
  49.5 0.7 collective-permute-start.20
  50.2 9.1 %collective-permute-done.19.refs_1_ = bf16[64,1024]{1,0:T(8,128)(2,1)S(1)} collective-permute-done((bf16[64,1024]{1,0:T(8,128)(2,1)S(1)}, bf16[64,1024]{1,0:T(8,128)(2,1)S(1)}, u32[]{:S(2)}, u32[]{:S(2)}) %collective-permute-start.19) | collective-permute-done | bytes 131104 | tf_op jit(solution)/shard_map/ppermute | solution.py:549
  59.3 3.3 %collective-permute-start.24 = (bf16[64,1024]{1,0:T(8,128)(2,1)S(1)}, bf16[64,1024]{1,0:T(8,128)(2,1)S(1)}, u32[]{:S(2)}, u32[]{:S(2)}) collective-permute-start(bf16[64,1024]{1,0:T(8,128)(2,1)S(1)} %shard_map.121.refs_3_.refs_0_), channel_id=1, source_target_pairs={{0,4},{1,5},{2,6},{3,7},{4,0},{5,1},{6,2},{7,3},{8,12},{9,13},{10,... | collective-permute-start | bytes 393224 | tf_op jit(solution)/shard_map/ppermute | solution.py:440
  62.7 0.9 %collective-permute-start.25 = (bf16[64,1024]{1,0:T(8,128)(2,1)S(1)}, bf16[64,1024]{1,0:T(8,128)(2,1)S(1)}, u32[]{:S(2)}, u32[]{:S(2)}) collective-permute-start(bf16[64,1024]{1,0:T(8,128)(2,1)S(1)} %shard_map.121.refs_3_.refs_0_), channel_id=1, source_target_pairs={{0,8},{1,9},{2,10},{3,11},{4,12},{5,13},{6,14},{7,15},{8,0},{9,1},... | collective-permute-start | bytes 393224 | tf_op jit(solution)/shard_map/ppermute | solution.py:440
  63.6 1.5 %collective-permute-start.26 = (bf16[64,1024]{1,0:T(8,128)(2,1)S(1)}, bf16[64,1024]{1,0:T(8,128)(2,1)S(1)}, u32[]{:S(2)}, u32[]{:S(2)}) collective-permute-start(bf16[64,1024]{1,0:T(8,128)(2,1)S(1)} %shard_map.121.refs_3_.refs_0_), channel_id=1, source_target_pairs={{0,12},{1,13},{2,14},{3,15},{4,8},{5,9},{6,10},{7,11},{8,4},{9,5},... | collective-permute-start | bytes 393224 | tf_op jit(solution)/shard_map/ppermute | solution.py:440
  65.1 0.1 collective-permute-start.14
  65.2 0.0 copy-start
  65.2 0.2 shard_map.122
  65.4 0.5 collective-permute-start.21
  65.9 0.7 collective-permute-done.24.refs_1_
  66.6 2.5 %collective-permute-start.22 = (bf16[256,256]{1,0:T(8,128)(2,1)S(1)}, bf16[256,256]{1,0:T(8,128)(2,1)S(1)}, u32[]{:S(2)}, u32[]{:S(2)}) collective-permute-start(bf16[256,256]{1,0:T(8,128)(2,1)S(1)} %get-tuple-element.76), channel_id=1, source_target_pairs={{0,2},{1,3},{2,0},{3,1},{4,6},{5,7},{6,4},{7,5},{8,10},{9,11},{10,... | collective-permute-start | bytes 393224 | tf_op jit(solution)/shard_map/ppermute | solution.py:437
  69.1 1.2 %shard_map.119 = (bf16[128,1024]{1,0:T(8,128)(2,1)}, bf16[128,1024]{1,0:T(8,128)(2,1)}, f32[8,128]{1,0:T(8,128)S(1)}) custom-call(bf16[512,1024]{1,0:T(8,128)(2,1)S(1)} %copy-done, bf16[256,1024]{1,0:T(8,128)(2,1)S(1)} %collective-permute-done.refs_2_.refs_1_, bf16[256,1024]{1,0:T(8,128)(2,1)S(1)} %collective-permute-done.1.refs_8_.refs_2_, ...), custom_call_target="tpu_custom_call" | custom-call | flops 1073741824 | bytes 4194304 | tf_op jit(solution)/shard_map/pallas_call | solution.py:38
  70.3 3.6 %collective-permute-done.25.refs_2_ = bf16[64,1024]{1,0:T(8,128)(2,1)S(1)} collective-permute-done((bf16[64,1024]{1,0:T(8,128)(2,1)S(1)}, bf16[64,1024]{1,0:T(8,128)(2,1)S(1)}, u32[]{:S(2)}, u32[]{:S(2)}) %collective-permute-start.25) | collective-permute-done | bytes 131104 | tf_op jit(solution)/shard_map/ppermute | solution.py:440
  73.9 1.1 %collective-permute-done.23.refs_3_.refs_6_ = bf16[256,256]{1,0:T(8,128)(2,1)S(1)} collective-permute-done((bf16[256,256]{1,0:T(8,128)(2,1)S(1)}, bf16[256,256]{1,0:T(8,128)(2,1)S(1)}, u32[]{:S(2)}, u32[]{:S(2)}) %collective-permute-start.23) | collective-permute-done | bytes 131104 | tf_op jit(solution)/shard_map/ppermute | solution.py:437
  75.0 0.2 collective-permute-start.27
  75.2 0.8 %shard_map.123 = (bf16[128,1024]{1,0:T(8,128)(2,1)}, bf16[128,1024]{1,0:T(8,128)(2,1)}) custom-call(bf16[256,256]{1,0:T(8,128)(2,1)S(1)} %get-tuple-element.74.refs_0_, bf16[256,256]{1,0:T(8,128)(2,1)S(1)} %collective-permute-done.21.refs_1_.refs_4_, bf16[256,256]{1,0:T(8,128)(2,1)S(1)} %collective-permute-done.22.refs_2_.refs_5_, ...), custom_call_target="tpu_custom_call" | custom-call | flops 1048576 | bytes 1048576 | tf_op jit(solution)/shard_map/pallas_call | solution.py:38
  76.0 1.0 %collective-permute-done.27.refs_1_ = bf16[256,1024]{1,0:T(8,128)(2,1)S(1)} collective-permute-done((bf16[256,1024]{1,0:T(8,128)(2,1)S(1)}, bf16[256,1024]{1,0:T(8,128)(2,1)S(1)}, u32[]{:S(2)}, u32[]{:S(2)}) %collective-permute-start.27) | collective-permute-done | bytes 524320 | tf_op jit(solution)/shard_map/ppermute | solution.py:437
  77.0 1.5 %shard_map.125 = f32[512,1024]{1,0:T(8,128)} custom-call(bf16[256,1024]{1,0:T(8,128)(2,1)S(1)} %shard_map.124.refs_0_, bf16[256,1024]{1,0:T(8,128)(2,1)S(1)} %collective-permute-done.27.refs_1_), custom_call_target="tpu_custom_call" | custom-call | flops 1048576 | bytes 4194304 | tf_op jit(solution)/shard_map/pallas_call | solution.py:38
  (26 shorter events, 0.2 us)
Async XLA Ops:
  2.1 9.8 %collective-permute-start.2 = (bf16[896,256]{1,0:T(8,128)(2,1)S(1)}, bf16[896,256]{1,0:T(8,128)(2,1)S(1)}, u32[]{:S(2)}, u32[]{:S(2)}) collective-permute-start(bf16[896,256]{1,0:T(8,128)(2,1)S(1)} %get-tuple-element.46), channel_id=1, source_target_pairs={{0,1},{1,0},{2,3},{3,2},{4,5},{5,4},{6,7},{7,6},{8,9},{9,8},{10,11... | collective-permute-start | bytes 1376264 | tf_op jit(solution)/shard_map/ppermute | solution.py:437
  2.6 6.9 %collective-permute-start.3 = (bf16[256,256]{1,0:T(8,128)(2,1)S(1)}, bf16[256,256]{1,0:T(8,128)(2,1)S(1)}, u32[]{:S(2)}, u32[]{:S(2)}) collective-permute-start(bf16[256,256]{1,0:T(8,128)(2,1)S(1)} %get-tuple-element.47), channel_id=1, source_target_pairs={{0,2},{1,3},{2,0},{3,1},{4,6},{5,7},{6,4},{7,5},{8,10},{9,11},{10,... | collective-permute-start | bytes 393224 | tf_op jit(solution)/shard_map/ppermute | solution.py:437
  5.2 6.6 %collective-permute-start.4 = (bf16[256,256]{1,0:T(8,128)(2,1)S(1)}, bf16[256,256]{1,0:T(8,128)(2,1)S(1)}, u32[]{:S(2)}, u32[]{:S(2)}) collective-permute-start(bf16[256,256]{1,0:T(8,128)(2,1)S(1)} %get-tuple-element.48), channel_id=1, source_target_pairs={{0,3},{1,2},{2,1},{3,0},{4,7},{5,6},{6,5},{7,4},{8,11},{9,10},{10,... | collective-permute-start | bytes 393224 | tf_op jit(solution)/shard_map/ppermute | solution.py:437
  5.3 6.6 %collective-permute-start.7 = (bf16[256,256]{1,0:T(8,128)(2,1)S(1)}, bf16[256,256]{1,0:T(8,128)(2,1)S(1)}, u32[]{:S(2)}, u32[]{:S(2)}) collective-permute-start(bf16[256,256]{1,0:T(8,128)(2,1)S(1)} %shard_map.112), channel_id=1, source_target_pairs={{0,4},{1,5},{2,6},{3,7},{4,0},{5,1},{6,2},{7,3},{8,12},{9,13},{10,... | collective-permute-start | bytes 393224 | tf_op jit(solution)/shard_map/ppermute | solution.py:440
  7.1 4.8 %collective-permute-start.8 = (bf16[256,256]{1,0:T(8,128)(2,1)S(1)}, bf16[256,256]{1,0:T(8,128)(2,1)S(1)}, u32[]{:S(2)}, u32[]{:S(2)}) collective-permute-start(bf16[256,256]{1,0:T(8,128)(2,1)S(1)} %shard_map.112), channel_id=1, source_target_pairs={{4,8},{5,9},{6,10},{7,11},{8,4},{9,5},{10,6},{11,7},{20,24},{21,25... | collective-permute-start | bytes 393224 | tf_op jit(solution)/shard_map/ppermute | solution.py:447
  9.5 13.4 %collective-permute-start = (bf16[256,1024]{1,0:T(8,128)(2,1)S(1)}, bf16[256,1024]{1,0:T(8,128)(2,1)S(1)}, u32[]{:S(2)}, u32[]{:S(2)}) collective-permute-start(bf16[256,1024]{1,0:T(8,128)(2,1)S(1)} %get-tuple-element.43.refs_1_), channel_id=1, source_target_pairs={{0,16},{16,0},{1,17},{17,1},{2,18},{18,2},{3,19},{19,3},{4,20},{20... | collective-permute-start | bytes 1572872 | tf_op jit(solution)/shard_map/ppermute | solution.py:485
  11.9 16.7 %collective-permute-start.10 = (bf16[768,256]{1,0:T(8,128)(2,1)S(1)}, bf16[768,256]{1,0:T(8,128)(2,1)S(1)}, u32[]{:S(2)}, u32[]{:S(2)}) collective-permute-start(bf16[768,256]{1,0:T(8,128)(2,1)S(1)} %shard_map.113), channel_id=1, source_target_pairs={{4,8},{5,9},{6,10},{7,11},{8,4},{9,5},{10,6},{11,7},{20,24},{21,25... | collective-permute-start | bytes 1179656 | tf_op jit(solution)/shard_map/ppermute | solution.py:447
  12.6 16.0 %collective-permute-start.9 = (bf16[768,256]{1,0:T(8,128)(2,1)S(1)}, bf16[768,256]{1,0:T(8,128)(2,1)S(1)}, u32[]{:S(2)}, u32[]{:S(2)}) collective-permute-start(bf16[768,256]{1,0:T(8,128)(2,1)S(1)} %shard_map.113), channel_id=1, source_target_pairs={{0,4},{1,5},{2,6},{3,7},{4,0},{5,1},{6,2},{7,3},{8,12},{9,13},{10,... | collective-permute-start | bytes 1179656 | tf_op jit(solution)/shard_map/ppermute | solution.py:440
  19.6 9.0 %collective-permute-start.5 = (bf16[640,256]{1,0:T(8,128)(2,1)S(1)}, bf16[640,256]{1,0:T(8,128)(2,1)S(1)}, u32[]{:S(2)}, u32[]{:S(2)}) collective-permute-start(bf16[640,256]{1,0:T(8,128)(2,1)S(1)} %get-tuple-element.52), channel_id=1, source_target_pairs={{0,2},{1,3},{2,0},{3,1},{4,6},{5,7},{6,4},{7,5},{8,10},{9,11},{10,... | collective-permute-start | bytes 983048 | tf_op jit(solution)/shard_map/ppermute | solution.py:437
  21.1 7.5 %collective-permute-start.6 = (bf16[128,256]{1,0:T(8,128)(2,1)S(1)}, bf16[128,256]{1,0:T(8,128)(2,1)S(1)}, u32[]{:S(2)}, u32[]{:S(2)}) collective-permute-start(bf16[128,256]{1,0:T(8,128)(2,1)S(1)} %get-tuple-element.53.refs_3_), channel_id=1, source_target_pairs={{0,3},{1,2},{2,1},{3,0},{4,7},{5,6},{6,5},{7,4},{8,11},{9,10},{10,... | collective-permute-start | bytes 196616 | tf_op jit(solution)/shard_map/ppermute | solution.py:437
  23.0 15.6 %collective-permute-start.1 = (bf16[256,1024]{1,0:T(8,128)(2,1)S(1)}, bf16[256,1024]{1,0:T(8,128)(2,1)S(1)}, u32[]{:S(2)}, u32[]{:S(2)}) collective-permute-start(bf16[256,1024]{1,0:T(8,128)(2,1)S(1)} %collective-permute-done.refs_2_.refs_1_), channel_id=1, source_target_pairs={{0,1},{1,0},{2,3},{3,2},{4,5},{5,4},{6,7},{7,6},{8,9},{9,8},{10,11... | collective-permute-start | bytes 1572872 | tf_op jit(solution)/shard_map/ppermute | solution.py:437
  28.6 4.4 %collective-permute-start.11 = (bf16[640,256]{1,0:T(8,128)(2,1)S(1)}, bf16[640,256]{1,0:T(8,128)(2,1)S(1)}, u32[]{:S(2)}, u32[]{:S(2)}) collective-permute-start(bf16[640,256]{1,0:T(8,128)(2,1)S(1)} %collective-permute-done.5.refs_6_.refs_5_), channel_id=1, source_target_pairs={{0,1},{1,0},{2,3},{3,2},{4,5},{5,4},{6,7},{7,6},{8,9},{9,8},{10,11... | collective-permute-start | bytes 983048 | tf_op jit(solution)/shard_map/ppermute | solution.py:437
  34.1 12.6 %collective-permute-start.12 = (bf16[64,1024]{1,0:T(8,128)(2,1)S(1)}, bf16[64,1024]{1,0:T(8,128)(2,1)S(1)}, u32[]{:S(2)}, u32[]{:S(2)}) collective-permute-start(bf16[64,1024]{1,0:T(8,128)(2,1)S(1)} %get-tuple-element.64), channel_id=1, source_target_pairs={{0,4},{1,5},{2,6},{3,7},{4,0},{5,1},{6,2},{7,3},{8,12},{9,13},{10,... | collective-permute-start | bytes 393224 | tf_op jit(solution)/shard_map/ppermute | solution.py:440
  35.1 13.2 %collective-permute-start.17 = (bf16[64,1024]{1,0:T(8,128)(2,1)S(1)}, bf16[64,1024]{1,0:T(8,128)(2,1)S(1)}, u32[]{:S(2)}, u32[]{:S(2)}) collective-permute-start(bf16[64,1024]{1,0:T(8,128)(2,1)S(1)} %get-tuple-element.72), channel_id=1, source_target_pairs={{0,8},{1,9},{2,10},{3,11},{4,12},{5,13},{6,14},{7,15},{8,0},{9,1},... | collective-permute-start | bytes 393224 | tf_op jit(solution)/shard_map/ppermute | solution.py:440
  36.2 12.1 %collective-permute-start.18 = (bf16[64,1024]{1,0:T(8,128)(2,1)S(1)}, bf16[64,1024]{1,0:T(8,128)(2,1)S(1)}, u32[]{:S(2)}, u32[]{:S(2)}) collective-permute-start(bf16[64,1024]{1,0:T(8,128)(2,1)S(1)} %get-tuple-element.73), channel_id=1, source_target_pairs={{0,12},{1,13},{2,14},{3,15},{4,8},{5,9},{6,10},{7,11},{8,4},{9,5},... | collective-permute-start | bytes 393224 | tf_op jit(solution)/shard_map/ppermute | solution.py:440
  45.8 19.3 %collective-permute-start.15 = (bf16[1024,256]{1,0:T(8,128)(2,1)S(1)}, bf16[1024,256]{1,0:T(8,128)(2,1)S(1)}, u32[]{:S(2)}, u32[]{:S(2)}) collective-permute-start(bf16[1024,256]{1,0:T(8,128)(2,1)S(1)} %get-tuple-element.69), channel_id=1, source_target_pairs={{0,4},{1,5},{2,6},{3,7},{4,0},{5,1},{6,2},{7,3},{8,12},{9,13},{10,... | collective-permute-start | bytes 1572872 | tf_op jit(solution)/shard_map/ppermute | solution.py:440
  46.0 19.2 %collective-permute-start.16 = (bf16[1024,256]{1,0:T(8,128)(2,1)S(1)}, bf16[1024,256]{1,0:T(8,128)(2,1)S(1)}, u32[]{:S(2)}, u32[]{:S(2)}) collective-permute-start(bf16[1024,256]{1,0:T(8,128)(2,1)S(1)} %get-tuple-element.70), channel_id=1, source_target_pairs={{4,8},{5,9},{6,10},{7,11},{8,4},{9,5},{10,6},{11,7},{20,24},{21,25... | collective-permute-start | bytes 1572872 | tf_op jit(solution)/shard_map/ppermute | solution.py:447
  46.7 12.6 %collective-permute-start.13 = (bf16[512,256]{1,0:T(8,128)(2,1)S(1)}, bf16[512,256]{1,0:T(8,128)(2,1)S(1)}, u32[]{:S(2)}, u32[]{:S(2)}) collective-permute-start(bf16[512,256]{1,0:T(8,128)(2,1)S(1)} %shard_map.117), channel_id=1, source_target_pairs={{0,2},{1,3},{2,0},{3,1},{4,6},{5,7},{6,4},{7,5},{8,10},{9,11},{10,... | collective-permute-start | bytes 786440 | tf_op jit(solution)/shard_map/ppermute | solution.py:437
  48.4 10.9 %collective-permute-start.19 = (bf16[64,1024]{1,0:T(8,128)(2,1)S(1)}, bf16[64,1024]{1,0:T(8,128)(2,1)S(1)}, u32[]{:S(2)}, u32[]{:S(2)}) collective-permute-start(bf16[64,1024]{1,0:T(8,128)(2,1)S(1)} %shard_map.120.refs_0_), channel_id=1, source_target_pairs={{0,2},{1,3},{2,18},{3,19},{4,6},{5,7},{6,22},{7,23},{8,10},{9,11},... | collective-permute-start | bytes 393224 | tf_op jit(solution)/shard_map/ppermute | solution.py:549
  49.5 9.8 %collective-permute-start.20 = (bf16[64,1024]{1,0:T(8,128)(2,1)S(1)}, bf16[64,1024]{1,0:T(8,128)(2,1)S(1)}, u32[]{:S(2)}, u32[]{:S(2)}) collective-permute-start(bf16[64,1024]{1,0:T(8,128)(2,1)S(1)} %shard_map.120.refs_0_), channel_id=1, source_target_pairs={{2,16},{3,17},{6,20},{7,21},{10,24},{11,25},{14,28},{15,29},{16,2}... | collective-permute-start | bytes 393224 | tf_op jit(solution)/shard_map/ppermute | solution.py:550
  59.3 7.3 %collective-permute-start.24 = (bf16[64,1024]{1,0:T(8,128)(2,1)S(1)}, bf16[64,1024]{1,0:T(8,128)(2,1)S(1)}, u32[]{:S(2)}, u32[]{:S(2)}) collective-permute-start(bf16[64,1024]{1,0:T(8,128)(2,1)S(1)} %shard_map.121.refs_3_.refs_0_), channel_id=1, source_target_pairs={{0,4},{1,5},{2,6},{3,7},{4,0},{5,1},{6,2},{7,3},{8,12},{9,13},{10,... | collective-permute-start | bytes 393224 | tf_op jit(solution)/shard_map/ppermute | solution.py:440
  62.7 11.2 %collective-permute-start.25 = (bf16[64,1024]{1,0:T(8,128)(2,1)S(1)}, bf16[64,1024]{1,0:T(8,128)(2,1)S(1)}, u32[]{:S(2)}, u32[]{:S(2)}) collective-permute-start(bf16[64,1024]{1,0:T(8,128)(2,1)S(1)} %shard_map.121.refs_3_.refs_0_), channel_id=1, source_target_pairs={{0,8},{1,9},{2,10},{3,11},{4,12},{5,13},{6,14},{7,15},{8,0},{9,1},... | collective-permute-start | bytes 393224 | tf_op jit(solution)/shard_map/ppermute | solution.py:440
  63.6 10.3 %collective-permute-start.26 = (bf16[64,1024]{1,0:T(8,128)(2,1)S(1)}, bf16[64,1024]{1,0:T(8,128)(2,1)S(1)}, u32[]{:S(2)}, u32[]{:S(2)}) collective-permute-start(bf16[64,1024]{1,0:T(8,128)(2,1)S(1)} %shard_map.121.refs_3_.refs_0_), channel_id=1, source_target_pairs={{0,12},{1,13},{2,14},{3,15},{4,8},{5,9},{6,10},{7,11},{8,4},{9,5},... | collective-permute-start | bytes 393224 | tf_op jit(solution)/shard_map/ppermute | solution.py:440
  65.1 4.0 %collective-permute-start.14 = (bf16[512,256]{1,0:T(8,128)(2,1)S(1)}, bf16[512,256]{1,0:T(8,128)(2,1)S(1)}, u32[]{:S(2)}, u32[]{:S(2)}) collective-permute-start(bf16[512,256]{1,0:T(8,128)(2,1)S(1)} %shard_map.118), channel_id=1, source_target_pairs={{0,1},{1,0},{2,3},{3,2},{4,5},{5,4},{6,7},{7,6},{8,9},{9,8},{10,11... | collective-permute-start | bytes 786440 | tf_op jit(solution)/shard_map/ppermute | solution.py:437
  65.2 3.9 %copy-start = (bf16[512,1024]{1,0:T(8,128)(2,1)S(1)}, bf16[512,1024]{1,0:T(8,128)(2,1)}, u32[]{:S(2)}) copy-start(bf16[512,1024]{1,0:T(8,128)(2,1)} %refs_0_.3) | copy-start | bytes 3145732
  65.4 8.5 %collective-permute-start.21 = (bf16[256,256]{1,0:T(8,128)(2,1)S(1)}, bf16[256,256]{1,0:T(8,128)(2,1)S(1)}, u32[]{:S(2)}, u32[]{:S(2)}) collective-permute-start(bf16[256,256]{1,0:T(8,128)(2,1)S(1)} %get-tuple-element.75), channel_id=1, source_target_pairs={{0,1},{1,0},{2,3},{3,2},{4,5},{5,4},{6,7},{7,6},{8,9},{9,8},{10,11... | collective-permute-start | bytes 393224 | tf_op jit(solution)/shard_map/ppermute | solution.py:437
  66.6 7.3 %collective-permute-start.22 = (bf16[256,256]{1,0:T(8,128)(2,1)S(1)}, bf16[256,256]{1,0:T(8,128)(2,1)S(1)}, u32[]{:S(2)}, u32[]{:S(2)}) collective-permute-start(bf16[256,256]{1,0:T(8,128)(2,1)S(1)} %get-tuple-element.76), channel_id=1, source_target_pairs={{0,2},{1,3},{2,0},{3,1},{4,6},{5,7},{6,4},{7,5},{8,10},{9,11},{10,... | collective-permute-start | bytes 393224 | tf_op jit(solution)/shard_map/ppermute | solution.py:437
  69.1 5.9 %collective-permute-start.23 = (bf16[256,256]{1,0:T(8,128)(2,1)S(1)}, bf16[256,256]{1,0:T(8,128)(2,1)S(1)}, u32[]{:S(2)}, u32[]{:S(2)}) collective-permute-start(bf16[256,256]{1,0:T(8,128)(2,1)S(1)} %get-tuple-element.77), channel_id=1, source_target_pairs={{0,3},{1,2},{2,1},{3,0},{4,7},{5,6},{6,5},{7,4},{8,11},{9,10},{10,... | collective-permute-start | bytes 393224 | tf_op jit(solution)/shard_map/ppermute | solution.py:437
  75.0 2.0 %collective-permute-start.27 = (bf16[256,1024]{1,0:T(8,128)(2,1)S(1)}, bf16[256,1024]{1,0:T(8,128)(2,1)S(1)}, u32[]{:S(2)}, u32[]{:S(2)}) collective-permute-start(bf16[256,1024]{1,0:T(8,128)(2,1)S(1)} %shard_map.124.refs_0_), channel_id=1, source_target_pairs={{0,1},{1,0},{2,3},{3,2},{4,5},{5,4},{6,7},{7,6},{8,9},{9,8},{10,11... | collective-permute-start | bytes 1572872 | tf_op jit(solution)/shard_map/ppermute | solution.py:437

commit v5 on v4

--- a/solution.py
+++ b/solution.py
@@ -179,7 +179,7 @@
     own_rest = refs[group]
     far_rest = refs[group + 1 : 2 * group - 1]
     sides = refs[2 * group - 1 : 2 * group + 3]
-    keys, vals, keys_t, queries, att_t, att, stats, vals_t = refs[2 * group + 3 :]
+    keys, vals, keys_t, queries, att_t, att, stats, att_far, vals_t = refs[2 * group + 3 :]
     rows, cols = far_rest[-1].shape
     plane = group * rows
     span = rows + 2 * WINDOW
@@ -233,6 +233,9 @@
         stats[unit, 1:2, :] = share
         prob = (power * share).astype(BF16)
     mix(count - 1, prob)
+    for m in range(2, group):
+        taken = pl.ds(pl.multiple_of((inner ^ m) * rows, 128), rows)
+        att_far[(m - 2) * rows : (m - 1) * rows, :] = att[taken, :]
 
 
 def middle_kernel(group, fast, att_t, near, far, *refs):
@@ -277,7 +280,7 @@
 
 
 def backward_kernel(
-    group, limits, keys, vals, keys_t, queries, grad_att, stats, att,
+    group, limits, keys, vals, keys_t, queries, grad_att, stats,
     to_first, own, to_second, *refs,
 ):
     mine, near, far, key_sum, value_sum, grad_query = refs
@@ -322,10 +325,9 @@
         grad_score = (prob * (grad_prob - centre) * HEAD_DIM ** (-0.5)).astype(BF16)
         behind = (query, grad, prob.astype(BF16), grad_score)
     end(count - 1, *behind)
-    for m, (target, base) in enumerate(((mine, 0), (near, 0), (far, 0), (far, 2 * rows))):
+    for m, (target, base) in enumerate(((mine, 0), (near, 0), (far, 0), (far, rows))):
         taken = pl.ds(pl.multiple_of((inner ^ m) * rows, 128), rows)
         target[base : base + rows, :] = grad_query[taken, :]
-        target[base + rows : base + 2 * rows, :] = att[taken, :]
     even = 1 - lax.rem(place // group, 2)
     for target, side in ((to_first, 2 * even), (own, 1), (to_second, 2 - 2 * even)):
         kept = pl.ds(pl.multiple_of(side * plane, 128), plane)
@@ -345,10 +347,13 @@
             pieces[m][part * rows : (part + 1) * rows, :] = summed.astype(BF16)
 
 
-def relay_kernel(near, far, out):
-    size = near.shape[0]
-    out[0:size, :] = near[...]
-    out[size : 2 * size, :] = far[size : 2 * size, :]
+def relay_kernel(group, near, far, att, att_far, out):
+    rows = near.shape[0]
+    inner = lax.rem(lax.axis_index("seq"), group)
+    out[0:rows, :] = near[...]
+    out[rows : 2 * rows, :] = far[rows : 2 * rows, :]
+    out[2 * rows : 3 * rows, :] = att[pl.ds(pl.multiple_of((inner ^ 1) * rows, 128), rows), :]
+    out[3 * rows : 4 * rows, :] = att_far[rows : 2 * rows, :]
 
 
 def unpack_kernel(group, *refs):
@@ -362,18 +367,25 @@
             outs[part][:, at] = pieces[m][part * rows : (part + 1) * rows, :]
 
 
-def project_kernel(group, fast, near, far, farther, mine, early, relayed, grad_query, out, done, att):
+def project_kernel(
+    group, fast, near, far, farther, mine, early, att_mine, att_early, relayed,
+    grad_query, out, done, att,
+):
     rows, width = out.shape
     cols = width // group
     half = width // 2
     inner = lax.rem(lax.axis_index("seq"), group)
     first = lax.axis_index("doc") if fast else 0
-    held = ((mine, 0), (relayed, 0), (early, 0), (relayed, 2 * rows))
+    own = pl.ds(pl.multiple_of(inner * rows, 128), rows)
+    held = (
+        (mine[...], att_mine[own, :]),
+        (relayed[0:rows, :], relayed[2 * rows : 3 * rows, :]),
+        (early[0:rows, :], att_early[0:rows, :]),
+        (relayed[rows : 2 * rows, :], relayed[3 * rows : 4 * rows, :]),
+    )
     for m in range(group):
         at = pl.ds(pl.multiple_of((inner ^ m) * cols, 128), cols)
-        source, base = held[m]
-        grad_query[:, at] = source[base : base + rows, :]
-        att[:, at] = source[base + rows : base + 2 * rows, :]
+        grad_query[:, at], att[:, at] = held[m]
     total = dot_nn(att[:, pl.ds(pl.multiple_of(first * half, 128), half)], near[...])
     for side, weight in ((0, far), (1, farther)):
         start = (1 - first) * half + (lax.rem(inner, 2) ^ side) * cols
@@ -492,15 +504,16 @@
         near = far = chunks[0]
         half_near, half_far = whole[: width // 2], chunks[1:]
 
-    keys, vals, keys_t, query_all, att_t, att, stats = call(
+    keys, vals, keys_t, query_all, att_t, att, stats, att_far = call(
         functools.partial(forward_kernel, group),
         [((3 * plane, cols), BF16)] * 2
         + [((cols, 3 * plane), BF16), ((plane, cols), BF16), ((cols, plane), BF16)]
-        + [((plane, cols), BF16), ((units, 8, 2 * rows), F32)],
+        + [((plane, cols), BF16), ((units, 8, 2 * rows), F32), ((2 * rows, cols), BF16)],
         (limits, own_kv, near_all, *far_kv, own_rest, *far_rest, *sides),
         scratch=[pltpu.VMEM((cols, 3 * plane), BF16)],
         flops=4 << 30, moved=4 << 20, vmem=32,
     )
+    att_early = inner_swap(att_far, 2)
     middle_out = (
         [((cols // outer_count, width), BF16)] * outer_count if fast else [((cols, width), F32)]
     )
@@ -519,9 +532,9 @@
     to_first, own, to_second, early_own, early_near, early_far = call(
         functools.partial(backward_kernel, group),
         [((2 * plane, cols), BF16), ((2 * plane, cols), F32), ((2 * plane, cols), BF16)]
-        + [((2 * rows, cols), BF16)] * 2
-        + [((4 * rows, cols), BF16)],
-        (limits, keys, vals, keys_t, query_all, grad_att, stats, att),
+        + [((rows, cols), BF16)] * 2
+        + [((2 * rows, cols), BF16)],
+        (limits, keys, vals, keys_t, query_all, grad_att, stats),
         after=half_far[1:],
         scratch=[pltpu.VMEM((3 * plane, cols), F32)] * 2 + [pltpu.VMEM((plane, cols), BF16)],
         flops=8 << 30, moved=4 << 20, vmem=32,
@@ -565,14 +578,15 @@
         early = inner_swap(early_far, 2)
 
     (relayed,) = call(
-        relay_kernel, [((4 * rows, cols), BF16)], (early_near, early),
+        functools.partial(relay_kernel, group), [((4 * rows, cols), BF16)],
+        (early_near, early, att, att_early),
         after=(), flops=1 << 18, moved=1 << 20,
     )
     relayed = inner_swap(relayed, 1)
     grad_query, layer_out, projected = call(
         functools.partial(project_kernel, group, fast),
         [((rows, width), BF16)] * 2 + [((8, 128), F32)],
-        (half_near, *half_far, early_own, early, relayed),
+        (half_near, *half_far, early_own, early, att, att_early, relayed),
         scratch=[pltpu.VMEM((rows, width), BF16)],
         flops=1 << 30, moved=4 << 20,
     )

time: 78.7 us -> 77.8 us (0.989)
  waiting for transfers between devices: 25 us -> 20.7 us
  starting transfers between devices: 34.5 us -> 37.9 us
    ppermute x1, waiting for transfers between devices: 9.1 us -> 0.35 us  [body(): got_first = lax.ppermute(line, ('doc', 'seq'), first_pairs)]
    ppermute x13 -> x14, starting transfers between devices: 9.55 us -> 13.2 us  [inner_swap(): return lax.ppermute(value, 'seq', [(i, i ^ m) for i in range(seq_count)])]
    ppermute x13 -> x14, waiting for transfers between devices: 9.81 us -> 12.2 us  [inner_swap(): return lax.ppermute(value, 'seq', [(i, i ^ m) for i in range(seq_count)])]
    ppermute x9, waiting for transfers between devices: 4.27 us -> 6.36 us  [outer_swap(): lax.ppermute(value, 'seq', [(i, i ^ m * group) for i in range(seq_count)])]
  transfers between devices with their start and end apart: 28 -> 29, of which waited for: 9 -> 12; matrix products, arithmetic and copies ran while one was open for 0% -> 0% of each run, Pallas kernels for 19% -> 20%
where the time goes in v5:
time: 77.8 us; the launch traced here: 77.5 us
  starting transfers between devices  37.9 us (49%)
  waiting for transfers between devices  20.7 us (27%)
  Pallas kernels  18.1 us (23%)
  between operations  0.85 us (1%)
    ppermute x9, starting transfers between devices, outer_swap(): lax.ppermute(value, 'seq', [(i, i ^ m * group) for i in range(seq_count)])  18.5 us
    pallas_call x16, Pallas kernels, call(): pl.pallas_call(run, out_shape=outs, in_specs=[HBM] * hbm + [VMEM] * (coun...  18.1 us
    ppermute x14, starting transfers between devices, inner_swap(): return lax.ppermute(value, 'seq', [(i, i ^ m) for i in range(seq_count)])  13.2 us
    ppermute x14, waiting for transfers between devices, inner_swap(): return lax.ppermute(value, 'seq', [(i, i ^ m) for i in range(seq_count)])  12.2 us
    ppermute x9, waiting for transfers between devices, outer_swap(): lax.ppermute(value, 'seq', [(i, i ^ m * group) for i in range(seq_count)])  6.36 us
    ppermute x3, starting transfers between devices, outer_second(): lax.ppermute(value, 'seq', [(a, b) for a, b in pairs_of if 0 <= b < seq_c...  2.03 us
    ppermute x1, starting transfers between devices, body(): far = lax.ppermute(near, 'doc', [(0, 1), (1, 0)])  1.92 us
    ppermute x1, waiting for transfers between devices, body(): far = lax.ppermute(near, 'doc', [(0, 1), (1, 0)])  1.8 us
  transfers between devices with their start and end apart: 29, of which 12 were waited for; matrix products, arithmetic and copies ran while one was open for 0% of the time, Pallas kernels for 20%

profile of v5, /device:TPU:0, one launch (start us, length us, event | category | flops | bytes accessed | tf_op | source)
XLA Modules:
  0.0 77.5 jit_solution(14258150855969907498)
XLA Ops:
  0.6 1.4 %shard_map.110 = (bf16[256,256]{1,0:T(8,128)(2,1)S(1)}, bf16[256,256]{1,0:T(8,128)(2,1)S(1)}, bf16[256,256]{1,0:T(8,128)(2,1)S(1)}, bf16[640,256]{1,0:T(8,128)(2...) custom-call(s32[1,4]{1,0:T(1,128)} %refs_0_.2, ...), custom_call_target="tpu_custom_call" | custom-call | flops 1048576 | bytes 4194304 | tf_op jit(solution)/shard_map/pallas_call | solution.py:38
  2.1 0.5 collective-permute-start.2
  2.6 2.6 %collective-permute-start.3 = (bf16[256,256]{1,0:T(8,128)(2,1)S(1)}, bf16[256,256]{1,0:T(8,128)(2,1)S(1)}, u32[]{:S(2)}, u32[]{:S(2)}) collective-permute-start(bf16[256,256]{1,0:T(8,128)(2,1)S(1)} %get-tuple-element.48), channel_id=1, source_target_pairs={{0,2},{1,3},{2,0},{3,1},{4,6},{5,7},{6,4},{7,5},{8,10},{9,11},{10,... | collective-permute-start | bytes 393224 | tf_op jit(solution)/shard_map/ppermute | solution.py:449
  5.2 0.1 collective-permute-start.4
  5.3 1.8 %collective-permute-start.7 = (bf16[256,256]{1,0:T(8,128)(2,1)S(1)}, bf16[256,256]{1,0:T(8,128)(2,1)S(1)}, u32[]{:S(2)}, u32[]{:S(2)}) collective-permute-start(bf16[256,256]{1,0:T(8,128)(2,1)S(1)} %shard_map.112), channel_id=1, source_target_pairs={{0,4},{1,5},{2,6},{3,7},{4,0},{5,1},{6,2},{7,3},{8,12},{9,13},{10,... | collective-permute-start | bytes 393224 | tf_op jit(solution)/shard_map/ppermute | solution.py:452
  7.1 0.7 collective-permute-start.8
  7.8 1.8 %collective-permute-done.3.refs_3_.refs_1_ = bf16[256,256]{1,0:T(8,128)(2,1)S(1)} collective-permute-done((bf16[256,256]{1,0:T(8,128)(2,1)S(1)}, bf16[256,256]{1,0:T(8,128)(2,1)S(1)}, u32[]{:S(2)}, u32[]{:S(2)}) %collective-permute-start.3) | collective-permute-done | bytes 131104 | tf_op jit(solution)/shard_map/ppermute | solution.py:449
  9.5 1.9 %collective-permute-start = (bf16[256,1024]{1,0:T(8,128)(2,1)S(1)}, bf16[256,1024]{1,0:T(8,128)(2,1)S(1)}, u32[]{:S(2)}, u32[]{:S(2)}) collective-permute-start(bf16[256,1024]{1,0:T(8,128)(2,1)S(1)} %get-tuple-element.44.refs_1_), channel_id=1, source_target_pairs={{0,16},{16,0},{1,17},{17,1},{2,18},{18,2},{3,19},{19,3},{4,20},{20... | collective-permute-start | bytes 1572872 | tf_op jit(solution)/shard_map/ppermute | solution.py:497
  11.5 0.4 collective-permute-done.4.refs_4_.refs_2_
  11.9 0.7 collective-permute-start.10
  12.6 7.0 %collective-permute-start.9 = (bf16[768,256]{1,0:T(8,128)(2,1)S(1)}, bf16[768,256]{1,0:T(8,128)(2,1)S(1)}, u32[]{:S(2)}, u32[]{:S(2)}) collective-permute-start(bf16[768,256]{1,0:T(8,128)(2,1)S(1)} %shard_map.113), channel_id=1, source_target_pairs={{0,4},{1,5},{2,6},{3,7},{4,0},{5,1},{6,2},{7,3},{8,12},{9,13},{10,... | collective-permute-start | bytes 1179656 | tf_op jit(solution)/shard_map/ppermute | solution.py:452
  19.6 1.5 %collective-permute-start.5 = (bf16[640,256]{1,0:T(8,128)(2,1)S(1)}, bf16[640,256]{1,0:T(8,128)(2,1)S(1)}, u32[]{:S(2)}, u32[]{:S(2)}) collective-permute-start(bf16[640,256]{1,0:T(8,128)(2,1)S(1)} %get-tuple-element.53), channel_id=1, source_target_pairs={{0,2},{1,3},{2,0},{3,1},{4,6},{5,7},{6,4},{7,5},{8,10},{9,11},{10,... | collective-permute-start | bytes 983048 | tf_op jit(solution)/shard_map/ppermute | solution.py:449
  21.2 1.8 %collective-permute-done.refs_2_.refs_1_ = bf16[256,1024]{1,0:T(8,128)(2,1)S(1)} collective-permute-done((bf16[256,1024]{1,0:T(8,128)(2,1)S(1)}, bf16[256,1024]{1,0:T(8,128)(2,1)S(1)}, u32[]{:S(2)}, u32[]{:S(2)}) %collective-permute-start) | collective-permute-done | bytes 524320 | tf_op jit(solution)/shard_map/ppermute | solution.py:497
  23.0 5.6 %collective-permute-done.5.refs_6_.refs_5_ = bf16[640,256]{1,0:T(8,128)(2,1)S(1)} collective-permute-done((bf16[640,256]{1,0:T(8,128)(2,1)S(1)}, bf16[640,256]{1,0:T(8,128)(2,1)S(1)}, u32[]{:S(2)}, u32[]{:S(2)}) %collective-permute-start.5) | collective-permute-done | bytes 327712 | tf_op jit(solution)/shard_map/ppermute | solution.py:449
  28.6 4.3 %shard_map.114 = (bf16[1536,256]{1,0:T(8,128)(2,1)S(1)}, bf16[1536,256]{1,0:T(8,128)(2,1)S(1)}, bf16[256,1536]{1,0:T(8,128)(2,1)S(1)}, bf16[512,256]{1,0:T(8,128...) custom-call(s32[8,512]{1,0:T(8,128)S(1)} %get-tuple-element.45.refs_, ...), custom_call_target="tpu_custom_call" | custom-call | flops 4294967296 | bytes 4194304 | tf_op jit(solution)/shard_map/pallas_call | solution.py:38
  33.0 1.1 %shard_map.115 = (bf16[512,256]{1,0:T(8,128)(2,1)S(1)}, bf16[64,1024]{1,0:T(8,128)(2,1)S(1)}, bf16[64,1024]{1,0:T(8,128)(2,1)S(1)}, bf16[64,1024]{1,0:T(8,128)(2,1)S(1)}, bf16[64,1024]{1,0:T(8,128)(2,1)S(1)}) custom-call(bf16[256,512]{1,0:T(8,128)(2,1)S(1)} %get-tuple-element.59.refs_0_, bf16[256,1024]{1,0:T(8,128)(2,1)S(1)} %get-tuple-element.44.refs_1_, ...), custom_call_target="tpu_custom_call" | custom-call | flops 1073741824 | bytes 4194304 | tf_op jit(solution)/shard_map/pallas_call | solution.py:38
  34.1 1.0 %collective-permute-start.12 = (bf16[64,1024]{1,0:T(8,128)(2,1)S(1)}, bf16[64,1024]{1,0:T(8,128)(2,1)S(1)}, u32[]{:S(2)}, u32[]{:S(2)}) collective-permute-start(bf16[64,1024]{1,0:T(8,128)(2,1)S(1)} %get-tuple-element.64), channel_id=1, source_target_pairs={{0,4},{1,5},{2,6},{3,7},{4,0},{5,1},{6,2},{7,3},{8,12},{9,13},{10,... | collective-permute-start | bytes 393224 | tf_op jit(solution)/shard_map/ppermute | solution.py:452
  35.1 1.1 %collective-permute-start.18 = (bf16[64,1024]{1,0:T(8,128)(2,1)S(1)}, bf16[64,1024]{1,0:T(8,128)(2,1)S(1)}, u32[]{:S(2)}, u32[]{:S(2)}) collective-permute-start(bf16[64,1024]{1,0:T(8,128)(2,1)S(1)} %get-tuple-element.74), channel_id=1, source_target_pairs={{0,8},{1,9},{2,10},{3,11},{4,12},{5,13},{6,14},{7,15},{8,0},{9,1},... | collective-permute-start | bytes 393224 | tf_op jit(solution)/shard_map/ppermute | solution.py:452
  36.2 2.3 %collective-permute-start.19 = (bf16[64,1024]{1,0:T(8,128)(2,1)S(1)}, bf16[64,1024]{1,0:T(8,128)(2,1)S(1)}, u32[]{:S(2)}, u32[]{:S(2)}) collective-permute-start(bf16[64,1024]{1,0:T(8,128)(2,1)S(1)} %get-tuple-element.75), channel_id=1, source_target_pairs={{0,12},{1,13},{2,14},{3,15},{4,8},{5,9},{6,10},{7,11},{8,4},{9,5},... | collective-permute-start | bytes 393224 | tf_op jit(solution)/shard_map/ppermute | solution.py:452
  38.5 7.3 %shard_map.116 = (bf16[1024,256]{1,0:T(8,128)(2,1)S(1)}, f32[1024,256]{1,0:T(8,128)S(1)}, bf16[1024,256]{1,0:T(8,128)(2,1)S(1)}, bf16[128,256]{1,0:T(8,128)(2,1)...) custom-call(s32[8,512]{1,0:T(8,128)S(1)} %get-tuple-element.45.refs_0_, ...), custom_call_target="tpu_custom_call" | custom-call | flops 8589934592 | bytes 4194304 | tf_op jit(solution)/shard_map/pallas_call | solution.py:38
  45.9 0.1 collective-permute-start.16
  46.0 0.7 collective-permute-start.17
  46.7 1.2 %collective-permute-done.18.refs_2_ = bf16[64,1024]{1,0:T(8,128)(2,1)S(1)} collective-permute-done((bf16[64,1024]{1,0:T(8,128)(2,1)S(1)}, bf16[64,1024]{1,0:T(8,128)(2,1)S(1)}, u32[]{:S(2)}, u32[]{:S(2)}) %collective-permute-start.18) | collective-permute-done | bytes 131104 | tf_op jit(solution)/shard_map/ppermute | solution.py:452
  47.9 0.1 shard_map.120.refs_0_
  48.0 1.6 %collective-permute-start.20 = (bf16[64,1024]{1,0:T(8,128)(2,1)S(1)}, bf16[64,1024]{1,0:T(8,128)(2,1)S(1)}, u32[]{:S(2)}, u32[]{:S(2)}) collective-permute-start(bf16[64,1024]{1,0:T(8,128)(2,1)S(1)} %shard_map.120.refs_0_), channel_id=1, source_target_pairs={{0,2},{1,3},{2,18},{3,19},{4,6},{5,7},{6,22},{7,23},{8,10},{9,11},... | collective-permute-start | bytes 393224 | tf_op jit(solution)/shard_map/ppermute | solution.py:562
  49.6 0.7 collective-permute-start.21
  50.2 3.3 %collective-permute-start.13 = (bf16[256,256]{1,0:T(8,128)(2,1)S(1)}, bf16[256,256]{1,0:T(8,128)(2,1)S(1)}, u32[]{:S(2)}, u32[]{:S(2)}) collective-permute-start(bf16[256,256]{1,0:T(8,128)(2,1)S(1)} %shard_map.117), channel_id=1, source_target_pairs={{0,2},{1,3},{2,0},{3,1},{4,6},{5,7},{6,4},{7,5},{8,10},{9,11},{10,... | collective-permute-start | bytes 393224 | tf_op jit(solution)/shard_map/ppermute | solution.py:449
  53.5 0.4 collective-permute-done.20.refs_1_
  53.9 2.6 %collective-permute-start.14 = (bf16[256,256]{1,0:T(8,128)(2,1)S(1)}, bf16[256,256]{1,0:T(8,128)(2,1)S(1)}, u32[]{:S(2)}, u32[]{:S(2)}) collective-permute-start(bf16[256,256]{1,0:T(8,128)(2,1)S(1)} %get-tuple-element.66), channel_id=1, source_target_pairs={{0,2},{1,3},{2,0},{3,1},{4,6},{5,7},{6,4},{7,5},{8,10},{9,11},{10,... | collective-permute-start | bytes 393224 | tf_op jit(solution)/shard_map/ppermute | solution.py:449
  56.5 2.4 %collective-permute-done.13.refs_1_.refs_4_.refs_3_ = bf16[256,256]{1,0:T(8,128)(2,1)S(1)} collective-permute-done((bf16[256,256]{1,0:T(8,128)(2,1)S(1)}, bf16[256,256]{1,0:T(8,128)(2,1)S(1)}, u32[]{:S(2)}, u32[]{:S(2)}) %collective-permute-start.13) | collective-permute-done | bytes 131104 | tf_op jit(solution)/shard_map/ppermute | solution.py:449
  58.9 2.6 %collective-permute-start.25 = (bf16[64,1024]{1,0:T(8,128)(2,1)S(1)}, bf16[64,1024]{1,0:T(8,128)(2,1)S(1)}, u32[]{:S(2)}, u32[]{:S(2)}) collective-permute-start(bf16[64,1024]{1,0:T(8,128)(2,1)S(1)} %shard_map.121.refs_3_.refs_0_), channel_id=1, source_target_pairs={{0,4},{1,5},{2,6},{3,7},{4,0},{5,1},{6,2},{7,3},{8,12},{9,13},{10,... | collective-permute-start | bytes 393224 | tf_op jit(solution)/shard_map/ppermute | solution.py:452
  61.6 1.0 %collective-permute-start.26 = (bf16[64,1024]{1,0:T(8,128)(2,1)S(1)}, bf16[64,1024]{1,0:T(8,128)(2,1)S(1)}, u32[]{:S(2)}, u32[]{:S(2)}) collective-permute-start(bf16[64,1024]{1,0:T(8,128)(2,1)S(1)} %shard_map.121.refs_3_.refs_0_), channel_id=1, source_target_pairs={{0,8},{1,9},{2,10},{3,11},{4,12},{5,13},{6,14},{7,15},{8,0},{9,1},... | collective-permute-start | bytes 393224 | tf_op jit(solution)/shard_map/ppermute | solution.py:452
  62.5 1.5 %collective-permute-start.27 = (bf16[64,1024]{1,0:T(8,128)(2,1)S(1)}, bf16[64,1024]{1,0:T(8,128)(2,1)S(1)}, u32[]{:S(2)}, u32[]{:S(2)}) collective-permute-start(bf16[64,1024]{1,0:T(8,128)(2,1)S(1)} %shard_map.121.refs_3_.refs_0_), channel_id=1, source_target_pairs={{0,12},{1,13},{2,14},{3,15},{4,8},{5,9},{6,10},{7,11},{8,4},{9,5},... | collective-permute-start | bytes 393224 | tf_op jit(solution)/shard_map/ppermute | solution.py:452
  64.0 0.1 collective-permute-start.15
  64.1 0.0 copy-start
  64.1 0.2 shard_map.122
  64.3 0.5 collective-permute-start.22
  64.8 2.0 %collective-permute-done.25.refs_1_ = bf16[64,1024]{1,0:T(8,128)(2,1)S(1)} collective-permute-done((bf16[64,1024]{1,0:T(8,128)(2,1)S(1)}, bf16[64,1024]{1,0:T(8,128)(2,1)S(1)}, u32[]{:S(2)}, u32[]{:S(2)}) %collective-permute-start.25) | collective-permute-done | bytes 131104 | tf_op jit(solution)/shard_map/ppermute | solution.py:452
  66.8 0.9 %collective-permute-start.23 = (bf16[256,256]{1,0:T(8,128)(2,1)S(1)}, bf16[256,256]{1,0:T(8,128)(2,1)S(1)}, u32[]{:S(2)}, u32[]{:S(2)}) collective-permute-start(bf16[256,256]{1,0:T(8,128)(2,1)S(1)} %get-tuple-element.78), channel_id=1, source_target_pairs={{0,2},{1,3},{2,0},{3,1},{4,6},{5,7},{6,4},{7,5},{8,10},{9,11},{10,... | collective-permute-start | bytes 393224 | tf_op jit(solution)/shard_map/ppermute | solution.py:449
  67.8 0.1 collective-permute-start.24
  67.9 1.2 %shard_map.119 = (bf16[128,1024]{1,0:T(8,128)(2,1)}, bf16[128,1024]{1,0:T(8,128)(2,1)}, f32[8,128]{1,0:T(8,128)S(1)}) custom-call(bf16[512,1024]{1,0:T(8,128)(2,1)S(1)} %copy-done, bf16[256,1024]{1,0:T(8,128)(2,1)S(1)} %collective-permute-done.refs_2_.refs_1_, bf16[256,1024]{1,0:T(8,128)(2,1)S(1)} %collective-permute-done.1.refs_7_.refs_2_, ...), custom_call_target="tpu_custom_call" | custom-call | flops 1073741824 | bytes 4194304 | tf_op jit(solution)/shard_map/pallas_call | solution.py:38
  69.1 3.1 %collective-permute-done.26.refs_2_ = bf16[64,1024]{1,0:T(8,128)(2,1)S(1)} collective-permute-done((bf16[64,1024]{1,0:T(8,128)(2,1)S(1)}, bf16[64,1024]{1,0:T(8,128)(2,1)S(1)}, u32[]{:S(2)}, u32[]{:S(2)}) %collective-permute-start.26) | collective-permute-done | bytes 131104 | tf_op jit(solution)/shard_map/ppermute | solution.py:452
  72.2 0.7 collective-permute-done.23.refs_2_.refs_5_
  72.9 0.6 collective-permute-done.24.refs_3_.refs_6_
  73.5 1.0 %collective-permute-start.28 = (bf16[256,1024]{1,0:T(8,128)(2,1)S(1)}, bf16[256,1024]{1,0:T(8,128)(2,1)S(1)}, u32[]{:S(2)}, u32[]{:S(2)}) collective-permute-start(bf16[256,1024]{1,0:T(8,128)(2,1)S(1)} %shard_map.124.refs_0_), channel_id=1, source_target_pairs={{0,1},{1,0},{2,3},{3,2},{4,5},{5,4},{6,7},{7,6},{8,9},{9,8},{10,11... | collective-permute-start | bytes 1572872 | tf_op jit(solution)/shard_map/ppermute | solution.py:449
  74.5 0.8 %shard_map.123 = (bf16[128,1024]{1,0:T(8,128)(2,1)}, bf16[128,1024]{1,0:T(8,128)(2,1)}) custom-call(bf16[256,256]{1,0:T(8,128)(2,1)S(1)} %get-tuple-element.76.refs_0_, bf16[256,256]{1,0:T(8,128)(2,1)S(1)} %collective-permute-done.22.refs_1_.refs_4_, bf16[256,256]{1,0:T(8,128)(2,1)S(1)} %collective-permute-done.23.refs_2_.refs_5_, ...), custom_call_target="tpu_custom_call" | custom-call | flops 1048576 | bytes 1048576 | tf_op jit(solution)/shard_map/pallas_call | solution.py:38
  75.4 0.7 collective-permute-done.28.refs_1_
  76.1 1.5 %shard_map.125 = f32[512,1024]{1,0:T(8,128)} custom-call(bf16[256,1024]{1,0:T(8,128)(2,1)S(1)} %shard_map.124.refs_0_, bf16[256,1024]{1,0:T(8,128)(2,1)S(1)} %collective-permute-done.28.refs_1_), custom_call_target="tpu_custom_call" | custom-call | flops 1048576 | bytes 4194304 | tf_op jit(solution)/shard_map/pallas_call | solution.py:38
  (28 shorter events, 0.2 us)
Async XLA Ops:
  2.1 9.8 %collective-permute-start.2 = (bf16[896,256]{1,0:T(8,128)(2,1)S(1)}, bf16[896,256]{1,0:T(8,128)(2,1)S(1)}, u32[]{:S(2)}, u32[]{:S(2)}) collective-permute-start(bf16[896,256]{1,0:T(8,128)(2,1)S(1)} %get-tuple-element.47), channel_id=1, source_target_pairs={{0,1},{1,0},{2,3},{3,2},{4,5},{5,4},{6,7},{7,6},{8,9},{9,8},{10,11... | collective-permute-start | bytes 1376264 | tf_op jit(solution)/shard_map/ppermute | solution.py:449
  2.6 6.9 %collective-permute-start.3 = (bf16[256,256]{1,0:T(8,128)(2,1)S(1)}, bf16[256,256]{1,0:T(8,128)(2,1)S(1)}, u32[]{:S(2)}, u32[]{:S(2)}) collective-permute-start(bf16[256,256]{1,0:T(8,128)(2,1)S(1)} %get-tuple-element.48), channel_id=1, source_target_pairs={{0,2},{1,3},{2,0},{3,1},{4,6},{5,7},{6,4},{7,5},{8,10},{9,11},{10,... | collective-permute-start | bytes 393224 | tf_op jit(solution)/shard_map/ppermute | solution.py:449
  5.2 6.6 %collective-permute-start.4 = (bf16[256,256]{1,0:T(8,128)(2,1)S(1)}, bf16[256,256]{1,0:T(8,128)(2,1)S(1)}, u32[]{:S(2)}, u32[]{:S(2)}) collective-permute-start(bf16[256,256]{1,0:T(8,128)(2,1)S(1)} %get-tuple-element.49), channel_id=1, source_target_pairs={{0,3},{1,2},{2,1},{3,0},{4,7},{5,6},{6,5},{7,4},{8,11},{9,10},{10,... | collective-permute-start | bytes 393224 | tf_op jit(solution)/shard_map/ppermute | solution.py:449
  5.3 6.6 %collective-permute-start.7 = (bf16[256,256]{1,0:T(8,128)(2,1)S(1)}, bf16[256,256]{1,0:T(8,128)(2,1)S(1)}, u32[]{:S(2)}, u32[]{:S(2)}) collective-permute-start(bf16[256,256]{1,0:T(8,128)(2,1)S(1)} %shard_map.112), channel_id=1, source_target_pairs={{0,4},{1,5},{2,6},{3,7},{4,0},{5,1},{6,2},{7,3},{8,12},{9,13},{10,... | collective-permute-start | bytes 393224 | tf_op jit(solution)/shard_map/ppermute | solution.py:452
  7.1 4.8 %collective-permute-start.8 = (bf16[256,256]{1,0:T(8,128)(2,1)S(1)}, bf16[256,256]{1,0:T(8,128)(2,1)S(1)}, u32[]{:S(2)}, u32[]{:S(2)}) collective-permute-start(bf16[256,256]{1,0:T(8,128)(2,1)S(1)} %shard_map.112), channel_id=1, source_target_pairs={{4,8},{5,9},{6,10},{7,11},{8,4},{9,5},{10,6},{11,7},{20,24},{21,25... | collective-permute-start | bytes 393224 | tf_op jit(solution)/shard_map/ppermute | solution.py:459
  9.5 13.4 %collective-permute-start = (bf16[256,1024]{1,0:T(8,128)(2,1)S(1)}, bf16[256,1024]{1,0:T(8,128)(2,1)S(1)}, u32[]{:S(2)}, u32[]{:S(2)}) collective-permute-start(bf16[256,1024]{1,0:T(8,128)(2,1)S(1)} %get-tuple-element.44.refs_1_), channel_id=1, source_target_pairs={{0,16},{16,0},{1,17},{17,1},{2,18},{18,2},{3,19},{19,3},{4,20},{20... | collective-permute-start | bytes 1572872 | tf_op jit(solution)/shard_map/ppermute | solution.py:497
  11.9 16.7 %collective-permute-start.10 = (bf16[768,256]{1,0:T(8,128)(2,1)S(1)}, bf16[768,256]{1,0:T(8,128)(2,1)S(1)}, u32[]{:S(2)}, u32[]{:S(2)}) collective-permute-start(bf16[768,256]{1,0:T(8,128)(2,1)S(1)} %shard_map.113), channel_id=1, source_target_pairs={{4,8},{5,9},{6,10},{7,11},{8,4},{9,5},{10,6},{11,7},{20,24},{21,25... | collective-permute-start | bytes 1179656 | tf_op jit(solution)/shard_map/ppermute | solution.py:459
  12.6 16.0 %collective-permute-start.9 = (bf16[768,256]{1,0:T(8,128)(2,1)S(1)}, bf16[768,256]{1,0:T(8,128)(2,1)S(1)}, u32[]{:S(2)}, u32[]{:S(2)}) collective-permute-start(bf16[768,256]{1,0:T(8,128)(2,1)S(1)} %shard_map.113), channel_id=1, source_target_pairs={{0,4},{1,5},{2,6},{3,7},{4,0},{5,1},{6,2},{7,3},{8,12},{9,13},{10,... | collective-permute-start | bytes 1179656 | tf_op jit(solution)/shard_map/ppermute | solution.py:452
  19.6 9.0 %collective-permute-start.5 = (bf16[640,256]{1,0:T(8,128)(2,1)S(1)}, bf16[640,256]{1,0:T(8,128)(2,1)S(1)}, u32[]{:S(2)}, u32[]{:S(2)}) collective-permute-start(bf16[640,256]{1,0:T(8,128)(2,1)S(1)} %get-tuple-element.53), channel_id=1, source_target_pairs={{0,2},{1,3},{2,0},{3,1},{4,6},{5,7},{6,4},{7,5},{8,10},{9,11},{10,... | collective-permute-start | bytes 983048 | tf_op jit(solution)/shard_map/ppermute | solution.py:449
  21.1 7.5 %collective-permute-start.6 = (bf16[128,256]{1,0:T(8,128)(2,1)S(1)}, bf16[128,256]{1,0:T(8,128)(2,1)S(1)}, u32[]{:S(2)}, u32[]{:S(2)}) collective-permute-start(bf16[128,256]{1,0:T(8,128)(2,1)S(1)} %get-tuple-element.54.refs_3_), channel_id=1, source_target_pairs={{0,3},{1,2},{2,1},{3,0},{4,7},{5,6},{6,5},{7,4},{8,11},{9,10},{10,... | collective-permute-start | bytes 196616 | tf_op jit(solution)/shard_map/ppermute | solution.py:449
  23.0 15.6 %collective-permute-start.1 = (bf16[256,1024]{1,0:T(8,128)(2,1)S(1)}, bf16[256,1024]{1,0:T(8,128)(2,1)S(1)}, u32[]{:S(2)}, u32[]{:S(2)}) collective-permute-start(bf16[256,1024]{1,0:T(8,128)(2,1)S(1)} %collective-permute-done.refs_2_.refs_1_), channel_id=1, source_target_pairs={{0,1},{1,0},{2,3},{3,2},{4,5},{5,4},{6,7},{7,6},{8,9},{9,8},{10,11... | collective-permute-start | bytes 1572872 | tf_op jit(solution)/shard_map/ppermute | solution.py:449
  28.6 4.4 %collective-permute-start.11 = (bf16[640,256]{1,0:T(8,128)(2,1)S(1)}, bf16[640,256]{1,0:T(8,128)(2,1)S(1)}, u32[]{:S(2)}, u32[]{:S(2)}) collective-permute-start(bf16[640,256]{1,0:T(8,128)(2,1)S(1)} %collective-permute-done.5.refs_6_.refs_5_), channel_id=1, source_target_pairs={{0,1},{1,0},{2,3},{3,2},{4,5},{5,4},{6,7},{7,6},{8,9},{9,8},{10,11... | collective-permute-start | bytes 983048 | tf_op jit(solution)/shard_map/ppermute | solution.py:449
  34.1 12.6 %collective-permute-start.12 = (bf16[64,1024]{1,0:T(8,128)(2,1)S(1)}, bf16[64,1024]{1,0:T(8,128)(2,1)S(1)}, u32[]{:S(2)}, u32[]{:S(2)}) collective-permute-start(bf16[64,1024]{1,0:T(8,128)(2,1)S(1)} %get-tuple-element.64), channel_id=1, source_target_pairs={{0,4},{1,5},{2,6},{3,7},{4,0},{5,1},{6,2},{7,3},{8,12},{9,13},{10,... | collective-permute-start | bytes 393224 | tf_op jit(solution)/shard_map/ppermute | solution.py:452
  35.1 12.8 %collective-permute-start.18 = (bf16[64,1024]{1,0:T(8,128)(2,1)S(1)}, bf16[64,1024]{1,0:T(8,128)(2,1)S(1)}, u32[]{:S(2)}, u32[]{:S(2)}) collective-permute-start(bf16[64,1024]{1,0:T(8,128)(2,1)S(1)} %get-tuple-element.74), channel_id=1, source_target_pairs={{0,8},{1,9},{2,10},{3,11},{4,12},{5,13},{6,14},{7,15},{8,0},{9,1},... | collective-permute-start | bytes 393224 | tf_op jit(solution)/shard_map/ppermute | solution.py:452
  36.2 11.7 %collective-permute-start.19 = (bf16[64,1024]{1,0:T(8,128)(2,1)S(1)}, bf16[64,1024]{1,0:T(8,128)(2,1)S(1)}, u32[]{:S(2)}, u32[]{:S(2)}) collective-permute-start(bf16[64,1024]{1,0:T(8,128)(2,1)S(1)} %get-tuple-element.75), channel_id=1, source_target_pairs={{0,12},{1,13},{2,14},{3,15},{4,8},{5,9},{6,10},{7,11},{8,4},{9,5},... | collective-permute-start | bytes 393224 | tf_op jit(solution)/shard_map/ppermute | solution.py:452
  45.9 18.1 %collective-permute-start.16 = (bf16[1024,256]{1,0:T(8,128)(2,1)S(1)}, bf16[1024,256]{1,0:T(8,128)(2,1)S(1)}, u32[]{:S(2)}, u32[]{:S(2)}) collective-permute-start(bf16[1024,256]{1,0:T(8,128)(2,1)S(1)} %get-tuple-element.71), channel_id=1, source_target_pairs={{0,4},{1,5},{2,6},{3,7},{4,0},{5,1},{6,2},{7,3},{8,12},{9,13},{10,... | collective-permute-start | bytes 1572872 | tf_op jit(solution)/shard_map/ppermute | solution.py:452
  46.0 18.2 %collective-permute-start.17 = (bf16[1024,256]{1,0:T(8,128)(2,1)S(1)}, bf16[1024,256]{1,0:T(8,128)(2,1)S(1)}, u32[]{:S(2)}, u32[]{:S(2)}) collective-permute-start(bf16[1024,256]{1,0:T(8,128)(2,1)S(1)} %get-tuple-element.72), channel_id=1, source_target_pairs={{4,8},{5,9},{6,10},{7,11},{8,4},{9,5},{10,6},{11,7},{20,24},{21,25... | collective-permute-start | bytes 1572872 | tf_op jit(solution)/shard_map/ppermute | solution.py:459
  48.0 5.9 %collective-permute-start.20 = (bf16[64,1024]{1,0:T(8,128)(2,1)S(1)}, bf16[64,1024]{1,0:T(8,128)(2,1)S(1)}, u32[]{:S(2)}, u32[]{:S(2)}) collective-permute-start(bf16[64,1024]{1,0:T(8,128)(2,1)S(1)} %shard_map.120.refs_0_), channel_id=1, source_target_pairs={{0,2},{1,3},{2,18},{3,19},{4,6},{5,7},{6,22},{7,23},{8,10},{9,11},... | collective-permute-start | bytes 393224 | tf_op jit(solution)/shard_map/ppermute | solution.py:562
  49.6 6.9 %collective-permute-start.21 = (bf16[64,1024]{1,0:T(8,128)(2,1)S(1)}, bf16[64,1024]{1,0:T(8,128)(2,1)S(1)}, u32[]{:S(2)}, u32[]{:S(2)}) collective-permute-start(bf16[64,1024]{1,0:T(8,128)(2,1)S(1)} %shard_map.120.refs_0_), channel_id=1, source_target_pairs={{2,16},{3,17},{6,20},{7,21},{10,24},{11,25},{14,28},{15,29},{16,2}... | collective-permute-start | bytes 393224 | tf_op jit(solution)/shard_map/ppermute | solution.py:563
  50.2 8.6 %collective-permute-start.13 = (bf16[256,256]{1,0:T(8,128)(2,1)S(1)}, bf16[256,256]{1,0:T(8,128)(2,1)S(1)}, u32[]{:S(2)}, u32[]{:S(2)}) collective-permute-start(bf16[256,256]{1,0:T(8,128)(2,1)S(1)} %shard_map.117), channel_id=1, source_target_pairs={{0,2},{1,3},{2,0},{3,1},{4,6},{5,7},{6,4},{7,5},{8,10},{9,11},{10,... | collective-permute-start | bytes 393224 | tf_op jit(solution)/shard_map/ppermute | solution.py:449
  53.9 8.6 %collective-permute-start.14 = (bf16[256,256]{1,0:T(8,128)(2,1)S(1)}, bf16[256,256]{1,0:T(8,128)(2,1)S(1)}, u32[]{:S(2)}, u32[]{:S(2)}) collective-permute-start(bf16[256,256]{1,0:T(8,128)(2,1)S(1)} %get-tuple-element.66), channel_id=1, source_target_pairs={{0,2},{1,3},{2,0},{3,1},{4,6},{5,7},{6,4},{7,5},{8,10},{9,11},{10,... | collective-permute-start | bytes 393224 | tf_op jit(solution)/shard_map/ppermute | solution.py:449
  58.9 7.9 %collective-permute-start.25 = (bf16[64,1024]{1,0:T(8,128)(2,1)S(1)}, bf16[64,1024]{1,0:T(8,128)(2,1)S(1)}, u32[]{:S(2)}, u32[]{:S(2)}) collective-permute-start(bf16[64,1024]{1,0:T(8,128)(2,1)S(1)} %shard_map.121.refs_3_.refs_0_), channel_id=1, source_target_pairs={{0,4},{1,5},{2,6},{3,7},{4,0},{5,1},{6,2},{7,3},{8,12},{9,13},{10,... | collective-permute-start | bytes 393224 | tf_op jit(solution)/shard_map/ppermute | solution.py:452
  61.6 10.6 %collective-permute-start.26 = (bf16[64,1024]{1,0:T(8,128)(2,1)S(1)}, bf16[64,1024]{1,0:T(8,128)(2,1)S(1)}, u32[]{:S(2)}, u32[]{:S(2)}) collective-permute-start(bf16[64,1024]{1,0:T(8,128)(2,1)S(1)} %shard_map.121.refs_3_.refs_0_), channel_id=1, source_target_pairs={{0,8},{1,9},{2,10},{3,11},{4,12},{5,13},{6,14},{7,15},{8,0},{9,1},... | collective-permute-start | bytes 393224 | tf_op jit(solution)/shard_map/ppermute | solution.py:452
  62.5 9.7 %collective-permute-start.27 = (bf16[64,1024]{1,0:T(8,128)(2,1)S(1)}, bf16[64,1024]{1,0:T(8,128)(2,1)S(1)}, u32[]{:S(2)}, u32[]{:S(2)}) collective-permute-start(bf16[64,1024]{1,0:T(8,128)(2,1)S(1)} %shard_map.121.refs_3_.refs_0_), channel_id=1, source_target_pairs={{0,12},{1,13},{2,14},{3,15},{4,8},{5,9},{6,10},{7,11},{8,4},{9,5},... | collective-permute-start | bytes 393224 | tf_op jit(solution)/shard_map/ppermute | solution.py:452
  64.0 3.7 %collective-permute-start.15 = (bf16[512,256]{1,0:T(8,128)(2,1)S(1)}, bf16[512,256]{1,0:T(8,128)(2,1)S(1)}, u32[]{:S(2)}, u32[]{:S(2)}) collective-permute-start(bf16[512,256]{1,0:T(8,128)(2,1)S(1)} %shard_map.118), channel_id=1, source_target_pairs={{0,1},{1,0},{2,3},{3,2},{4,5},{5,4},{6,7},{7,6},{8,9},{9,8},{10,11... | collective-permute-start | bytes 786440 | tf_op jit(solution)/shard_map/ppermute | solution.py:449
  64.1 3.7 %copy-start = (bf16[512,1024]{1,0:T(8,128)(2,1)S(1)}, bf16[512,1024]{1,0:T(8,128)(2,1)}, u32[]{:S(2)}) copy-start(bf16[512,1024]{1,0:T(8,128)(2,1)} %refs_0_.3) | copy-start | bytes 3145732
  64.3 7.9 %collective-permute-start.22 = (bf16[256,256]{1,0:T(8,128)(2,1)S(1)}, bf16[256,256]{1,0:T(8,128)(2,1)S(1)}, u32[]{:S(2)}, u32[]{:S(2)}) collective-permute-start(bf16[256,256]{1,0:T(8,128)(2,1)S(1)} %get-tuple-element.77), channel_id=1, source_target_pairs={{0,1},{1,0},{2,3},{3,2},{4,5},{5,4},{6,7},{7,6},{8,9},{9,8},{10,11... | collective-permute-start | bytes 393224 | tf_op jit(solution)/shard_map/ppermute | solution.py:449
  66.8 6.1 %collective-permute-start.23 = (bf16[256,256]{1,0:T(8,128)(2,1)S(1)}, bf16[256,256]{1,0:T(8,128)(2,1)S(1)}, u32[]{:S(2)}, u32[]{:S(2)}) collective-permute-start(bf16[256,256]{1,0:T(8,128)(2,1)S(1)} %get-tuple-element.78), channel_id=1, source_target_pairs={{0,2},{1,3},{2,0},{3,1},{4,6},{5,7},{6,4},{7,5},{8,10},{9,11},{10,... | collective-permute-start | bytes 393224 | tf_op jit(solution)/shard_map/ppermute | solution.py:449
  67.8 5.7 %collective-permute-start.24 = (bf16[256,256]{1,0:T(8,128)(2,1)S(1)}, bf16[256,256]{1,0:T(8,128)(2,1)S(1)}, u32[]{:S(2)}, u32[]{:S(2)}) collective-permute-start(bf16[256,256]{1,0:T(8,128)(2,1)S(1)} %get-tuple-element.79), channel_id=1, source_target_pairs={{0,3},{1,2},{2,1},{3,0},{4,7},{5,6},{6,5},{7,4},{8,11},{9,10},{10,... | collective-permute-start | bytes 393224 | tf_op jit(solution)/shard_map/ppermute | solution.py:449
  73.5 2.5 %collective-permute-start.28 = (bf16[256,1024]{1,0:T(8,128)(2,1)S(1)}, bf16[256,1024]{1,0:T(8,128)(2,1)S(1)}, u32[]{:S(2)}, u32[]{:S(2)}) collective-permute-start(bf16[256,1024]{1,0:T(8,128)(2,1)S(1)} %shard_map.124.refs_0_), channel_id=1, source_target_pairs={{0,1},{1,0},{2,3},{3,2},{4,5},{5,4},{6,7},{7,6},{8,9},{9,8},{10,11... | collective-permute-start | bytes 1572872 | tf_op jit(solution)/shard_map/ppermute | solution.py:449

commit v6 on v5

--- a/solution.py
+++ b/solution.py
@@ -563,7 +563,7 @@
         got_second = lax.ppermute(line, ("doc", "seq"), second_pairs)
         early = inner_swap(early_far, 2)
         (final,) = call(
-            functools.partial(cross_kernel, group), part_shape, (line, got_first, got_second), after=(early,),
+            functools.partial(cross_kernel, group), part_shape, (line, got_first, got_second),
             flops=2 << 30, moved=1 << 19,
         )
         gathered = [final] + [outer_swap(final, m) for m in range(1, outer_count)]

time: 77.8 us -> 77.6 us (level)
    ppermute x1, waiting for transfers between devices: 0.35 us -> 4.84 us  [body(): got_first = lax.ppermute(line, ('doc', 'seq'), first_pairs)]
    ppermute x14, waiting for transfers between devices: 12.2 us -> 9.24 us  [inner_swap(): return lax.ppermute(value, 'seq', [(i, i ^ m) for i in range(seq_count)])]
    ppermute x9, waiting for transfers between devices: 6.36 us -> 4.29 us  [outer_swap(): lax.ppermute(value, 'seq', [(i, i ^ m * group) for i in range(seq_count)])]
    ppermute x9, starting transfers between devices: 18.5 us -> 19.7 us  [outer_swap(): lax.ppermute(value, 'seq', [(i, i ^ m * group) for i in range(seq_count)])]
  transfers between devices with their start and end apart: 29 -> 29, of which waited for: 12 -> 9; matrix products, arithmetic and copies ran while one was open for 0% -> 0% of each run, Pallas kernels for 20% -> 20%
where the time goes in v6:
time: 77.6 us; the launch traced here: 77.4 us
  starting transfers between devices  38.3 us (49%)
  waiting for transfers between devices  20.2 us (26%)
  Pallas kernels  18.1 us (23%)
  between operations  0.85 us (1%)
    ppermute x9, starting transfers between devices, outer_swap(): lax.ppermute(value, 'seq', [(i, i ^ m * group) for i in range(seq_count)])  19.7 us
    pallas_call x16, Pallas kernels, call(): pl.pallas_call(run, out_shape=outs, in_specs=[HBM] * hbm + [VMEM] * (coun...  18.1 us
    ppermute x14, starting transfers between devices, inner_swap(): return lax.ppermute(value, 'seq', [(i, i ^ m) for i in range(seq_count)])  12.7 us
    ppermute x14, waiting for transfers between devices, inner_swap(): return lax.ppermute(value, 'seq', [(i, i ^ m) for i in range(seq_count)])  9.24 us
    ppermute x1, waiting for transfers between devices, body(): got_first = lax.ppermute(line, ('doc', 'seq'), first_pairs)  4.84 us
    ppermute x9, waiting for transfers between devices, outer_swap(): lax.ppermute(value, 'seq', [(i, i ^ m * group) for i in range(seq_count)])  4.29 us
    ppermute x3, starting transfers between devices, outer_second(): lax.ppermute(value, 'seq', [(a, b) for a, b in pairs_of if 0 <= b < seq_c...  2.03 us
    ppermute x1, starting transfers between devices, body(): far = lax.ppermute(near, 'doc', [(0, 1), (1, 0)])  1.92 us
  transfers between devices with their start and end apart: 29, of which 9 were waited for; matrix products, arithmetic and copies ran while one was open for 0% of the time, Pallas kernels for 20%

profile of v6, /device:TPU:0, one launch (start us, length us, event | category | flops | bytes accessed | tf_op | source)
XLA Modules:
  0.0 77.4 jit_solution(15684733941095841995)
XLA Ops:
  0.6 1.4 %shard_map.110 = (bf16[256,256]{1,0:T(8,128)(2,1)S(1)}, bf16[256,256]{1,0:T(8,128)(2,1)S(1)}, bf16[256,256]{1,0:T(8,128)(2,1)S(1)}, bf16[640,256]{1,0:T(8,128)(2...) custom-call(s32[1,4]{1,0:T(1,128)} %refs_0_.2, ...), custom_call_target="tpu_custom_call" | custom-call | flops 1048576 | bytes 4194304 | tf_op jit(solution)/shard_map/pallas_call | solution.py:38
  2.1 0.5 collective-permute-start.2
  2.6 2.6 %collective-permute-start.3 = (bf16[256,256]{1,0:T(8,128)(2,1)S(1)}, bf16[256,256]{1,0:T(8,128)(2,1)S(1)}, u32[]{:S(2)}, u32[]{:S(2)}) collective-permute-start(bf16[256,256]{1,0:T(8,128)(2,1)S(1)} %get-tuple-element.48), channel_id=1, source_target_pairs={{0,2},{1,3},{2,0},{3,1},{4,6},{5,7},{6,4},{7,5},{8,10},{9,11},{10,... | collective-permute-start | bytes 393224 | tf_op jit(solution)/shard_map/ppermute | solution.py:449
  5.2 0.1 collective-permute-start.4
  5.3 1.8 %collective-permute-start.7 = (bf16[256,256]{1,0:T(8,128)(2,1)S(1)}, bf16[256,256]{1,0:T(8,128)(2,1)S(1)}, u32[]{:S(2)}, u32[]{:S(2)}) collective-permute-start(bf16[256,256]{1,0:T(8,128)(2,1)S(1)} %shard_map.112), channel_id=1, source_target_pairs={{0,4},{1,5},{2,6},{3,7},{4,0},{5,1},{6,2},{7,3},{8,12},{9,13},{10,... | collective-permute-start | bytes 393224 | tf_op jit(solution)/shard_map/ppermute | solution.py:452
  7.1 0.7 collective-permute-start.8
  7.8 1.8 %collective-permute-done.3.refs_3_.refs_1_ = bf16[256,256]{1,0:T(8,128)(2,1)S(1)} collective-permute-done((bf16[256,256]{1,0:T(8,128)(2,1)S(1)}, bf16[256,256]{1,0:T(8,128)(2,1)S(1)}, u32[]{:S(2)}, u32[]{:S(2)}) %collective-permute-start.3) | collective-permute-done | bytes 131104 | tf_op jit(solution)/shard_map/ppermute | solution.py:449
  9.5 1.9 %collective-permute-start = (bf16[256,1024]{1,0:T(8,128)(2,1)S(1)}, bf16[256,1024]{1,0:T(8,128)(2,1)S(1)}, u32[]{:S(2)}, u32[]{:S(2)}) collective-permute-start(bf16[256,1024]{1,0:T(8,128)(2,1)S(1)} %get-tuple-element.44.refs_1_), channel_id=1, source_target_pairs={{0,16},{16,0},{1,17},{17,1},{2,18},{18,2},{3,19},{19,3},{4,20},{20... | collective-permute-start | bytes 1572872 | tf_op jit(solution)/shard_map/ppermute | solution.py:497
  11.5 0.4 collective-permute-done.4.refs_4_.refs_2_
  11.8 0.0 collective-permute-done.2.refs_2_.refs_0_.refs_4_
  11.9 0.0 collective-permute-done.8.refs_5_.refs_9_
  11.9 0.7 collective-permute-start.10
  12.6 7.0 %collective-permute-start.9 = (bf16[768,256]{1,0:T(8,128)(2,1)S(1)}, bf16[768,256]{1,0:T(8,128)(2,1)S(1)}, u32[]{:S(2)}, u32[]{:S(2)}) collective-permute-start(bf16[768,256]{1,0:T(8,128)(2,1)S(1)} %shard_map.113), channel_id=1, source_target_pairs={{0,4},{1,5},{2,6},{3,7},{4,0},{5,1},{6,2},{7,3},{8,12},{9,13},{10,... | collective-permute-start | bytes 1179656 | tf_op jit(solution)/shard_map/ppermute | solution.py:452
  19.6 1.5 %collective-permute-start.5 = (bf16[640,256]{1,0:T(8,128)(2,1)S(1)}, bf16[640,256]{1,0:T(8,128)(2,1)S(1)}, u32[]{:S(2)}, u32[]{:S(2)}) collective-permute-start(bf16[640,256]{1,0:T(8,128)(2,1)S(1)} %get-tuple-element.53), channel_id=1, source_target_pairs={{0,2},{1,3},{2,0},{3,1},{4,6},{5,7},{6,4},{7,5},{8,10},{9,11},{10,... | collective-permute-start | bytes 983048 | tf_op jit(solution)/shard_map/ppermute | solution.py:449
  21.2 1.8 %collective-permute-done.refs_2_.refs_1_ = bf16[256,1024]{1,0:T(8,128)(2,1)S(1)} collective-permute-done((bf16[256,1024]{1,0:T(8,128)(2,1)S(1)}, bf16[256,1024]{1,0:T(8,128)(2,1)S(1)}, u32[]{:S(2)}, u32[]{:S(2)}) %collective-permute-start) | collective-permute-done | bytes 524320 | tf_op jit(solution)/shard_map/ppermute | solution.py:497
  23.0 5.6 %collective-permute-done.5.refs_6_.refs_5_ = bf16[640,256]{1,0:T(8,128)(2,1)S(1)} collective-permute-done((bf16[640,256]{1,0:T(8,128)(2,1)S(1)}, bf16[640,256]{1,0:T(8,128)(2,1)S(1)}, u32[]{:S(2)}, u32[]{:S(2)}) %collective-permute-start.5) | collective-permute-done | bytes 327712 | tf_op jit(solution)/shard_map/ppermute | solution.py:449
  28.6 0.0 collective-permute-done.6.refs_7_
  28.6 4.3 %shard_map.114 = (bf16[1536,256]{1,0:T(8,128)(2,1)S(1)}, bf16[1536,256]{1,0:T(8,128)(2,1)S(1)}, bf16[256,1536]{1,0:T(8,128)(2,1)S(1)}, bf16[512,256]{1,0:T(8,128...) custom-call(s32[8,512]{1,0:T(8,128)S(1)} %get-tuple-element.45.refs_, ...), custom_call_target="tpu_custom_call" | custom-call | flops 4294967296 | bytes 4194304 | tf_op jit(solution)/shard_map/pallas_call | solution.py:38
  33.0 1.1 %shard_map.115 = (bf16[512,256]{1,0:T(8,128)(2,1)S(1)}, bf16[64,1024]{1,0:T(8,128)(2,1)S(1)}, bf16[64,1024]{1,0:T(8,128)(2,1)S(1)}, bf16[64,1024]{1,0:T(8,128)(2,1)S(1)}, bf16[64,1024]{1,0:T(8,128)(2,1)S(1)}) custom-call(bf16[256,512]{1,0:T(8,128)(2,1)S(1)} %get-tuple-element.59.refs_0_, bf16[256,1024]{1,0:T(8,128)(2,1)S(1)} %get-tuple-element.44.refs_1_, ...), custom_call_target="tpu_custom_call" | custom-call | flops 1073741824 | bytes 4194304 | tf_op jit(solution)/shard_map/pallas_call | solution.py:38
  34.1 1.0 %collective-permute-start.12 = (bf16[64,1024]{1,0:T(8,128)(2,1)S(1)}, bf16[64,1024]{1,0:T(8,128)(2,1)S(1)}, u32[]{:S(2)}, u32[]{:S(2)}) collective-permute-start(bf16[64,1024]{1,0:T(8,128)(2,1)S(1)} %get-tuple-element.64), channel_id=1, source_target_pairs={{0,4},{1,5},{2,6},{3,7},{4,0},{5,1},{6,2},{7,3},{8,12},{9,13},{10,... | collective-permute-start | bytes 393224 | tf_op jit(solution)/shard_map/ppermute | solution.py:452
  35.1 1.1 %collective-permute-start.18 = (bf16[64,1024]{1,0:T(8,128)(2,1)S(1)}, bf16[64,1024]{1,0:T(8,128)(2,1)S(1)}, u32[]{:S(2)}, u32[]{:S(2)}) collective-permute-start(bf16[64,1024]{1,0:T(8,128)(2,1)S(1)} %get-tuple-element.74), channel_id=1, source_target_pairs={{0,8},{1,9},{2,10},{3,11},{4,12},{5,13},{6,14},{7,15},{8,0},{9,1},... | collective-permute-start | bytes 393224 | tf_op jit(solution)/shard_map/ppermute | solution.py:452
  36.2 2.3 %collective-permute-start.19 = (bf16[64,1024]{1,0:T(8,128)(2,1)S(1)}, bf16[64,1024]{1,0:T(8,128)(2,1)S(1)}, u32[]{:S(2)}, u32[]{:S(2)}) collective-permute-start(bf16[64,1024]{1,0:T(8,128)(2,1)S(1)} %get-tuple-element.75), channel_id=1, source_target_pairs={{0,12},{1,13},{2,14},{3,15},{4,8},{5,9},{6,10},{7,11},{8,4},{9,5},... | collective-permute-start | bytes 393224 | tf_op jit(solution)/shard_map/ppermute | solution.py:452
  38.5 7.3 %shard_map.116 = (bf16[1024,256]{1,0:T(8,128)(2,1)S(1)}, f32[1024,256]{1,0:T(8,128)S(1)}, bf16[1024,256]{1,0:T(8,128)(2,1)S(1)}, bf16[128,256]{1,0:T(8,128)(2,1)...) custom-call(s32[8,512]{1,0:T(8,128)S(1)} %get-tuple-element.45.refs_0_, ...), custom_call_target="tpu_custom_call" | custom-call | flops 8589934592 | bytes 4194304 | tf_op jit(solution)/shard_map/pallas_call | solution.py:38
  45.9 0.1 collective-permute-start.16
  46.0 0.7 collective-permute-start.17
  46.7 1.6 %collective-permute-start.14 = (bf16[256,256]{1,0:T(8,128)(2,1)S(1)}, bf16[256,256]{1,0:T(8,128)(2,1)S(1)}, u32[]{:S(2)}, u32[]{:S(2)}) collective-permute-start(bf16[256,256]{1,0:T(8,128)(2,1)S(1)} %get-tuple-element.66), channel_id=1, source_target_pairs={{0,2},{1,3},{2,0},{3,1},{4,6},{5,7},{6,4},{7,5},{8,10},{9,11},{10,... | collective-permute-start | bytes 393224 | tf_op jit(solution)/shard_map/ppermute | solution.py:449
  48.3 0.1 shard_map.120.refs_0_
  48.3 1.2 %collective-permute-start.20 = (bf16[64,1024]{1,0:T(8,128)(2,1)S(1)}, bf16[64,1024]{1,0:T(8,128)(2,1)S(1)}, u32[]{:S(2)}, u32[]{:S(2)}) collective-permute-start(bf16[64,1024]{1,0:T(8,128)(2,1)S(1)} %shard_map.120.refs_0_), channel_id=1, source_target_pairs={{0,2},{1,3},{2,18},{3,19},{4,6},{5,7},{6,22},{7,23},{8,10},{9,11},... | collective-permute-start | bytes 393224 | tf_op jit(solution)/shard_map/ppermute | solution.py:562
  49.6 0.7 collective-permute-start.21
  50.2 4.8 %collective-permute-done.20.refs_1_ = bf16[64,1024]{1,0:T(8,128)(2,1)S(1)} collective-permute-done((bf16[64,1024]{1,0:T(8,128)(2,1)S(1)}, bf16[64,1024]{1,0:T(8,128)(2,1)S(1)}, u32[]{:S(2)}, u32[]{:S(2)}) %collective-permute-start.20) | collective-permute-done | bytes 131104 | tf_op jit(solution)/shard_map/ppermute | solution.py:562
  55.1 3.9 %collective-permute-start.13 = (bf16[256,256]{1,0:T(8,128)(2,1)S(1)}, bf16[256,256]{1,0:T(8,128)(2,1)S(1)}, u32[]{:S(2)}, u32[]{:S(2)}) collective-permute-start(bf16[256,256]{1,0:T(8,128)(2,1)S(1)} %shard_map.117), channel_id=1, source_target_pairs={{0,2},{1,3},{2,0},{3,1},{4,6},{5,7},{6,4},{7,5},{8,10},{9,11},{10,... | collective-permute-start | bytes 393224 | tf_op jit(solution)/shard_map/ppermute | solution.py:449
  59.0 3.9 %collective-permute-start.25 = (bf16[64,1024]{1,0:T(8,128)(2,1)S(1)}, bf16[64,1024]{1,0:T(8,128)(2,1)S(1)}, u32[]{:S(2)}, u32[]{:S(2)}) collective-permute-start(bf16[64,1024]{1,0:T(8,128)(2,1)S(1)} %shard_map.121.refs_3_.refs_0_), channel_id=1, source_target_pairs={{0,4},{1,5},{2,6},{3,7},{4,0},{5,1},{6,2},{7,3},{8,12},{9,13},{10,... | collective-permute-start | bytes 393224 | tf_op jit(solution)/shard_map/ppermute | solution.py:452
  62.9 0.9 %collective-permute-start.26 = (bf16[64,1024]{1,0:T(8,128)(2,1)S(1)}, bf16[64,1024]{1,0:T(8,128)(2,1)S(1)}, u32[]{:S(2)}, u32[]{:S(2)}) collective-permute-start(bf16[64,1024]{1,0:T(8,128)(2,1)S(1)} %shard_map.121.refs_3_.refs_0_), channel_id=1, source_target_pairs={{0,8},{1,9},{2,10},{3,11},{4,12},{5,13},{6,14},{7,15},{8,0},{9,1},... | collective-permute-start | bytes 393224 | tf_op jit(solution)/shard_map/ppermute | solution.py:452
  63.8 1.5 %collective-permute-start.27 = (bf16[64,1024]{1,0:T(8,128)(2,1)S(1)}, bf16[64,1024]{1,0:T(8,128)(2,1)S(1)}, u32[]{:S(2)}, u32[]{:S(2)}) collective-permute-start(bf16[64,1024]{1,0:T(8,128)(2,1)S(1)} %shard_map.121.refs_3_.refs_0_), channel_id=1, source_target_pairs={{0,12},{1,13},{2,14},{3,15},{4,8},{5,9},{6,10},{7,11},{8,4},{9,5},... | collective-permute-start | bytes 393224 | tf_op jit(solution)/shard_map/ppermute | solution.py:452
  65.4 0.1 collective-permute-start.15
  65.4 0.0 copy-start
  65.5 0.2 shard_map.122
  65.6 0.5 collective-permute-start.22
  66.2 0.8 collective-permute-done.25.refs_1_
  66.9 0.0 collective-permute-done.15.refs_7_
  67.0 0.6 collective-permute-start.24
  67.6 1.2 %shard_map.119 = (bf16[128,1024]{1,0:T(8,128)(2,1)}, bf16[128,1024]{1,0:T(8,128)(2,1)}, f32[8,128]{1,0:T(8,128)S(1)}) custom-call(bf16[512,1024]{1,0:T(8,128)(2,1)S(1)} %copy-done, bf16[256,1024]{1,0:T(8,128)(2,1)S(1)} %collective-permute-done.refs_2_.refs_1_, bf16[256,1024]{1,0:T(8,128)(2,1)S(1)} %collective-permute-done.1.refs_7_.refs_2_, ...), custom_call_target="tpu_custom_call" | custom-call | flops 1073741824 | bytes 4194304 | tf_op jit(solution)/shard_map/pallas_call | solution.py:38
  68.8 3.5 %collective-permute-done.26.refs_2_ = bf16[64,1024]{1,0:T(8,128)(2,1)S(1)} collective-permute-done((bf16[64,1024]{1,0:T(8,128)(2,1)S(1)}, bf16[64,1024]{1,0:T(8,128)(2,1)S(1)}, u32[]{:S(2)}, u32[]{:S(2)}) %collective-permute-start.26) | collective-permute-done | bytes 131104 | tf_op jit(solution)/shard_map/ppermute | solution.py:452
  72.3 0.7 collective-permute-done.23.refs_2_.refs_5_
  73.1 1.3 %collective-permute-start.28 = (bf16[256,1024]{1,0:T(8,128)(2,1)S(1)}, bf16[256,1024]{1,0:T(8,128)(2,1)S(1)}, u32[]{:S(2)}, u32[]{:S(2)}) collective-permute-start(bf16[256,1024]{1,0:T(8,128)(2,1)S(1)} %shard_map.124.refs_0_), channel_id=1, source_target_pairs={{0,1},{1,0},{2,3},{3,2},{4,5},{5,4},{6,7},{7,6},{8,9},{9,8},{10,11... | collective-permute-start | bytes 1572872 | tf_op jit(solution)/shard_map/ppermute | solution.py:449
  74.4 0.8 %shard_map.123 = (bf16[128,1024]{1,0:T(8,128)(2,1)}, bf16[128,1024]{1,0:T(8,128)(2,1)}) custom-call(bf16[256,256]{1,0:T(8,128)(2,1)S(1)} %get-tuple-element.76.refs_0_, bf16[256,256]{1,0:T(8,128)(2,1)S(1)} %collective-permute-done.22.refs_1_.refs_4_, bf16[256,256]{1,0:T(8,128)(2,1)S(1)} %collective-permute-done.23.refs_2_.refs_5_, ...), custom_call_target="tpu_custom_call" | custom-call | flops 1048576 | bytes 1048576 | tf_op jit(solution)/shard_map/pallas_call | solution.py:38
  75.2 0.7 collective-permute-done.28.refs_1_
  75.9 1.5 %shard_map.125 = f32[512,1024]{1,0:T(8,128)} custom-call(bf16[256,1024]{1,0:T(8,128)(2,1)S(1)} %shard_map.124.refs_0_, bf16[256,1024]{1,0:T(8,128)(2,1)S(1)} %collective-permute-done.28.refs_1_), custom_call_target="tpu_custom_call" | custom-call | flops 1048576 | bytes 4194304 | tf_op jit(solution)/shard_map/pallas_call | solution.py:38
  (28 shorter events, 0.2 us)
Async XLA Ops:
  2.1 9.8 %collective-permute-start.2 = (bf16[896,256]{1,0:T(8,128)(2,1)S(1)}, bf16[896,256]{1,0:T(8,128)(2,1)S(1)}, u32[]{:S(2)}, u32[]{:S(2)}) collective-permute-start(bf16[896,256]{1,0:T(8,128)(2,1)S(1)} %get-tuple-element.47), channel_id=1, source_target_pairs={{0,1},{1,0},{2,3},{3,2},{4,5},{5,4},{6,7},{7,6},{8,9},{9,8},{10,11... | collective-permute-start | bytes 1376264 | tf_op jit(solution)/shard_map/ppermute | solution.py:449
  2.6 6.9 %collective-permute-start.3 = (bf16[256,256]{1,0:T(8,128)(2,1)S(1)}, bf16[256,256]{1,0:T(8,128)(2,1)S(1)}, u32[]{:S(2)}, u32[]{:S(2)}) collective-permute-start(bf16[256,256]{1,0:T(8,128)(2,1)S(1)} %get-tuple-element.48), channel_id=1, source_target_pairs={{0,2},{1,3},{2,0},{3,1},{4,6},{5,7},{6,4},{7,5},{8,10},{9,11},{10,... | collective-permute-start | bytes 393224 | tf_op jit(solution)/shard_map/ppermute | solution.py:449
  5.2 6.6 %collective-permute-start.4 = (bf16[256,256]{1,0:T(8,128)(2,1)S(1)}, bf16[256,256]{1,0:T(8,128)(2,1)S(1)}, u32[]{:S(2)}, u32[]{:S(2)}) collective-permute-start(bf16[256,256]{1,0:T(8,128)(2,1)S(1)} %get-tuple-element.49), channel_id=1, source_target_pairs={{0,3},{1,2},{2,1},{3,0},{4,7},{5,6},{6,5},{7,4},{8,11},{9,10},{10,... | collective-permute-start | bytes 393224 | tf_op jit(solution)/shard_map/ppermute | solution.py:449
  5.3 6.6 %collective-permute-start.7 = (bf16[256,256]{1,0:T(8,128)(2,1)S(1)}, bf16[256,256]{1,0:T(8,128)(2,1)S(1)}, u32[]{:S(2)}, u32[]{:S(2)}) collective-permute-start(bf16[256,256]{1,0:T(8,128)(2,1)S(1)} %shard_map.112), channel_id=1, source_target_pairs={{0,4},{1,5},{2,6},{3,7},{4,0},{5,1},{6,2},{7,3},{8,12},{9,13},{10,... | collective-permute-start | bytes 393224 | tf_op jit(solution)/shard_map/ppermute | solution.py:452
  7.1 4.8 %collective-permute-start.8 = (bf16[256,256]{1,0:T(8,128)(2,1)S(1)}, bf16[256,256]{1,0:T(8,128)(2,1)S(1)}, u32[]{:S(2)}, u32[]{:S(2)}) collective-permute-start(bf16[256,256]{1,0:T(8,128)(2,1)S(1)} %shard_map.112), channel_id=1, source_target_pairs={{4,8},{5,9},{6,10},{7,11},{8,4},{9,5},{10,6},{11,7},{20,24},{21,25... | collective-permute-start | bytes 393224 | tf_op jit(solution)/shard_map/ppermute | solution.py:459
  9.5 13.4 %collective-permute-start = (bf16[256,1024]{1,0:T(8,128)(2,1)S(1)}, bf16[256,1024]{1,0:T(8,128)(2,1)S(1)}, u32[]{:S(2)}, u32[]{:S(2)}) collective-permute-start(bf16[256,1024]{1,0:T(8,128)(2,1)S(1)} %get-tuple-element.44.refs_1_), channel_id=1, source_target_pairs={{0,16},{16,0},{1,17},{17,1},{2,18},{18,2},{3,19},{19,3},{4,20},{20... | collective-permute-start | bytes 1572872 | tf_op jit(solution)/shard_map/ppermute | solution.py:497
  11.9 16.7 %collective-permute-start.10 = (bf16[768,256]{1,0:T(8,128)(2,1)S(1)}, bf16[768,256]{1,0:T(8,128)(2,1)S(1)}, u32[]{:S(2)}, u32[]{:S(2)}) collective-permute-start(bf16[768,256]{1,0:T(8,128)(2,1)S(1)} %shard_map.113), channel_id=1, source_target_pairs={{4,8},{5,9},{6,10},{7,11},{8,4},{9,5},{10,6},{11,7},{20,24},{21,25... | collective-permute-start | bytes 1179656 | tf_op jit(solution)/shard_map/ppermute | solution.py:459
  12.6 16.0 %collective-permute-start.9 = (bf16[768,256]{1,0:T(8,128)(2,1)S(1)}, bf16[768,256]{1,0:T(8,128)(2,1)S(1)}, u32[]{:S(2)}, u32[]{:S(2)}) collective-permute-start(bf16[768,256]{1,0:T(8,128)(2,1)S(1)} %shard_map.113), channel_id=1, source_target_pairs={{0,4},{1,5},{2,6},{3,7},{4,0},{5,1},{6,2},{7,3},{8,12},{9,13},{10,... | collective-permute-start | bytes 1179656 | tf_op jit(solution)/shard_map/ppermute | solution.py:452
  19.6 9.0 %collective-permute-start.5 = (bf16[640,256]{1,0:T(8,128)(2,1)S(1)}, bf16[640,256]{1,0:T(8,128)(2,1)S(1)}, u32[]{:S(2)}, u32[]{:S(2)}) collective-permute-start(bf16[640,256]{1,0:T(8,128)(2,1)S(1)} %get-tuple-element.53), channel_id=1, source_target_pairs={{0,2},{1,3},{2,0},{3,1},{4,6},{5,7},{6,4},{7,5},{8,10},{9,11},{10,... | collective-permute-start | bytes 983048 | tf_op jit(solution)/shard_map/ppermute | solution.py:449
  21.1 7.5 %collective-permute-start.6 = (bf16[128,256]{1,0:T(8,128)(2,1)S(1)}, bf16[128,256]{1,0:T(8,128)(2,1)S(1)}, u32[]{:S(2)}, u32[]{:S(2)}) collective-permute-start(bf16[128,256]{1,0:T(8,128)(2,1)S(1)} %get-tuple-element.54.refs_3_), channel_id=1, source_target_pairs={{0,3},{1,2},{2,1},{3,0},{4,7},{5,6},{6,5},{7,4},{8,11},{9,10},{10,... | collective-permute-start | bytes 196616 | tf_op jit(solution)/shard_map/ppermute | solution.py:449
  23.0 15.6 %collective-permute-start.1 = (bf16[256,1024]{1,0:T(8,128)(2,1)S(1)}, bf16[256,1024]{1,0:T(8,128)(2,1)S(1)}, u32[]{:S(2)}, u32[]{:S(2)}) collective-permute-start(bf16[256,1024]{1,0:T(8,128)(2,1)S(1)} %collective-permute-done.refs_2_.refs_1_), channel_id=1, source_target_pairs={{0,1},{1,0},{2,3},{3,2},{4,5},{5,4},{6,7},{7,6},{8,9},{9,8},{10,11... | collective-permute-start | bytes 1572872 | tf_op jit(solution)/shard_map/ppermute | solution.py:449
  28.6 4.4 %collective-permute-start.11 = (bf16[640,256]{1,0:T(8,128)(2,1)S(1)}, bf16[640,256]{1,0:T(8,128)(2,1)S(1)}, u32[]{:S(2)}, u32[]{:S(2)}) collective-permute-start(bf16[640,256]{1,0:T(8,128)(2,1)S(1)} %collective-permute-done.5.refs_6_.refs_5_), channel_id=1, source_target_pairs={{0,1},{1,0},{2,3},{3,2},{4,5},{5,4},{6,7},{7,6},{8,9},{9,8},{10,11... | collective-permute-start | bytes 983048 | tf_op jit(solution)/shard_map/ppermute | solution.py:449
  34.1 12.6 %collective-permute-start.12 = (bf16[64,1024]{1,0:T(8,128)(2,1)S(1)}, bf16[64,1024]{1,0:T(8,128)(2,1)S(1)}, u32[]{:S(2)}, u32[]{:S(2)}) collective-permute-start(bf16[64,1024]{1,0:T(8,128)(2,1)S(1)} %get-tuple-element.64), channel_id=1, source_target_pairs={{0,4},{1,5},{2,6},{3,7},{4,0},{5,1},{6,2},{7,3},{8,12},{9,13},{10,... | collective-permute-start | bytes 393224 | tf_op jit(solution)/shard_map/ppermute | solution.py:452
  35.1 13.2 %collective-permute-start.18 = (bf16[64,1024]{1,0:T(8,128)(2,1)S(1)}, bf16[64,1024]{1,0:T(8,128)(2,1)S(1)}, u32[]{:S(2)}, u32[]{:S(2)}) collective-permute-start(bf16[64,1024]{1,0:T(8,128)(2,1)S(1)} %get-tuple-element.74), channel_id=1, source_target_pairs={{0,8},{1,9},{2,10},{3,11},{4,12},{5,13},{6,14},{7,15},{8,0},{9,1},... | collective-permute-start | bytes 393224 | tf_op jit(solution)/shard_map/ppermute | solution.py:452
  36.2 12.1 %collective-permute-start.19 = (bf16[64,1024]{1,0:T(8,128)(2,1)S(1)}, bf16[64,1024]{1,0:T(8,128)(2,1)S(1)}, u32[]{:S(2)}, u32[]{:S(2)}) collective-permute-start(bf16[64,1024]{1,0:T(8,128)(2,1)S(1)} %get-tuple-element.75), channel_id=1, source_target_pairs={{0,12},{1,13},{2,14},{3,15},{4,8},{5,9},{6,10},{7,11},{8,4},{9,5},... | collective-permute-start | bytes 393224 | tf_op jit(solution)/shard_map/ppermute | solution.py:452
  45.9 19.5 %collective-permute-start.16 = (bf16[1024,256]{1,0:T(8,128)(2,1)S(1)}, bf16[1024,256]{1,0:T(8,128)(2,1)S(1)}, u32[]{:S(2)}, u32[]{:S(2)}) collective-permute-start(bf16[1024,256]{1,0:T(8,128)(2,1)S(1)} %get-tuple-element.71), channel_id=1, source_target_pairs={{0,4},{1,5},{2,6},{3,7},{4,0},{5,1},{6,2},{7,3},{8,12},{9,13},{10,... | collective-permute-start | bytes 1572872 | tf_op jit(solution)/shard_map/ppermute | solution.py:452
  46.0 19.5 %collective-permute-start.17 = (bf16[1024,256]{1,0:T(8,128)(2,1)S(1)}, bf16[1024,256]{1,0:T(8,128)(2,1)S(1)}, u32[]{:S(2)}, u32[]{:S(2)}) collective-permute-start(bf16[1024,256]{1,0:T(8,128)(2,1)S(1)} %get-tuple-element.72), channel_id=1, source_target_pairs={{4,8},{5,9},{6,10},{7,11},{8,4},{9,5},{10,6},{11,7},{20,24},{21,25... | collective-permute-start | bytes 1572872 | tf_op jit(solution)/shard_map/ppermute | solution.py:459
  46.7 16.2 %collective-permute-start.14 = (bf16[256,256]{1,0:T(8,128)(2,1)S(1)}, bf16[256,256]{1,0:T(8,128)(2,1)S(1)}, u32[]{:S(2)}, u32[]{:S(2)}) collective-permute-start(bf16[256,256]{1,0:T(8,128)(2,1)S(1)} %get-tuple-element.66), channel_id=1, source_target_pairs={{0,2},{1,3},{2,0},{3,1},{4,6},{5,7},{6,4},{7,5},{8,10},{9,11},{10,... | collective-permute-start | bytes 393224 | tf_op jit(solution)/shard_map/ppermute | solution.py:449
  48.3 6.8 %collective-permute-start.20 = (bf16[64,1024]{1,0:T(8,128)(2,1)S(1)}, bf16[64,1024]{1,0:T(8,128)(2,1)S(1)}, u32[]{:S(2)}, u32[]{:S(2)}) collective-permute-start(bf16[64,1024]{1,0:T(8,128)(2,1)S(1)} %shard_map.120.refs_0_), channel_id=1, source_target_pairs={{0,2},{1,3},{2,18},{3,19},{4,6},{5,7},{6,22},{7,23},{8,10},{9,11},... | collective-permute-start | bytes 393224 | tf_op jit(solution)/shard_map/ppermute | solution.py:562
  49.6 9.4 %collective-permute-start.21 = (bf16[64,1024]{1,0:T(8,128)(2,1)S(1)}, bf16[64,1024]{1,0:T(8,128)(2,1)S(1)}, u32[]{:S(2)}, u32[]{:S(2)}) collective-permute-start(bf16[64,1024]{1,0:T(8,128)(2,1)S(1)} %shard_map.120.refs_0_), channel_id=1, source_target_pairs={{2,16},{3,17},{6,20},{7,21},{10,24},{11,25},{14,28},{15,29},{16,2}... | collective-permute-start | bytes 393224 | tf_op jit(solution)/shard_map/ppermute | solution.py:563
  55.1 8.7 %collective-permute-start.13 = (bf16[256,256]{1,0:T(8,128)(2,1)S(1)}, bf16[256,256]{1,0:T(8,128)(2,1)S(1)}, u32[]{:S(2)}, u32[]{:S(2)}) collective-permute-start(bf16[256,256]{1,0:T(8,128)(2,1)S(1)} %shard_map.117), channel_id=1, source_target_pairs={{0,2},{1,3},{2,0},{3,1},{4,6},{5,7},{6,4},{7,5},{8,10},{9,11},{10,... | collective-permute-start | bytes 393224 | tf_op jit(solution)/shard_map/ppermute | solution.py:449
  59.0 7.9 %collective-permute-start.25 = (bf16[64,1024]{1,0:T(8,128)(2,1)S(1)}, bf16[64,1024]{1,0:T(8,128)(2,1)S(1)}, u32[]{:S(2)}, u32[]{:S(2)}) collective-permute-start(bf16[64,1024]{1,0:T(8,128)(2,1)S(1)} %shard_map.121.refs_3_.refs_0_), channel_id=1, source_target_pairs={{0,4},{1,5},{2,6},{3,7},{4,0},{5,1},{6,2},{7,3},{8,12},{9,13},{10,... | collective-permute-start | bytes 393224 | tf_op jit(solution)/shard_map/ppermute | solution.py:452
  62.9 9.4 %collective-permute-start.26 = (bf16[64,1024]{1,0:T(8,128)(2,1)S(1)}, bf16[64,1024]{1,0:T(8,128)(2,1)S(1)}, u32[]{:S(2)}, u32[]{:S(2)}) collective-permute-start(bf16[64,1024]{1,0:T(8,128)(2,1)S(1)} %shard_map.121.refs_3_.refs_0_), channel_id=1, source_target_pairs={{0,8},{1,9},{2,10},{3,11},{4,12},{5,13},{6,14},{7,15},{8,0},{9,1},... | collective-permute-start | bytes 393224 | tf_op jit(solution)/shard_map/ppermute | solution.py:452
  63.8 8.5 %collective-permute-start.27 = (bf16[64,1024]{1,0:T(8,128)(2,1)S(1)}, bf16[64,1024]{1,0:T(8,128)(2,1)S(1)}, u32[]{:S(2)}, u32[]{:S(2)}) collective-permute-start(bf16[64,1024]{1,0:T(8,128)(2,1)S(1)} %shard_map.121.refs_3_.refs_0_), channel_id=1, source_target_pairs={{0,12},{1,13},{2,14},{3,15},{4,8},{5,9},{6,10},{7,11},{8,4},{9,5},... | collective-permute-start | bytes 393224 | tf_op jit(solution)/shard_map/ppermute | solution.py:452
  65.4 1.6 %collective-permute-start.15 = (bf16[512,256]{1,0:T(8,128)(2,1)S(1)}, bf16[512,256]{1,0:T(8,128)(2,1)S(1)}, u32[]{:S(2)}, u32[]{:S(2)}) collective-permute-start(bf16[512,256]{1,0:T(8,128)(2,1)S(1)} %shard_map.118), channel_id=1, source_target_pairs={{0,1},{1,0},{2,3},{3,2},{4,5},{5,4},{6,7},{7,6},{8,9},{9,8},{10,11... | collective-permute-start | bytes 786440 | tf_op jit(solution)/shard_map/ppermute | solution.py:449
  65.4 2.2 %copy-start = (bf16[512,1024]{1,0:T(8,128)(2,1)S(1)}, bf16[512,1024]{1,0:T(8,128)(2,1)}, u32[]{:S(2)}) copy-start(bf16[512,1024]{1,0:T(8,128)(2,1)} %refs_0_.3) | copy-start | bytes 3145732
  65.6 6.7 %collective-permute-start.22 = (bf16[256,256]{1,0:T(8,128)(2,1)S(1)}, bf16[256,256]{1,0:T(8,128)(2,1)S(1)}, u32[]{:S(2)}, u32[]{:S(2)}) collective-permute-start(bf16[256,256]{1,0:T(8,128)(2,1)S(1)} %get-tuple-element.77), channel_id=1, source_target_pairs={{0,1},{1,0},{2,3},{3,2},{4,5},{5,4},{6,7},{7,6},{8,9},{9,8},{10,11... | collective-permute-start | bytes 393224 | tf_op jit(solution)/shard_map/ppermute | solution.py:449
  66.9 6.1 %collective-permute-start.23 = (bf16[256,256]{1,0:T(8,128)(2,1)S(1)}, bf16[256,256]{1,0:T(8,128)(2,1)S(1)}, u32[]{:S(2)}, u32[]{:S(2)}) collective-permute-start(bf16[256,256]{1,0:T(8,128)(2,1)S(1)} %get-tuple-element.78), channel_id=1, source_target_pairs={{0,2},{1,3},{2,0},{3,1},{4,6},{5,7},{6,4},{7,5},{8,10},{9,11},{10,... | collective-permute-start | bytes 393224 | tf_op jit(solution)/shard_map/ppermute | solution.py:449
  67.0 6.1 %collective-permute-start.24 = (bf16[256,256]{1,0:T(8,128)(2,1)S(1)}, bf16[256,256]{1,0:T(8,128)(2,1)S(1)}, u32[]{:S(2)}, u32[]{:S(2)}) collective-permute-start(bf16[256,256]{1,0:T(8,128)(2,1)S(1)} %get-tuple-element.79), channel_id=1, source_target_pairs={{0,3},{1,2},{2,1},{3,0},{4,7},{5,6},{6,5},{7,4},{8,11},{9,10},{10,... | collective-permute-start | bytes 393224 | tf_op jit(solution)/shard_map/ppermute | solution.py:449
  73.1 2.8 %collective-permute-start.28 = (bf16[256,1024]{1,0:T(8,128)(2,1)S(1)}, bf16[256,1024]{1,0:T(8,128)(2,1)S(1)}, u32[]{:S(2)}, u32[]{:S(2)}) collective-permute-start(bf16[256,1024]{1,0:T(8,128)(2,1)S(1)} %shard_map.124.refs_0_), channel_id=1, source_target_pairs={{0,1},{1,0},{2,3},{3,2},{4,5},{5,4},{6,7},{7,6},{8,9},{9,8},{10,11... | collective-permute-start | bytes 1572872 | tf_op jit(solution)/shard_map/ppermute | solution.py:449
